TPU v7x, 128 devices: a whole 4x4x4 slice. The times are simulated.
128 devices in a mesh: dp: 4 (over x), ctx: 16 (over z, y_hi, core), tp: 2 (over y_lo).
Axes of the slice: x: 4, y: 4 (y_hi: 2, y_lo: 2; y = y_hi * 2 + y_lo), z: 4, core: 2. Of those that a mesh axis runs over, the one named last changes fastest.
Arguments:
- tokens: bfloat16 [4, 4096, 2048], P('dp', 'ctx'), may hold values from -6 to 6
- w_query: bfloat16 [2048, 2048], P(('dp', 'ctx'), 'tp'), may hold values from -0.125 to 0.125
- w_key: bfloat16 [2048, 256], P(('dp', 'ctx'), 'tp'), may hold values from -0.125 to 0.125
- w_value: bfloat16 [2048, 256], P(('dp', 'ctx'), 'tp'), may hold values from -0.125 to 0.125
- w_output: bfloat16 [2048, 2048], P('tp', ('dp', 'ctx')), may hold values from -0.375 to 0.375
- w_gate: bfloat16 [2048, 5632], P(('dp', 'ctx'), 'tp'), may hold values from -0.125 to 0.125
- w_up: bfloat16 [2048, 5632], P(('dp', 'ctx'), 'tp'), may hold values from -0.125 to 0.125
- w_down: bfloat16 [5632, 2048], P('tp', ('dp', 'ctx')), may hold values from -0.078125 to 0.078125
- norm_attn: bfloat16 [2048], P(('dp', 'ctx')), may hold values from 0.5 to 1.5
- norm_ffn: bfloat16 [2048], P(('dp', 'ctx')), may hold values from 0.5 to 1.5
- cotangent: bfloat16 [4, 4096, 2048], P('dp', 'ctx'), may hold values from -6 to 6
Outputs:
- block_out: bfloat16 [4, 4096, 2048], P('dp', 'ctx')
- input_grad: float32 [4, 4096, 2048], P('dp', 'ctx')
- grad_query: float32 [2048, 2048], P(('dp', 'ctx'), 'tp')
- grad_key: float32 [2048, 256], P(('dp', 'ctx'), 'tp')
- grad_value: float32 [2048, 256], P(('dp', 'ctx'), 'tp')
- grad_output: float32 [2048, 2048], P('tp', ('dp', 'ctx'))
- grad_gate: float32 [2048, 5632], P(('dp', 'ctx'), 'tp')
- grad_up: float32 [2048, 5632], P(('dp', 'ctx'), 'tp')
- grad_down: float32 [5632, 2048], P('tp', ('dp', 'ctx'))
- grad_norm_attn: float32 [2048], P(('dp', 'ctx'))
- grad_norm_ffn: float32 [2048], P(('dp', 'ctx'))
All inputs are finite; a program needn't handle non-finite values.
Results may differ from a plain program's by a relative error of at most 0.025.
Values may be sent and summed in bfloat16 or wider, within the bound.
No kernel may reach another device: no remote copies, remote signals or barrier semaphores. Data moves between devices by JAX's collectives and lax.ppermute only.
A program may use at most 256 MiB of HBM per device.

v0:
```python
import jax
import jax.numpy as jnp
from jax import lax
from jax.sharding import PartitionSpec as P

HD = 64


epsilon = 1e-05
rope_base = 10000.0
masked_low = -1e30


def passed_along(array, axis, by):
    length = lax.axis_size(axis)
    return lax.ppermute(array, axis, [(i, (i + by) % length) for i in range(length)])


def shifted(value, axis, steps):
    count = lax.axis_size(axis)
    first, last = (max(0, -steps), min(count, count - steps))
    return lax.ppermute(value, axis, [(source, source + steps) for source in range(first, last)])


def tables(positions, width):
    half_width = width // 2
    freqs = rope_base ** (-2.0 * jnp.arange(half_width, dtype=jnp.float32) / width)
    angles = positions[:, None] * freqs[None, :]
    cosine = jnp.cos(angles)
    sine = jnp.sin(angles)
    return (jnp.concatenate([cosine, cosine], -1), jnp.concatenate([sine, sine], -1))


def rotate(values, cosine, sine):
    half_width = values.shape[-1] // 2
    turned = jnp.concatenate([-values[..., half_width:], values[..., :half_width]], -1)
    return values * cosine[:, None, :] + turned * sine[:, None, :]


def rotate_back(grads, cosine, sine):
    half_width = grads.shape[-1] // 2
    spun = grads * sine[:, None, :]
    turned = jnp.concatenate([spun[..., half_width:], -spun[..., :half_width]], -1)
    return grads * cosine[:, None, :] + turned


def attend(running, query_grp, keys, values, query_pos, key_pos, scale):

    def compute(state_in):
        run_max, run_sum, run_acc = state_in
        scores = (
            jnp.einsum("tgjd,sgd->gjts", query_grp, keys, preferred_element_type=jnp.float32)
            * scale
        )
        visible = key_pos[None, :] <= query_pos[:, None]
        scores = jnp.where(visible, scores, masked_low)
        new_max = jnp.maximum(run_max, jnp.max(scores, axis=-1))
        probs = jnp.where(visible, jnp.exp(scores - new_max[..., None]), 0.0)
        factor = jnp.exp(run_max - new_max)
        new_sum = run_sum * factor + jnp.sum(probs, axis=-1)
        added = jnp.einsum(
            "gjts,sgd->gjtd", probs.astype(jnp.bfloat16), values, preferred_element_type=jnp.float32
        )
        return (new_max, new_sum, run_acc * factor[..., None] + added)

    def keep_state(state_in):
        return state_in

    usable = jnp.logical_and(key_pos[0] >= 0, key_pos[0] <= query_pos[-1])
    return lax.cond(usable, compute, keep_state, running)


def attend_back(
    running, query_grp, grad_grp, log_sum, row_delta, keys, values, query_pos, key_pos, scale
):

    def compute(state_in):
        grad_q, grad_k, grad_v = state_in
        scores = (
            jnp.einsum("tgjd,sgd->gjts", query_grp, keys, preferred_element_type=jnp.float32)
            * scale
        )
        visible = key_pos[None, :] <= query_pos[:, None]
        probs = jnp.where(visible, jnp.exp(scores - log_sum[..., None]), 0.0)
        grad_v = grad_v + jnp.einsum(
            "gjts,tgjd->sgd",
            probs.astype(jnp.bfloat16),
            grad_grp,
            preferred_element_type=jnp.float32,
        )
        grad_probs = jnp.einsum(
            "tgjd,sgd->gjts", grad_grp, values, preferred_element_type=jnp.float32
        )
        grad_scores = (probs * (grad_probs - row_delta[..., None]) * scale).astype(jnp.bfloat16)
        grad_q = grad_q + jnp.einsum(
            "gjts,sgd->tgjd", grad_scores, keys, preferred_element_type=jnp.float32
        )
        grad_k = grad_k + jnp.einsum(
            "gjts,tgjd->sgd", grad_scores, query_grp, preferred_element_type=jnp.float32
        )
        return (grad_q, grad_k, grad_v)

    def keep_state(state_in):
        return state_in

    usable = jnp.logical_and(key_pos[0] >= 0, key_pos[0] <= query_pos[-1])
    return lax.cond(usable, compute, keep_state, running)


def pass_grads(grad_k, grad_v):
    return (
        passed_along(grad_k.astype(jnp.bfloat16), "ctx", 1).astype(grad_k.dtype),
        passed_along(grad_v.astype(jnp.bfloat16), "ctx", 1).astype(grad_v.dtype),
    )


def on_device(
    tokens, w_query, w_key, w_value, w_output, w_gate, w_up, w_down, norm_attn, norm_ffn, cotangent
):
    f32 = jnp.float32
    bf16 = jnp.bfloat16
    rows_local = (w_query, w_key, w_value, w_gate, w_up, norm_attn, norm_ffn)
    cols_local = (w_output, w_down)
    wq_full, wk_full, wv_full, wg_full, wu_full, gain_one, gain_two = (
        lax.all_gather(rows_local[0], ("dp", "ctx"), axis=0, tiled=True),
        lax.all_gather(rows_local[1], ("dp", "ctx"), axis=0, tiled=True),
        lax.all_gather(rows_local[2], ("dp", "ctx"), axis=0, tiled=True),
        lax.all_gather(rows_local[3], ("dp", "ctx"), axis=0, tiled=True),
        lax.all_gather(rows_local[4], ("dp", "ctx"), axis=0, tiled=True),
        lax.all_gather(rows_local[5], ("dp", "ctx"), axis=0, tiled=True),
        lax.all_gather(rows_local[6], ("dp", "ctx"), axis=0, tiled=True),
    )
    wo_full, wd_full = (
        lax.all_gather(cols_local[0], ("dp", "ctx"), axis=1, tiled=True),
        lax.all_gather(cols_local[1], ("dp", "ctx"), axis=1, tiled=True),
    )
    inputs = tokens[0].astype(f32)
    rows_here = inputs.shape[0]
    q_heads = wq_full.shape[1] // HD
    kv_heads = wk_full.shape[1] // HD
    group = q_heads // kv_heads
    scale = HD ** (-0.5)
    ctx_index = lax.axis_index("ctx")
    ctx_count = lax.axis_size("ctx")
    local_pos = jnp.arange(rows_here, dtype=jnp.int32)
    query_pos = ctx_index * rows_here + local_pos
    cosine, sine = tables(query_pos.astype(f32), HD)
    gain_attn = gain_one.astype(f32)
    gain_mlp = gain_two.astype(f32)
    inverse_one = lax.rsqrt(jnp.mean(inputs * inputs, axis=-1, keepdims=True) + epsilon)
    normed_one = (inputs * inverse_one * gain_attn).astype(bf16)
    query_lin = jnp.dot(normed_one, wq_full, preferred_element_type=f32).reshape(
        rows_here, q_heads, HD
    )
    query_grp = rotate(query_lin, cosine, sine).astype(bf16).reshape(rows_here, kv_heads, group, HD)
    key_lin = jnp.dot(normed_one, wk_full, preferred_element_type=f32).reshape(
        rows_here, kv_heads, HD
    )
    keys_own = rotate(key_lin, cosine, sine).astype(bf16)
    values_own = (
        jnp.dot(normed_one, wv_full, preferred_element_type=f32)
        .astype(bf16)
        .reshape(rows_here, kv_heads, HD)
    )
    start_state = (
        jnp.full((kv_heads, group, rows_here), masked_low, f32),
        jnp.zeros((kv_heads, group, rows_here), f32),
        jnp.zeros((kv_heads, group, rows_here, HD), f32),
    )

    def cycle_turn(turn, carried):
        running, keys, values = carried
        source = ctx_index - turn
        running = attend(
            running, query_grp, keys, values, query_pos, source * rows_here + local_pos, scale
        )
        keys, values = shifted((keys, values), "ctx", 1)
        return (running, keys, values)

    running, keys, values = lax.fori_loop(
        0, ctx_count - 1, cycle_turn, (start_state, keys_own, values_own)
    )
    source = ctx_index - (ctx_count - 1)
    running = attend(
        running, query_grp, keys, values, query_pos, source * rows_here + local_pos, scale
    )
    run_max, run_sum, run_acc = running
    attn_raw = run_acc / run_sum[..., None]
    log_sum = run_max + jnp.log(run_sum)
    attn_low = attn_raw.transpose(2, 0, 1, 3).reshape(rows_here, q_heads * HD).astype(bf16)
    branch_one = lax.psum(
        jnp.dot(attn_low, wo_full, preferred_element_type=f32).astype(jnp.bfloat16), "tp"
    ).astype(jnp.float32)
    middle = inputs + branch_one
    inverse_two = lax.rsqrt(jnp.mean(middle * middle, axis=-1, keepdims=True) + epsilon)
    normed_two = (middle * inverse_two * gain_mlp).astype(bf16)
    gate_lin = jnp.dot(normed_two, wg_full, preferred_element_type=f32)
    up_lin = jnp.dot(normed_two, wu_full, preferred_element_type=f32)
    sigmoid_gate = jax.nn.sigmoid(gate_lin)
    inner = (gate_lin * sigmoid_gate * up_lin).astype(bf16)
    branch_two = lax.psum(
        jnp.dot(inner, wd_full, preferred_element_type=f32).astype(jnp.bfloat16), "tp"
    ).astype(jnp.float32)
    block_out = (middle + branch_two).astype(bf16)
    grad_in_low = cotangent[0]
    grad_top = grad_in_low.astype(f32)
    grad_inner = jnp.einsum("td,fd->tf", grad_in_low, wd_full, preferred_element_type=f32)
    grad_down = jnp.einsum("tf,td->fd", inner, grad_in_low, preferred_element_type=f32)
    grad_gate_lin = (
        grad_inner * up_lin * sigmoid_gate * (1.0 + gate_lin * (1.0 - sigmoid_gate))
    ).astype(bf16)
    grad_up_lin = (grad_inner * gate_lin * sigmoid_gate).astype(bf16)
    grad_gate = jnp.einsum("td,tf->df", normed_two, grad_gate_lin, preferred_element_type=f32)
    grad_up = jnp.einsum("td,tf->df", normed_two, grad_up_lin, preferred_element_type=f32)
    grad_norm_two = jnp.einsum(
        "tf,df->td", grad_gate_lin, wg_full, preferred_element_type=f32
    ) + jnp.einsum("tf,df->td", grad_up_lin, wu_full, preferred_element_type=f32)
    grad_norm_two = lax.psum(grad_norm_two.astype(jnp.bfloat16), "tp").astype(jnp.float32)
    scaled_two = gain_mlp * grad_norm_two
    grad_gain_two = jnp.sum(grad_norm_two * middle * inverse_two, axis=0)
    grad_middle = (
        grad_top
        + inverse_two * scaled_two
        - middle
        * (inverse_two * inverse_two * inverse_two)
        * jnp.mean(scaled_two * middle, axis=-1, keepdims=True)
    )
    grad_middle_low = grad_middle.astype(bf16)
    grad_output = jnp.einsum("tk,td->kd", attn_low, grad_middle_low, preferred_element_type=f32)
    grad_attn = jnp.einsum(
        "td,kd->tk", grad_middle_low, wo_full, preferred_element_type=f32
    ).astype(bf16)
    grad_grp = grad_attn.reshape(rows_here, kv_heads, group, HD)
    row_delta = jnp.einsum("tgjd,gjtd->gjt", grad_grp.astype(f32), attn_raw)
    back_start = (
        jnp.zeros((rows_here, kv_heads, group, HD), f32),
        jnp.zeros((rows_here, kv_heads, HD), f32),
        jnp.zeros((rows_here, kv_heads, HD), f32),
    )

    def back_turn(turn, carried):
        grad_q, keys, values, grad_k, grad_v = carried
        source = ctx_index - turn
        grad_q, grad_k, grad_v = attend_back(
            (grad_q, grad_k, grad_v),
            query_grp,
            grad_grp,
            log_sum,
            row_delta,
            keys,
            values,
            query_pos,
            source * rows_here + local_pos,
            scale,
        )
        grad_k, grad_v = pass_grads(grad_k, grad_v)
        keys, values = shifted((keys, values), "ctx", 1)
        return (grad_q, keys, values, grad_k, grad_v)

    grad_q, keys, values, grad_k, grad_v = lax.fori_loop(
        0,
        ctx_count - 1,
        back_turn,
        (back_start[0], keys_own, values_own, back_start[1], back_start[2]),
    )
    source = ctx_index - (ctx_count - 1)
    grad_q, grad_k, grad_v = attend_back(
        (grad_q, grad_k, grad_v),
        query_grp,
        grad_grp,
        log_sum,
        row_delta,
        keys,
        values,
        query_pos,
        source * rows_here + local_pos,
        scale,
    )
    grad_k, grad_v = pass_grads(grad_k, grad_v)
    grad_q_low = (
        rotate_back(grad_q.reshape(rows_here, q_heads, HD), cosine, sine)
        .reshape(rows_here, q_heads * HD)
        .astype(bf16)
    )
    grad_k_low = rotate_back(grad_k, cosine, sine).reshape(rows_here, kv_heads * HD).astype(bf16)
    grad_v_low = grad_v.reshape(rows_here, kv_heads * HD).astype(bf16)
    grad_query = jnp.einsum("td,tk->dk", normed_one, grad_q_low, preferred_element_type=f32)
    grad_key = jnp.einsum("td,tk->dk", normed_one, grad_k_low, preferred_element_type=f32)
    grad_value = jnp.einsum("td,tk->dk", normed_one, grad_v_low, preferred_element_type=f32)
    grad_norm_one = (
        jnp.einsum("tk,dk->td", grad_q_low, wq_full, preferred_element_type=f32)
        + jnp.einsum("tk,dk->td", grad_k_low, wk_full, preferred_element_type=f32)
        + jnp.einsum("tk,dk->td", grad_v_low, wv_full, preferred_element_type=f32)
    )
    grad_norm_one = lax.psum(grad_norm_one.astype(jnp.bfloat16), "tp").astype(jnp.float32)
    scaled_one = gain_attn * grad_norm_one
    grad_gain_one = jnp.sum(grad_norm_one * inputs * inverse_one, axis=0)
    input_grad = (
        grad_middle
        + inverse_one * scaled_one
        - inputs
        * (inverse_one * inverse_one * inverse_one)
        * jnp.mean(scaled_one * inputs, axis=-1, keepdims=True)
    )
    row_grads = (
        lax.psum_scatter(grad_query, ("dp", "ctx"), scatter_dimension=0, tiled=True),
        lax.psum_scatter(grad_key, ("dp", "ctx"), scatter_dimension=0, tiled=True),
        lax.psum_scatter(grad_value, ("dp", "ctx"), scatter_dimension=0, tiled=True),
        lax.psum_scatter(grad_gate, ("dp", "ctx"), scatter_dimension=0, tiled=True),
        lax.psum_scatter(grad_up, ("dp", "ctx"), scatter_dimension=0, tiled=True),
        lax.psum_scatter(grad_gain_one, ("dp", "ctx"), scatter_dimension=0, tiled=True),
        lax.psum_scatter(grad_gain_two, ("dp", "ctx"), scatter_dimension=0, tiled=True),
    )
    col_grads = (
        lax.psum_scatter(grad_output, ("dp", "ctx"), scatter_dimension=1, tiled=True),
        lax.psum_scatter(grad_down, ("dp", "ctx"), scatter_dimension=1, tiled=True),
    )
    out_output, out_down = (col_grads[0], col_grads[1])
    return (
        block_out[None],
        input_grad[None],
        row_grads[0],
        row_grads[1],
        row_grads[2],
        out_output,
        row_grads[3],
        row_grads[4],
        out_down,
        row_grads[5],
        row_grads[6],
    )


def solution(mesh):
    in_specs = (
        P("dp", "ctx", None),
        P(("dp", "ctx"), "tp"),
        P(("dp", "ctx"), "tp"),
        P(("dp", "ctx"), "tp"),
        P("tp", ("dp", "ctx")),
        P(("dp", "ctx"), "tp"),
        P(("dp", "ctx"), "tp"),
        P("tp", ("dp", "ctx")),
        P(("dp", "ctx")),
        P(("dp", "ctx")),
        P("dp", "ctx", None),
    )
    out_specs = (
        P("dp", "ctx", None),
        P("dp", "ctx", None),
        P(("dp", "ctx"), "tp"),
        P(("dp", "ctx"), "tp"),
        P(("dp", "ctx"), "tp"),
        P("tp", ("dp", "ctx")),
        P(("dp", "ctx"), "tp"),
        P(("dp", "ctx"), "tp"),
        P("tp", ("dp", "ctx")),
        P(("dp", "ctx")),
        P(("dp", "ctx")),
    )
    return jax.shard_map(
        on_device, mesh=mesh, in_specs=in_specs, out_specs=out_specs, check_vma=False
    )
```

profile of v0, /device:TPU:1, one launch (start us, length us, event | category | flops | bytes accessed | tf_op | source)
XLA Modules:
  0.0 3844.9 jit_solution(8345867042333617517)
XLA Ops:
  12.5 167.9 %all-reduce.5 = (bf16[2048]{0:T(1024)(128)(2,1)S(1)}, bf16[2048]{0:T(1024)(128)(2,1)S(1)}) all-reduce(bf16[2048]{0:T(1024)(128)(2,1)S(1)} %dynamic-update-slice, bf16[2048]{0:T(1024)(128)(2,1)S(1)} %dynamic-update-slice.1), channel_id=1, replica_groups=mesh['dp'=4,'ctx'=16,'tp'=2] {'dp','ctx'}, use_global_device_ids=true, to_apply=%add | all-reduce | flops 4096 | bytes 16384
  180.5 96.7 %all_gather.28 = bf16[2048,128]{1,0:T(8,128)(2,1)S(1)} all-gather(bf16[32,128]{1,0:T(8,128)(2,1)} %param.25), channel_id=1, replica_groups=mesh['dp'=4,'ctx'=16,'tp'=2] {'dp','ctx'}, dimensions={0}, use_global_device_ids=true | all-gather | bytes 532480 | tf_op jit(solution)/shard_map/all_gather | solution.py:126
  279.2 93.0 %all_gather.29 = bf16[2048,128]{1,0:T(8,128)(2,1)S(1)} all-gather(bf16[32,128]{1,0:T(8,128)(2,1)S(1)} %copy-done.39), channel_id=1, replica_groups=mesh['dp'=4,'ctx'=16,'tp'=2] {'dp','ctx'}, dimensions={0}, use_global_device_ids=true | all-gather | bytes 532480 | tf_op jit(solution)/shard_map/all_gather | solution.py:127
  388.1 193.2 %while.44 = (s32[]{:T(128)}, f32[2,8,256]{2,1,0:T(8,128)S(1)}, f32[2,8,256]{2,1,0:T(8,128)S(1)}, f32[2,8,256,64]{2,3,1,0:T(8,128)S(1)}, bf16[256,2,64]{0,2,1:T(8...) while((s32[]{:T(128)}, f32[2,8,256]{2,1,0:T(8,128)S(1)}, ...), condition=%wide.region_6.7_spmd.clone, body=%wide.region_1.6_spmd.clone.sunk | while | flops 282665216 | bytes 16649603 | solution.py:180
  427.2 7.5 collective-permute-start
  588.8 62.2 %all-reduce.11.cloned.1.call-done = bf16[256,2048]{1,0:T(8,128)(2,1)} async-done(((bf16[256,2048]{1,0:T(8,128)(2,1)}), bf16[256,2048]{1,0:T(8,128)(2,1)}) %all-reduce.11.cloned.1.call-update) | async-done | bytes 1048592 | tf_op jit(solution)/shard_map/psum | solution.py:191
  654.3 92.1 %all-gather.10.cloned.1.call-done = bf16[2048,2816]{1,0:T(8,128)(2,1)} async-done(((bf16[32,2816]{1,0:T(8,128)(2,1)}), bf16[2048,2816]{1,0:T(8,128)(2,1)}) %all-gather.10.cloned.1.call-update) | async-done | bytes 11534352 | tf_op jit(solution)/shard_map/all_gather | solution.py:128
  746.4 9.4 fusion.149
  755.8 82.3 %all-gather.12.cloned.1.call-done = bf16[2048,2816]{1,0:T(8,128)(2,1)} async-done(((bf16[32,2816]{1,0:T(8,128)(2,1)}), bf16[2048,2816]{1,0:T(8,128)(2,1)}) %all-gather.12.cloned.1.call-update) | async-done | bytes 11534352 | tf_op jit(solution)/shard_map/all_gather | solution.py:129
  838.0 9.3 fusion.150
  847.3 82.3 %all-gather.14.cloned.1.call-done = bf16[2816,2048]{0,1:T(8,128)(2,1)} async-done(((bf16[2816,32]{0,1:T(8,128)(2,1)}), bf16[2816,2048]{0,1:T(8,128)(2,1)}) %all-gather.14.cloned.1.call-update) | async-done | bytes 11534352 | tf_op jit(solution)/shard_map/all_gather | solution.py:135
  929.7 11.1 multiply_convert_fusion
  940.8 7.0 fusion.151
  947.9 8.4 fusion.86
  956.4 8.9 convolution_convert_fusion
  965.3 35.1 all-reduce.13.cloned.1.call-done
  1011.9 282.4 %while.45 = (s32[]{:T(128)}, f32[256,2,8,64]{0,3,2,1:T(8,128)S(1)}, bf16[256,2,64]{0,2,1:T(8,128)(2,1)S(1)}, bf16[256,2,64]{0,2,1:T(8,128)(2,1)S(1)}, f32[256,2,...) while((s32[]{:T(128)}, f32[256,2,8,64]{0,3,2,1:T(8,128)S(1)}, ...), condition=%wide.region_19.0_spmd.clone, body=%wide.region_16.19_spmd.clone.sunk | while | flops 683213056 | bytes 28888680 | solution.py:260
  1057.3 9.3 collective-permute-start.4
  1103.6 8.8 collective-permute-start.2
  1194.2 8.6 collective-permute-start.2
  1308.4 6.9 fusion.130
  1320.3 12.7 fusion.153
  1333.0 12.6 fusion.154
  1346.0 13.6 fusion.114
  1360.3 18.1 all-reduce.15.cloned.1.call-done
  1380.3 322.3 %all-reduce.4 = (f32[2048]{0:T(1024)S(1)}, f32[2048]{0:T(1024)S(1)}) all-reduce(f32[2048]{0:T(1024)S(1)} %get-tuple-element.761, f32[2048]{0:T(1024)S(1)} %copy-done.27), channel_id=9, replica_groups=mesh['dp'=4,'ctx'=16,'tp'=2] {'dp','ctx'}, use_global_device_ids=true, to_apply=%region_32.33.clone | all-reduce | flops 4096 | bytes 32768
  1709.2 329.4 %reduce-scatter.12.cloned.1.call-done = f32[32,128]{1,0:T(8,128)} async-done(((f32[2048,128]{1,0:T(8,128)}), f32[32,128]{1,0:T(8,128)}) %reduce-scatter.12.cloned.1.call-update) | async-done | bytes 16400 | tf_op jit(solution)/shard_map/reduce_scatter | solution.py:308
  2038.6 344.0 %reduce-scatter.14.cloned.1.call-done = f32[1024,32]{0,1:T(8,128)} async-done(((f32[1024,2048]{0,1:T(8,128)}), f32[1024,32]{0,1:T(8,128)}) %reduce-scatter.14.cloned.1.call-update) | async-done | bytes 131088 | tf_op jit(solution)/shard_map/reduce_scatter | solution.py:315
  2382.6 343.7 %reduce-scatter.8.cloned.1.call-done = f32[32,1024]{1,0:T(8,128)} async-done(((f32[2048,1024]{1,0:T(8,128)}), f32[32,1024]{1,0:T(8,128)}) %reduce-scatter.8.cloned.1.call-update) | async-done | bytes 131088 | tf_op jit(solution)/shard_map/reduce_scatter | solution.py:306
  2726.3 370.8 %reduce-scatter.16.cloned.1.call-done = f32[32,2816]{1,0:T(8,128)} async-done(((f32[2048,2816]{1,0:T(8,128)}), f32[32,2816]{1,0:T(8,128)}) %reduce-scatter.16.cloned.1.call-update) | async-done | bytes 360464 | tf_op jit(solution)/shard_map/reduce_scatter | solution.py:309
  3097.0 370.8 %reduce-scatter.18.cloned.1.call-done = f32[32,2816]{1,0:T(8,128)} async-done(((f32[2048,2816]{1,0:T(8,128)}), f32[32,2816]{1,0:T(8,128)}) %reduce-scatter.18.cloned.1.call-update) | async-done | bytes 360464 | tf_op jit(solution)/shard_map/reduce_scatter | solution.py:310
  3467.8 370.1 %reduce-scatter.20.cloned.1.call-done = f32[2816,32]{0,1:T(8,128)} async-done(((f32[2816,2048]{0,1:T(8,128)}), f32[2816,32]{0,1:T(8,128)}) %reduce-scatter.20.cloned.1.call-update) | async-done | bytes 360464 | tf_op jit(solution)/shard_map/reduce_scatter | solution.py:316
  (646 shorter events, 472.2 us)
Async XLA Ops:
  7.2 369.9 %all-gather.6.cloned.1.call-start = ((), (), s32[]{:S(2)}) async-start(), calls=%async_computation.7 | async-start | bytes 4259840 | tf_op jit(solution)/shard_map/all_gather | solution.py:125
  7.9 574.4 %all-gather.8.cloned.1.call-start = ((), (), s32[]{:S(2)}) async-start(), calls=%async_computation.8 | async-start | bytes 4259840 | tf_op jit(solution)/shard_map/all_gather | solution.py:134
  8.7 642.4 %all-reduce.11.cloned.1.call-start = ((), (), s32[]{:S(2)}) async-start(), calls=%async_computation.9 | async-start | bytes 2097152 | tf_op jit(solution)/shard_map/psum | solution.py:191
  388.7 14.0 collective-permute-start
  403.4 14.0 collective-permute-start
  427.2 14.0 collective-permute-start
  441.8 14.0 collective-permute-start
  467.0 12.7 collective-permute-start
  480.3 13.8 collective-permute-start
  518.2 13.8 collective-permute-start
  556.1 13.8 collective-permute-start
  587.0 159.4 %all-gather.10.cloned.1.call-start = ((), (), s32[]{:S(2)}) async-start(), calls=%async_computation.10 | async-start | bytes 11714560 | tf_op jit(solution)/shard_map/all_gather | solution.py:128
  587.5 250.5 %all-gather.12.cloned.1.call-start = ((), (), s32[]{:S(2)}) async-start(), calls=%async_computation.11 | async-start | bytes 11714560 | tf_op jit(solution)/shard_map/all_gather | solution.py:129
  588.1 341.5 %all-gather.14.cloned.1.call-start = ((), (), s32[]{:S(2)}) async-start(), calls=%async_computation.12 | async-start | bytes 11714560 | tf_op jit(solution)/shard_map/all_gather | solution.py:135
  588.7 411.7 %all-reduce.13.cloned.1.call-start = ((), (), s32[]{:S(2)}) async-start(), calls=%async_computation.13 | async-start | bytes 2097152 | tf_op jit(solution)/shard_map/psum | solution.py:218
  956.3 422.1 %all-reduce.15.cloned.1.call-start = ((), (), s32[]{:S(2)}) async-start(), calls=%async_computation.21 | async-start | bytes 4194304 | tf_op jit(solution)/shard_map/psum | solution.py:201
  1057.3 15.1 collective-permute-start.4
  1077.6 16.9 collective-permute-start.4
  1081.5 13.0 collective-permute-start.5
  1099.6 14.8 collective-permute-start.4
  1119.6 13.0 collective-permute-start.4
  1137.7 12.7 collective-permute-start.4
  1155.5 14.1 collective-permute-start.4
  1190.2 15.1 collective-permute-start.4
  1244.2 14.1 collective-permute-start.4
  1304.7 404.6 %reduce-scatter.10.cloned.1.call-start = ((), (), s32[]{:S(2)}) async-start(), calls=%async_computation.15 | async-start | bytes 1064960 | tf_op jit(solution)/shard_map/reduce_scatter | solution.py:307
  1306.6 732.0 %reduce-scatter.12.cloned.1.call-start = ((), (), s32[]{:S(2)}) async-start(), calls=%async_computation.16 | async-start | bytes 1064960 | tf_op jit(solution)/shard_map/reduce_scatter | solution.py:308
  1308.3 1074.3 %reduce-scatter.14.cloned.1.call-start = ((), (), s32[]{:S(2)}) async-start(), calls=%async_computation.17 | async-start | bytes 8519680 | tf_op jit(solution)/shard_map/reduce_scatter | solution.py:315
  1315.3 1410.9 %reduce-scatter.8.cloned.1.call-start = ((), (), s32[]{:S(2)}) async-start(), calls=%async_computation.14 | async-start | bytes 8519680 | tf_op jit(solution)/shard_map/reduce_scatter | solution.py:306
  1320.2 1776.8 %reduce-scatter.16.cloned.1.call-start = ((), (), s32[]{:S(2)}) async-start(), calls=%async_computation.18 | async-start | bytes 23429120 | tf_op jit(solution)/shard_map/reduce_scatter | solution.py:309
  1333.0 2134.8 %reduce-scatter.18.cloned.1.call-start = ((), (), s32[]{:S(2)}) async-start(), calls=%async_computation.19 | async-start | bytes 23429120 | tf_op jit(solution)/shard_map/reduce_scatter | solution.py:310
  1345.7 2492.3 %reduce-scatter.20.cloned.1.call-start = ((), (), s32[]{:S(2)}) async-start(), calls=%async_computation.20 | async-start | bytes 23429120 | tf_op jit(solution)/shard_map/reduce_scatter | solution.py:316
  (117 other events, 3021.2 us)
Sparse Core Ops, SparseCore 0:
  11.2 76.0 all-gather.5
  90.4 69.0 all-gather.7
  587.1 63.8 all-reduce.10
  654.4 91.9 all-gather.9
  749.8 88.2 all-gather.11
  841.4 88.2 all-gather.13
  956.5 43.8 all-reduce.12
  1304.8 73.5 all-reduce.14
  1381.5 326.7 reduce-scatter.9
  1711.0 327.5 reduce-scatter.11
  2041.7 340.8 reduce-scatter.13
  2385.5 340.6 reduce-scatter.7
  2729.4 367.5 reduce-scatter.15
  3100.0 367.7 reduce-scatter.17
  3470.8 367.0 reduce-scatter.19
where the time goes:
time: 3860 us; the launch traced here: 3840 us
  waiting for transfers between devices  2520 us (65%)
  blocking collectives  680 us (18%)
  starting transfers between devices  305 us (8%)
  matrix products  141 us (4%)
  local copies, waits for them, and re-layouts  91.1 us (2%)
  loops' own time  61.9 us (2%)
    unnamed x2, blocking collectives  490 us
    reduce_scatter x1, waiting for transfers between devices, on_device(): lax.psum_scatter(grad_up, ('dp', 'ctx'), scatter_dimension=0, tiled=True)  371 us
    reduce_scatter x1, waiting for transfers between devices, on_device(): lax.psum_scatter(grad_gate, ('dp', 'ctx'), scatter_dimension=0, tiled=True)  371 us
    reduce_scatter x1, waiting for transfers between devices, on_device(): lax.psum_scatter(grad_down, ('dp', 'ctx'), scatter_dimension=1, tiled=True)  370 us
    reduce_scatter x1, waiting for transfers between devices, on_device(): lax.psum_scatter(grad_output, ('dp', 'ctx'), scatter_dimension=1, tiled=T...  344 us
    reduce_scatter x1, waiting for transfers between devices, on_device(): lax.psum_scatter(grad_query, ('dp', 'ctx'), scatter_dimension=0, tiled=True)  344 us
    reduce_scatter x1, waiting for transfers between devices, on_device(): lax.psum_scatter(grad_value, ('dp', 'ctx'), scatter_dimension=0, tiled=True)  329 us
    ppermute x60, starting transfers between devices, shifted(): lax.ppermute(value, axis, [(source, source + steps) for source in range(f...  228 us
  transfers between devices with their start and end apart: 107, of which 27 were waited for; matrix products, arithmetic and copies ran while one was open for 4% of the time, Pallas kernels for 0%

commit v1 on v0

v1 whole, which is shorter than its diff:
```python
import functools

import jax
import jax.numpy as jnp
from jax import lax
from jax.experimental import pallas as pl
from jax.experimental.pallas import tpu as pltpu
from jax.sharding import Mesh, PartitionSpec as P

HD = 64
HEADS = 4
FF_BLOCK = 704
FF_PAD = 768
LOG2E = 1.4426950408889634
epsilon = 1e-05
rope_base = 10000.0
masked_low = -1e30
f32 = jnp.float32
bf16 = jnp.bfloat16

ALL = ("x", "z", "yh", "c")
MODEL = ("yh", "c")

NN = (((1,), (0,)), ((), ()))
NT = (((1,), (1,)), ((), ()))
TN = (((0,), (0,)), ((), ()))

VMEM = pl.BlockSpec(memory_space=pltpu.VMEM)
SMEM = pl.BlockSpec(memory_space=pltpu.SMEM)
BIG = pltpu.CompilerParams(vmem_limit_bytes=56 * 2**20)


def mm(a, b, dims):
    return lax.dot_general(a, b, dims, preferred_element_type=f32)


def turn(u, cosine, sine_signed):
    width = u.shape[-1]
    lane = lax.broadcasted_iota(jnp.int32, u.shape, 1)
    turned = jnp.where(
        lane % HD < HD // 2, pltpu.roll(u, width - HD // 2, 1), pltpu.roll(u, HD // 2, 1)
    )
    return u * cosine + turned * sine_signed


def qkv_kernel(x_ref, w_ref, cos_ref, sin_ref, q_ref, kv_ref):
    lin = mm(x_ref[...], w_ref[...], NN)
    cosine, sine = cos_ref[...], sin_ref[...]
    for part in range(2):
        cols = slice(part * 128, part * 128 + 128)
        q_ref[:, cols] = turn(lin[:, cols], cosine, sine).astype(bf16)
    kv = lin[:, 256:384]
    lane = lax.broadcasted_iota(jnp.int32, kv.shape, 1)
    kv_ref[...] = jnp.where(lane < HD, turn(kv, cosine, sine), kv).astype(bf16)


def qkv_project(x, w, cosine, sine):
    rows, depth = x.shape
    block = 256
    return pl.pallas_call(
        qkv_kernel,
        grid=(rows // block,),
        in_specs=[
            pl.BlockSpec((block, depth), lambda i: (i, 0)),
            pl.BlockSpec((depth, 384), lambda i: (0, 0)),
            pl.BlockSpec((block, 128), lambda i: (i, 0)),
            pl.BlockSpec((block, 128), lambda i: (i, 0)),
        ],
        out_specs=(
            pl.BlockSpec((block, 256), lambda i: (i, 0)),
            pl.BlockSpec((block, 128), lambda i: (i, 0)),
        ),
        out_shape=(
            jax.ShapeDtypeStruct((rows, 256), bf16),
            jax.ShapeDtypeStruct((rows, 128), bf16),
        ),
        cost_estimate=pl.CostEstimate(
            flops=2 * rows * depth * 384, bytes_accessed=6 * 2**20, transcendentals=0
        ),
        compiler_params=BIG,
        name="qkv_project",
    )(x, w, cosine, sine)


def attn_fwd_kernel(
    at_ref, q_ref, kv_ref, o_ref, ot_ref, lse_ref, q_pad, kvt, *, bq, bk
):
    rows = q_ref.shape[0]
    depth, flip = at_ref[0], at_ref[1]
    scale = HD**-0.5 * LOG2E
    for h in range(HEADS):
        q_pad[h, :, :HD] = q_ref[:, h * HD : (h + 1) * HD]
        q_pad[h, :, HD:] = jnp.zeros((rows, HD), bf16)

    def flip_over(b, _):
        kvt[b] = kv_ref[b].T
        return 0

    lax.fori_loop(0, depth + 1, flip_over, 0)
    pair = flip // bq

    def q_step(i, _):
        cols = pl.ds(pl.multiple_of(i * bq, bq), bq)
        queries = [q_pad[h, cols, :] for h in range(HEADS)]

        def block(b, offset, state, masked, count):
            keys = kv_ref[b, pl.ds(offset, count), :]
            values = kvt[b, HD:, pl.ds(offset, count)]
            scores = [mm(keys, queries[h], NT) * scale for h in range(HEADS)]
            if masked:
                k_pos = (lax.broadcasted_iota(jnp.int32, (count, bq), 0) + offset) ^ flip
                q_pos = (lax.broadcasted_iota(jnp.int32, (count, bq), 1) + i * bq) ^ flip
                visible = k_pos <= q_pos
                scores = [jnp.where(visible, s, masked_low) for s in scores]
            out = []
            for h in range(HEADS):
                top, total, acc = state[h]
                s = scores[h]
                new_top = jnp.maximum(top, jnp.max(s, axis=0, keepdims=True))
                p = jnp.exp2(s - new_top)
                fade = jnp.exp2(top - new_top)
                total = total * fade + jnp.sum(p, axis=0, keepdims=True)
                acc = acc * fade + mm(values, p.astype(bf16), NN)
                out.append((new_top, total, acc))
            return tuple(out)

        state = tuple(
            (
                jnp.full((1, bq), masked_low, f32),
                jnp.zeros((1, bq), f32),
                jnp.zeros((HD, bq), f32),
            )
            for _ in range(HEADS)
        )
        state = block(0, pl.multiple_of(i * bq, bq), state, True, bq)
        state = lax.fori_loop(
            0,
            i ^ pair,
            lambda j, st: block(0, pl.multiple_of((j ^ pair) * bq, bq), st, False, bq),
            state,
        )
        per = rows // bk
        state = lax.fori_loop(
            0,
            depth * per,
            lambda j, st: block(
                1 + j // per, pl.multiple_of((j % per) * bk, bk), st, False, bk
            ),
            state,
        )
        outs = []
        for h in range(HEADS):
            top, total, acc = state[h]
            lse_ref[pl.ds(h, 1), cols] = top + jnp.log2(total)
            outs.append(acc * (1.0 / total))
        o_t = jnp.concatenate(outs, 0)
        ot_ref[:, cols] = o_t
        o_ref[cols, :] = o_t.T.astype(bf16)
        return 0

    lax.fori_loop(0, rows // bq, q_step, 0)


def attn_fwd(at, q, kv):
    rows = q.shape[0]
    return pl.pallas_call(
        functools.partial(attn_fwd_kernel, bq=512, bk=512),
        out_shape=(
            jax.ShapeDtypeStruct((rows, HEADS * HD), bf16),
            jax.ShapeDtypeStruct((HEADS * HD, rows), f32),
            jax.ShapeDtypeStruct((HEADS, rows), f32),
        ),
        in_specs=[SMEM, VMEM, VMEM],
        out_specs=(VMEM, VMEM, VMEM),
        scratch_shapes=[
            pltpu.VMEM((HEADS, rows, 128), bf16),
            pltpu.VMEM((4, 128, rows), bf16),
        ],
        cost_estimate=pl.CostEstimate(
            flops=20 * 10**9, bytes_accessed=6 * 2**20, transcendentals=12 * 10**6
        ),
        compiler_params=BIG,
        name="attn_fwd",
    )(at, q, kv)


def attn_bwd_kernel(
    at_ref, q_ref, kv_ref, do_ref, ot_ref, lse_ref, dq_ref, dkv_ref,
    q_pad, do_pad, kt, dqt, delta, *, bq, bk,
):
    rows = q_ref.shape[0]
    depth, flip = at_ref[0], at_ref[1]
    scale = HD**-0.5 * LOG2E
    nothing = jnp.zeros((rows, HD), bf16)
    for h in range(HEADS):
        cols = slice(h * HD, (h + 1) * HD)
        q_pad[h, :, :HD] = q_ref[:, cols]
        q_pad[h, :, HD:] = nothing
        do_pad[h, :, :HD] = nothing
        do_pad[h, :, HD:] = do_ref[:, cols]
    do_t = do_ref[...].astype(f32).T
    for h in range(HEADS):
        cols = slice(h * HD, (h + 1) * HD)
        delta[pl.ds(h, 1), :] = jnp.sum(do_t[cols] * ot_ref[cols, :], axis=0, keepdims=True)

    def flip_over(b, _):
        kt[b] = kv_ref[b].T[:HD]
        return 0

    lax.fori_loop(0, depth + 1, flip_over, 0)
    dqt[...] = jnp.zeros_like(dqt)
    pair = flip // bq

    def tile(b, offset, i, masked, count, dkv):
        keys = kv_ref[b, pl.ds(offset, count), :]
        keys_t = kt[b, :, pl.ds(offset, count)]
        at = pl.ds(pl.multiple_of(i * bq, bq), bq)
        if masked:
            k_pos = (lax.broadcasted_iota(jnp.int32, (count, bq), 0) + offset) ^ flip
            q_pos = (lax.broadcasted_iota(jnp.int32, (count, bq), 1) + i * bq) ^ flip
            visible = k_pos <= q_pos
        for h in range(HEADS):
            query, grad = q_pad[h, at, :], do_pad[h, at, :]
            s = mm(keys, query, NT)
            p = jnp.exp2(s * scale - lse_ref[pl.ds(h, 1), at])
            if masked:
                p = jnp.where(visible, p, 0.0)
            dp = mm(keys, grad, NT)
            ds = (p * (dp - delta[pl.ds(h, 1), at])).astype(bf16)
            dkv = dkv + mm(p.astype(bf16), grad, NN) + mm(ds, query, NN)
            dqt[h * HD : (h + 1) * HD, at] += mm(keys_t, ds, NN)
        return dkv

    lane = lax.broadcasted_iota(jnp.int32, (1, 128), 1)
    out_scale = jnp.where(lane < HD, HD**-0.5, 1.0)
    per = rows // bk

    def far(j, _):
        b, offset = 1 + j // per, pl.multiple_of((j % per) * bk, bk)
        dkv = lax.fori_loop(
            0,
            rows // bq,
            lambda i, st: tile(b, offset, i, False, bk, st),
            jnp.zeros((bk, 128), f32),
        )
        dkv_ref[b, pl.ds(offset, bk), :] = (dkv * out_scale).astype(bf16)
        return 0

    lax.fori_loop(0, depth * per, far, 0)

    def clear(b, _):
        dkv_ref[b] = jnp.zeros(dkv_ref.shape[1:], bf16)
        return 0

    lax.fori_loop(1 + depth, dkv_ref.shape[0], clear, 0)

    def near(j, _):
        offset = pl.multiple_of(j * bq, bq)
        dkv = tile(0, offset, j, True, bq, jnp.zeros((bq, 128), f32))
        dkv = lax.fori_loop(
            (j ^ pair) + 1,
            rows // bq,
            lambda i, st: tile(0, offset, i ^ pair, False, bq, st),
            dkv,
        )
        dkv_ref[0, pl.ds(offset, bq), :] = (dkv * out_scale).astype(bf16)
        return 0

    lax.fori_loop(0, rows // bq, near, 0)
    dq_ref[...] = dqt[...].T * HD**-0.5


def attn_bwd(at, q, kv, do, ot, lse):
    rows = q.shape[0]
    return pl.pallas_call(
        functools.partial(attn_bwd_kernel, bq=512, bk=512),
        out_shape=(
            jax.ShapeDtypeStruct((rows, HEADS * HD), f32),
            jax.ShapeDtypeStruct(kv.shape, bf16),
        ),
        in_specs=[SMEM] + [VMEM] * 5,
        out_specs=(VMEM, VMEM),
        scratch_shapes=[
            pltpu.VMEM((HEADS, rows, 128), bf16),
            pltpu.VMEM((HEADS, rows, 128), bf16),
            pltpu.VMEM((4, HD, rows), bf16),
            pltpu.VMEM((HEADS * HD, rows), f32),
            pltpu.VMEM((HEADS, rows), f32),
        ],
        cost_estimate=pl.CostEstimate(
            flops=50 * 10**9, bytes_accessed=8 * 2**20, transcendentals=12 * 10**6
        ),
        compiler_params=BIG,
        name="attn_bwd",
    )(at, q, kv, do, ot, lse)


def ffn_kernel(hn_ref, cot_ref, w_ref, hid_ref, dgu_ref, y_ref, dn_ref):
    hn, cot = hn_ref[...], cot_ref[...]
    w_gate = w_ref[:, :FF_PAD]
    w_up = w_ref[:, FF_PAD : 2 * FF_PAD]
    w_down = w_ref[:, 2 * FF_PAD :]
    gate = mm(hn, w_gate, NN)
    up = mm(hn, w_up, NN)
    dhid = mm(cot, w_down, NN)
    sg = 1.0 / (1.0 + jnp.exp(-gate))
    act = gate * sg
    hid = (act * up).astype(bf16)
    dgate = (dhid * up * sg * (1.0 + gate * (1.0 - sg))).astype(bf16)
    dup = (dhid * act).astype(bf16)
    hid_ref[...] = hid
    dgu_ref[:, :FF_PAD] = dgate
    dgu_ref[:, FF_PAD:] = dup
    dn_ref[...] = (mm(dgate, w_gate, NT) + mm(dup, w_up, NT)).astype(bf16)
    y_ref[...] = mm(hid, w_down, NT).astype(bf16)


def ffn(hn, cot, w):
    rows, depth = hn.shape
    block = 256
    rowwise = lambda width: pl.BlockSpec((block, width), lambda i: (i, 0))
    return pl.pallas_call(
        ffn_kernel,
        grid=(rows // block,),
        in_specs=[
            rowwise(depth),
            rowwise(depth),
            pl.BlockSpec(w.shape, lambda i: (0, 0), pipeline_mode=pl.Buffered(1)),
        ],
        out_specs=(rowwise(FF_PAD), rowwise(2 * FF_PAD), rowwise(depth), rowwise(depth)),
        out_shape=(
            jax.ShapeDtypeStruct((rows, FF_PAD), bf16),
            jax.ShapeDtypeStruct((rows, 2 * FF_PAD), bf16),
            jax.ShapeDtypeStruct((rows, depth), bf16),
            jax.ShapeDtypeStruct((rows, depth), bf16),
        ),
        cost_estimate=pl.CostEstimate(
            flops=12 * rows * depth * FF_PAD,
            bytes_accessed=30 * 2**20,
            transcendentals=rows * FF_PAD,
        ),
        compiler_params=BIG,
        name="ffn",
    )(hn, cot, w)


def ffn_grad_kernel(hn_ref, cot_ref, dgu_ref, hid_ref, out_ref):
    out_ref[:, : 2 * FF_PAD] = mm(hn_ref[...], dgu_ref[...], TN).astype(bf16)
    out_ref[:, 2 * FF_PAD :] = mm(cot_ref[...], hid_ref[...], TN).astype(bf16)


def ffn_grad(hn, cot, dgu, hid):
    rows, depth = hn.shape
    block = 256
    return pl.pallas_call(
        ffn_grad_kernel,
        grid=(depth // block,),
        in_specs=[
            pl.BlockSpec((rows, block), lambda i: (0, i)),
            pl.BlockSpec((rows, block), lambda i: (0, i)),
            pl.BlockSpec((rows, 2 * FF_PAD), lambda i: (0, 0)),
            pl.BlockSpec((rows, FF_PAD), lambda i: (0, 0)),
        ],
        out_specs=pl.BlockSpec((block, 3 * FF_PAD), lambda i: (i, 0)),
        out_shape=jax.ShapeDtypeStruct((depth, 3 * FF_PAD), bf16),
        cost_estimate=pl.CostEstimate(
            flops=6 * rows * depth * FF_PAD, bytes_accessed=24 * 2**20, transcendentals=0
        ),
        compiler_params=BIG,
        name="ffn_grad",
    )(hn, cot, dgu, hid)


def dqkv_kernel(at_ref, dq_ref, dkv_ref, w_ref, cos_ref, sin_ref, dqkv_ref, dn_ref):
    cosine, sine = cos_ref[...], -sin_ref[...]
    core = at_ref[2]
    for part in range(2):
        cols = slice(part * 128, part * 128 + 128)
        dqkv_ref[:, cols] = turn(dq_ref[:, cols], cosine, sine).astype(bf16)
    dkv = dkv_ref[...]
    lane = lax.broadcasted_iota(jnp.int32, dkv.shape, 1)
    is_key = lane < HD
    turned = jnp.where(is_key, turn(dkv, cosine, sine), dkv)
    mine = jnp.where(is_key, 1 - core, core) > 0
    dqkv_ref[:, 256:] = jnp.where(mine, turned, 0.0).astype(bf16)
    dn_ref[...] = mm(dqkv_ref[...], w_ref[...], NT).astype(bf16)


def dqkv_project(at, dq, dkv, w, cosine, sine):
    rows, depth = dq.shape[0], w.shape[0]
    block = 256
    rowwise = lambda width: pl.BlockSpec((block, width), lambda i: (i, 0))
    return pl.pallas_call(
        dqkv_kernel,
        grid=(rows // block,),
        in_specs=[
            SMEM,
            rowwise(256),
            rowwise(128),
            pl.BlockSpec(w.shape, lambda i: (0, 0)),
            rowwise(128),
            rowwise(128),
        ],
        out_specs=(rowwise(384), rowwise(depth)),
        out_shape=(
            jax.ShapeDtypeStruct((rows, 384), bf16),
            jax.ShapeDtypeStruct((rows, depth), bf16),
        ),
        cost_estimate=pl.CostEstimate(
            flops=2 * rows * depth * 384, bytes_accessed=8 * 2**20, transcendentals=0
        ),
        compiler_params=BIG,
        name="dqkv_project",
    )(at, dq, dkv, w, cosine, sine)


def swap(value, axes):
    count = 2 ** len(axes)
    return lax.ppermute(value, axes, [(i, count - 1 - i) for i in range(count)])


def shifted(value, steps):
    first, last = max(0, -steps), min(4, 4 - steps)
    return lax.ppermute(value, "z", [(i, i + steps) for i in range(first, last)])


def gather_group(own):
    by_l = swap(own, ("yl",))
    by_d = swap(own, ("yh", "yl"))
    by_h = swap(own, ("yh",))
    by_c = swap(own, ("c",))
    return jnp.concatenate(
        [own, by_l, by_c, swap(by_l, ("c",)), by_h, by_d, swap(by_h, ("c",)), swap(by_d, ("c",))], 0
    )


def scatter_group(partial):
    n = partial.shape[0] // 8
    near = swap(partial[2 * n : 4 * n], ("c",))
    far = swap(partial[6 * n : 8 * n], ("c",))
    low = partial[: 2 * n].astype(f32) + near.astype(f32)
    high = (partial[4 * n : 6 * n].astype(f32) + far.astype(f32)).astype(bf16)
    by_l = swap(low[n:].astype(bf16), ("yl",))
    by_d = swap(high[n:], ("yh", "yl"))
    by_h = swap(high[:n], ("yh",))
    return low[:n] + by_l.astype(f32) + by_d.astype(f32) + by_h.astype(f32)


def gather_pieces(own):
    by_c = swap(own, ("c",))
    by_h = swap(own, ("yh",))
    return jnp.concatenate([own, by_c, by_h, swap(by_h, ("c",))], 0)


def to_owners(grad, width):
    parts = lax.all_to_all(grad.reshape(64, 32, width), ALL, 0, 0)
    return jnp.sum(parts.reshape(16, 4, 32, width).astype(f32), 0)


def both_halves(own, other, yl):
    rows = own.shape[0]
    whole = jnp.concatenate([own, other, own], 0)
    return lax.dynamic_slice_in_dim(whole, yl * rows, 2 * rows, 0)


def on_device(
    tokens, w_query, w_key, w_value, w_output, w_gate, w_up, w_down, norm_attn, norm_ffn, cotangent
):
    z, yh = lax.axis_index("z"), lax.axis_index("yh")
    core, yl = lax.axis_index("c"), lax.axis_index("yl")
    gain_one = norm_attn.astype(f32)[:, None]
    gain_two = norm_ffn.astype(f32)[:, None]
    flip = (yh * 4 + core * 2 + yl) * 128
    at = jnp.stack([z, flip, core]).astype(jnp.int32)

    def by_model(w):
        return w.reshape(32, 4, -1).transpose(1, 0, 2)

    def by_head(w):
        return jnp.repeat(w.reshape(32, 2, HD).transpose(1, 0, 2), 2, axis=0)

    scaled = lambda w, gain: (w.astype(f32) * gain).astype(bf16)
    qkv_rows = jnp.concatenate(
        [
            by_model(scaled(w_query, gain_one)),
            by_head(scaled(w_key, gain_one)),
            by_head(scaled(w_value, gain_one)),
        ],
        -1,
    )
    w_qkv = lax.all_to_all(
        jnp.broadcast_to(qkv_rows[None], (16, 4, 32, 384)).reshape(64, 32, 384), ALL, 0, 0
    ).reshape(2048, 384)

    def padded(w):
        return jnp.pad(by_model(w), ((0, 0), (0, 0), (0, FF_PAD - FF_BLOCK)))

    other_rows = jnp.concatenate(
        [
            by_model(w_output.T),
            padded(scaled(w_gate, gain_two)),
            padded(scaled(w_up, gain_two)),
            padded(w_down.T),
        ],
        -1,
    )
    other_rows = lax.all_to_all(other_rows, MODEL, 0, 0).reshape(128, 256 + 3 * FF_PAD)
    w_out = lax.all_gather(other_rows[:, :256], ("x", "z"), axis=0, tiled=True)
    w_ffn = lax.all_gather(other_rows[:, 256:], ("x", "z"), axis=0, tiled=True)

    both = lambda a: lax.dynamic_slice_in_dim(jnp.concatenate([a, a], 0), yl * 128, 256, 0)
    inputs = both(tokens[0]).astype(f32)
    inverse_one = lax.rsqrt(jnp.mean(inputs * inputs, axis=-1, keepdims=True) + epsilon)
    xh = gather_pieces((inputs * inverse_one).astype(bf16))
    inputs, inverse_one = inputs[:128], inverse_one[:128]
    cot_here = both(cotangent[0])
    cot = gather_pieces(cot_here)
    grad_top = cot_here[:128].astype(f32)

    positions = (z * 1024 + (jnp.arange(1024, dtype=jnp.int32) ^ flip)).astype(f32)
    freqs = rope_base ** (-2.0 * jnp.arange(HD // 2, dtype=f32) / HD)
    angles = positions[:, None] * freqs[None, :]
    cosine, sine = jnp.cos(angles), jnp.sin(angles)
    cosine = jnp.concatenate([cosine] * 4, -1)
    sine = jnp.concatenate([-sine, sine, -sine, sine], -1)

    q, kv = qkv_project(xh, w_qkv, cosine, sine)
    kv = jnp.stack([kv, shifted(kv, 1), shifted(kv, 2), shifted(kv, 3)])
    ob, o_t, lse = attn_fwd(at, q, kv)
    branch_one = scatter_group(mm(ob, w_out, NT).astype(bf16))
    middle = inputs + branch_one
    inverse_two = lax.rsqrt(jnp.mean(middle * middle, axis=-1, keepdims=True) + epsilon)
    hn = gather_group((middle * inverse_two).astype(bf16))

    hid, dgu, y, dn2 = ffn(hn, cot, w_ffn)
    dn2 = scatter_group(dn2)
    grad_ffn = ffn_grad(hn, cot, dgu, hid)
    grad_ffn = lax.psum_scatter(grad_ffn, ("x", "z"), scatter_dimension=0, tiled=True)
    grad_ffn = lax.all_to_all(grad_ffn.reshape(4, 32, 3 * FF_PAD), MODEL, 0, 0)
    dh = (
        grad_top
        + inverse_two * dn2
        - middle * inverse_two**3 * jnp.mean(dn2 * middle, axis=-1, keepdims=True)
    )
    gain_grad_two = jnp.sum(dn2 * middle * inverse_two, axis=0)
    dh_all = gather_group(dh.astype(bf16))
    block_out = (middle + scatter_group(y)).astype(bf16)
    block_out = both_halves(block_out, swap(block_out, ("yl",)), yl)

    do = mm(dh_all, w_out, NN).astype(bf16)
    grad_out = to_owners(mm(dh_all, ob, TN).astype(bf16), 256)
    dq, dkv = attn_bwd(at, q, kv, do, o_t, lse)
    dkv = (
        dkv[0].astype(f32)
        + shifted(dkv[1], -1).astype(f32)
        + shifted(dkv[2], -2).astype(f32)
        + shifted(dkv[3], -3).astype(f32)
    )
    other = swap(dkv, ("c",)).reshape(2, 2, 256, 2 * HD)[:, ::-1].reshape(1024, 2 * HD)
    dkv = dkv + other
    dqkv, dn1 = dqkv_project(at, dq, dkv, w_qkv, cosine, sine)
    grad_qkv = to_owners(mm(xh, dqkv, TN).astype(bf16), 384)
    dn1 = scatter_group(dn1)
    input_grad = (
        dh
        + inverse_one * dn1
        - inputs * inverse_one**3 * jnp.mean(dn1 * inputs, axis=-1, keepdims=True)
    )
    gain_grad_one = jnp.sum(dn1 * inputs * inverse_one, axis=0)
    input_grad = both_halves(input_grad, swap(input_grad, ("yl",)), yl)

    gains = jnp.stack([gain_grad_one.reshape(64, 32), gain_grad_two.reshape(64, 32)], 1)
    gains = jnp.sum(lax.all_to_all(gains.reshape(64, 64), ALL, 0, 0, tiled=True), 0)
    gains = gains + swap(gains, ("yl",))

    def joined(parts):
        return parts.transpose(1, 0, 2).reshape(32, -1)

    grad_ffn = grad_ffn.astype(f32)
    ffn_part = lambda k: joined(grad_ffn[:, :, k * FF_PAD : k * FF_PAD + FF_BLOCK])
    by_core = grad_qkv[:, :, 256:].reshape(2, 2, 32, 2 * HD).sum(1)
    return (
        block_out[None],
        input_grad[None],
        joined(grad_qkv[:, :, :256]) * gain_one,
        joined(by_core[:, :, :HD]) * gain_one,
        joined(by_core[:, :, HD:]) * gain_one,
        joined(grad_out).T,
        ffn_part(0) * gain_two,
        ffn_part(1) * gain_two,
        ffn_part(2).T,
        gains[:32] / gain_one[:, 0],
        gains[32:] / gain_two[:, 0],
    )


def solution(mesh):
    mesh = Mesh(mesh.devices.reshape(4, 4, 2, 2, 2), ("x", "z", "yh", "c", "yl"))
    ctx = ("z", "yh", "c")
    rows, cols = P(ALL, "yl"), P("yl", ALL)
    seq = P("x", ctx, None)
    vec = P(ALL)
    in_specs = (seq, rows, rows, rows, cols, rows, rows, cols, vec, vec, seq)
    out_specs = (seq, seq, rows, rows, rows, cols, rows, rows, cols, vec, vec)
    return jax.shard_map(
        on_device, mesh=mesh, in_specs=in_specs, out_specs=out_specs, check_vma=False
    )
```

time: 3860 us -> 587 us (0.15)
  waiting for transfers between devices: 2520 us -> 245 us
  blocking collectives: 680 us -> 16.5 us
  starting transfers between devices: 305 us -> 131 us
  matrix products: 141 us -> 12.9 us
  Pallas kernels: 0 us -> 80.2 us
  loops' own time: 61.9 us -> 0 us
  local copies, waits for them, and re-layouts: 91.1 us -> 32.1 us
    reduce_scatter x7 -> x1, waiting for transfers between devices: 2130 us -> 0.01 us  [on_device(): lax.psum_scatter(grad_ffn, ('x', 'z'), scatter_dimension=0, tiled=True)]
    unnamed x2 -> x0, blocking collectives: 490 us -> none
    all_gather x5 -> x2, waiting for transfers between devices: 257 us -> 0.01 us  [the longest x1 0.01 us: on_device(): w_out = lax.all_gather(other_rows[:, :256], ('x', 'z'), axis=0, tiled=True)]
    ppermute x92 -> x50, starting transfers between devices: 304 us -> 83.4 us  [the longest x44 70.1 us: swap(): return lax.ppermute(value, axes, [(i, count - 1 - i) for i in range(count)])]
    ppermute x92 -> x50, waiting for transfers between devices: 18.8 us -> 209 us  [the longest x44 132 us: swap(): return lax.ppermute(value, axes, [(i, count - 1 - i) for i in range(count)])]
    all_gather x2 -> x0, blocking collectives: 190 us -> none  [the longest x1 96.7 us: on_device(): lax.all_gather(rows_local[1], ('dp', 'ctx'), axis=0, tiled=True)]
    dot_general x35 -> x4, matrix products: 141 us -> 12.9 us  [mm(): return lax.dot_general(a, b, dims, preferred_element_type=f32)]
    psum x3 -> x0, waiting for transfers between devices: 115 us -> none  [the longest x1 62.2 us: on_device(): lax.psum(jnp.dot(attn_low, wo_full, preferred_element_type=f32).astype(jn...]
  transfers between devices with their start and end apart: 107 -> 58, of which waited for: 27 -> 25; matrix products, arithmetic and copies ran while one was open for 4% -> 13% of each run, Pallas kernels for 0% -> 9%
where the time goes in v1:
time: 587 us; the launch traced here: 578 us
  waiting for transfers between devices  245 us (42%)
  starting transfers between devices  131 us (22%)
  Pallas kernels  80.2 us (14%)
  other arithmetic  45.2 us (8%)
  local copies, waits for them, and re-layouts  32.1 us (5%)
  blocking collectives  16.5 us (3%)
  between operations  15 us (3%)
  matrix products  12.9 us (2%)
    ppermute x44, waiting for transfers between devices, swap(): return lax.ppermute(value, axes, [(i, count - 1 - i) for i in range(count)])  132 us
    ppermute x6, waiting for transfers between devices, shifted(): lax.ppermute(value, 'z', [(i, i + steps) for i in range(first, last)])  77.3 us
    ppermute x44, starting transfers between devices, swap(): return lax.ppermute(value, axes, [(i, count - 1 - i) for i in range(count)])  70.1 us
    pallas_call x1, Pallas kernels, ffn(): pl.pallas_call(ffn_kernel, grid=(rows // block,), in_specs=[rowwise(depth...  27.1 us
    all_to_all x2, starting transfers between devices, to_owners(): parts = lax.all_to_all(grad.reshape(64, 32, width), ALL, 0, 0)  21.3 us
    all_to_all x1, waiting for transfers between devices, on_device(): lax.all_to_all(gains.reshape(64, 64), ALL, 0, 0, tiled=True)  17.2 us
    all_to_all x1, blocking collectives, on_device(): lax.all_to_all(other_rows, MODEL, 0, 0).reshape(128, 256 + 3 * FF_PAD)  16.5 us
    pallas_call x1, Pallas kernels, ffn_grad(): pl.pallas_call(ffn_grad_kernel, grid=(depth // block,), in_specs=[pl.Bloc...  16 us
  transfers between devices with their start and end apart: 58, of which 25 were waited for; matrix products, arithmetic and copies ran while one was open for 13% of the time, Pallas kernels for 9%

profile of v1, /device:TPU:1, one launch (start us, length us, event | category | flops | bytes accessed | tf_op | source)
XLA Modules:
  0.0 578.4 jit_solution(6678291033658204130)
XLA Ops:
  11.8 16.5 %all_to_all.34 = bf16[4,32,2560]{2,1,0:T(8,128)(2,1)S(1)} all-to-all(bf16[4,32,2560]{2,1,0:T(8,128)(2,1)S(1)} %fusion.26), channel_id=1, replica_groups=mesh['x'=4,'z'=4,'yh'=2,'c'=2,'yl'=2] {'yh','c'}, dimensions={0} | all-to-all | bytes 1310720 | tf_op jit(solution)/shard_map/all_to_all | solution.py:507
  33.3 12.0 %all-to-all-start = ((bf16[64,32,384]{2,1,0:T(8,128)(2,1)}), bf16[64,32,384]{2,1,0:T(8,128)(2,1)}, u32[]{:S(2)}, u32[]{:S(2)}) async-start(bf16[64,32,384]{2,1,0:T(8,128)(2,1)} %bitcast.91), calls=%async_computation | async-start | bytes 3145728 | tf_op jit(solution)/shard_map/all_to_all | solution.py:491
  45.9 22.8 %collective-permute-done.1 = bf16[256,2048]{1,0:T(8,128)(2,1)} collective-permute-done((bf16[256,2048]{1,0:T(8,128)(2,1)S(1)}, bf16[256,2048]{1,0:T(8,128)(2,1)}, u32[]{:S(2)}, u32[]{:S(2)}) %collective-permute-start.1) | collective-permute-done | bytes 1048608 | tf_op jit(solution)/shard_map/ppermute | solution.py:419
  79.7 6.7 %qkv_project.1 = (bf16[1024,256]{1,0:T(8,128)(2,1)}, bf16[1024,128]{1,0:T(8,128)(2,1)}) custom-call(bf16[1024,2048]{1,0:T(8,128)(2,1)} %pad_maximum_fusion.x_ref, bf16[2048,384]{1,0:T(8,128)(2,1)} %bitcast.10.w_ref, f32[1024,128]{1,0:T(8,128)} %get-tuple-element.100.cos_ref, f32[1024,128]{1,0:T(8,128)} %get-tuple-element.101.sin_ref), custom_call_target="tpu_custom_call" | custom-call | flops 1610612736 | bytes 6291456 | tf_op jit(solution)/shard_map/qkv_project/pallas_call | solution.py:60
  86.4 5.7 collective-permute-start.5
  96.5 12.7 %collective-permute-done.5 = bf16[1024,128]{1,0:T(8,128)(2,1)S(1)} collective-permute-done((bf16[1024,128]{1,0:T(8,128)(2,1)}, bf16[1024,128]{1,0:T(8,128)(2,1)S(1)}, u32[]{:S(2)}, u32[]{:S(2)}) %collective-permute-start.5) | collective-permute-done | bytes 262176 | tf_op jit(solution)/shard_map/ppermute | solution.py:424
  114.6 8.9 %attn_fwd.1 = (bf16[1024,256]{1,0:T(8,128)(2,1)}, f32[256,1024]{1,0:T(8,128)}, f32[4,1024]{1,0:T(4,128)}) custom-call(s32[3]{0:T(128)} %pad_add_fusion.at_ref, bf16[1024,256]{1,0:T(8,128)(2,1)} %get-tuple-element.24.q_ref, bf16[4,1024,128]{2,1,0:T(8,128)(2,1)} %pad_maximum_fusion.2.kv_ref), custom_call_target="tpu_custom_call" | custom-call | flops 20000000000 | bytes 6291456 | tf_op jit(solution)/shard_map/attn_fwd/pallas_call | solution.py:166
  137.0 17.2 %collective-permute-done.19 = bf16[256,2048]{1,0:T(8,128)(2,1)S(1)} collective-permute-done((bf16[256,2048]{1,0:T(8,128)(2,1)S(1)}, bf16[256,2048]{1,0:T(8,128)(2,1)S(1)}, u32[]{:S(2)}, u32[]{:S(2)}) %collective-permute-start.19) | collective-permute-done | bytes 1048608 | tf_op jit(solution)/shard_map/ppermute | solution.py:419
  156.5 8.7 %collective-permute-done.7 = bf16[128,2048]{1,0:T(8,128)(2,1)S(1)} collective-permute-done((bf16[128,2048]{1,0:T(8,128)(2,1)S(1)}, bf16[128,2048]{1,0:T(8,128)(2,1)S(1)}, u32[]{:S(2)}, u32[]{:S(2)}) %collective-permute-start.7) | collective-permute-done | bytes 524320 | tf_op jit(solution)/shard_map/ppermute | solution.py:419
  167.1 9.6 %collective-permute-done.10 = bf16[128,2048]{1,0:T(8,128)(2,1)S(1)} collective-permute-done((bf16[128,2048]{1,0:T(8,128)(2,1)S(1)}, bf16[128,2048]{1,0:T(8,128)(2,1)S(1)}, u32[]{:S(2)}, u32[]{:S(2)}) %collective-permute-start.10) | collective-permute-done | bytes 524320 | tf_op jit(solution)/shard_map/ppermute | solution.py:419
  183.6 6.6 %collective-permute-done.11 = bf16[128,2048]{1,0:T(8,128)(2,1)S(1)} collective-permute-done((bf16[128,2048]{1,0:T(8,128)(2,1)S(1)}, bf16[128,2048]{1,0:T(8,128)(2,1)S(1)}, u32[]{:S(2)}, u32[]{:S(2)}) %collective-permute-start.11) | collective-permute-done | bytes 524320 | tf_op jit(solution)/shard_map/ppermute | solution.py:419
  197.0 9.3 %collective-permute-start.17 = (bf16[128,2048]{1,0:T(8,128)(2,1)S(1)}, bf16[128,2048]{1,0:T(8,128)(2,1)S(1)}, u32[]{:S(2)}, u32[]{:S(2)}) collective-permute-start(bf16[128,2048]{1,0:T(8,128)(2,1)S(1)} %collective-permute-done.15), channel_id=1, source_target_pairs={{0,2},{2,0},{1,3},{3,1},{4,6},{6,4},{5,7},{7,5},{8,10},{10,8},{9,1... | collective-permute-start | bytes 1572872 | tf_op jit(solution)/shard_map/ppermute | solution.py:419
  212.3 27.1 %ffn.1 = (bf16[1024,768]{1,0:T(8,128)(2,1)}, bf16[1024,1536]{1,0:T(8,128)(2,1)}, bf16[1024,2048]{1,0:T(8,128)(2,1)}, bf16[1024,2048]{1,0:T(8,128)(2,1)}) custom-call(bf16[1024,2048]{1,0:T(8,128)(2,1)} %constant_dynamic-update-slice_fusion.hn_ref, bf16[1024,2048]{1,0:T(8,128)(2,1)} %pad_maximum_fusion.1.cot_ref, ...), custom_call_target="tpu_custom_call" | custom-call | flops 19327352832 | bytes 31457280 | tf_op jit(solution)/shard_map/ffn/pallas_call | solution.py:322
  243.1 16.0 %ffn_grad.1 = bf16[2048,2304]{1,0:T(8,128)(2,1)} custom-call(bf16[1024,2048]{1,0:T(8,128)(2,1)} %constant_dynamic-update-slice_fusion.hn_ref, bf16[1024,2048]{1,0:T(8,128)(2,1)} %pad_maximum_fusion.1.cot_ref, bf16[1024,1536]{1,0:T(8,128)(2,1)} %get-tuple-element.35.dgu_ref, bf16[1024,768]{1,0:T(8,128)(2,1)} %get-tuple-element.36.hid_ref), custom_call_target="tpu_custom_call" | custom-call | flops 9663676416 | bytes 25165824 | tf_op jit(solution)/shard_map/ffn_grad/pallas_call | solution.py:355
  270.2 7.2 %collective-permute-done.22 = bf16[128,2048]{1,0:T(8,128)(2,1)S(1)} collective-permute-done((bf16[128,2048]{1,0:T(8,128)(2,1)S(1)}, bf16[128,2048]{1,0:T(8,128)(2,1)S(1)}, u32[]{:S(2)}, u32[]{:S(2)}) %collective-permute-start.22) | collective-permute-done | bytes 524320 | tf_op jit(solution)/shard_map/ppermute | solution.py:419
  279.3 10.2 %collective-permute-done.25 = bf16[128,2048]{1,0:T(8,128)(2,1)S(1)} collective-permute-done((bf16[128,2048]{1,0:T(8,128)(2,1)S(1)}, bf16[128,2048]{1,0:T(8,128)(2,1)S(1)}, u32[]{:S(2)}, u32[]{:S(2)}) %collective-permute-start.25) | collective-permute-done | bytes 524320 | tf_op jit(solution)/shard_map/ppermute | solution.py:419
  289.5 10.5 %collective-permute-done.28 = bf16[128,2048]{1,0:T(8,128)(2,1)S(1)} collective-permute-done((bf16[128,2048]{1,0:T(8,128)(2,1)S(1)}, bf16[128,2048]{1,0:T(8,128)(2,1)S(1)}, u32[]{:S(2)}, u32[]{:S(2)}) %collective-permute-start.28) | collective-permute-done | bytes 524320 | tf_op jit(solution)/shard_map/ppermute | solution.py:419
  301.7 10.3 %collective-permute-done.31 = bf16[128,2048]{1,0:T(8,128)(2,1)S(1)} collective-permute-done((bf16[128,2048]{1,0:T(8,128)(2,1)S(1)}, bf16[128,2048]{1,0:T(8,128)(2,1)S(1)}, u32[]{:S(2)}, u32[]{:S(2)}) %collective-permute-start.31) | collective-permute-done | bytes 524320 | tf_op jit(solution)/shard_map/ppermute | solution.py:419
  320.9 5.5 collective-permute-done.32
  331.7 8.1 %collective-permute-start.38 = (bf16[128,2048]{1,0:T(8,128)(2,1)S(1)}, bf16[128,2048]{1,0:T(8,128)(2,1)S(1)}, u32[]{:S(2)}, u32[]{:S(2)}) collective-permute-start(bf16[128,2048]{1,0:T(8,128)(2,1)S(1)} %collective-permute-done.36), channel_id=1, source_target_pairs={{0,2},{2,0},{1,3},{3,1},{4,6},{6,4},{5,7},{7,5},{8,10},{10,8},{9,1... | collective-permute-start | bytes 1572872 | tf_op jit(solution)/shard_map/ppermute | solution.py:419
  345.5 14.4 %attn_bwd.1 = (f32[1024,256]{1,0:T(8,128)}, bf16[4,1024,128]{2,1,0:T(8,128)(2,1)}) custom-call(s32[3]{0:T(128)} %pad_add_fusion.at_ref, bf16[1024,256]{1,0:T(8,128)(2,1)} %get-tuple-element.24.q_ref, bf16[4,1024,128]{2,1,0:T(8,128)(2,1)} %pad_maximum_fusion.2.kv_ref, bf16[1024,256]{1,0:T(8,128)(2,1)} %convolution_convert_fusion.3.do_ref, ...), custom_call_target="tpu_custom_call" | custom-call | flops 49999998976 | bytes 8388608 | tf_op jit(solution)/shard_map/attn_bwd/pallas_call | solution.py:275
  364.9 26.5 %collective-permute-done.39 = bf16[1024,128]{1,0:T(8,128)(2,1)S(1)} collective-permute-done((bf16[1024,128]{1,0:T(8,128)(2,1)S(1)}, bf16[1024,128]{1,0:T(8,128)(2,1)S(1)}, u32[]{:S(2)}, u32[]{:S(2)}) %collective-permute-start.39) | collective-permute-done | bytes 262176 | tf_op jit(solution)/shard_map/ppermute | solution.py:424
  391.4 34.9 %collective-permute-done.41 = bf16[1024,128]{1,0:T(8,128)(2,1)S(1)} collective-permute-done((bf16[1024,128]{1,0:T(8,128)(2,1)S(1)}, bf16[1024,128]{1,0:T(8,128)(2,1)S(1)}, u32[]{:S(2)}, u32[]{:S(2)}) %collective-permute-start.41) | collective-permute-done | bytes 262176 | tf_op jit(solution)/shard_map/ppermute | solution.py:424
  433.5 10.0 %all-to-all-start.3 = ((bf16[64,32,256]{2,1,0:T(8,128)(2,1)}), bf16[64,32,256]{2,1,0:T(8,128)(2,1)S(1)}, u32[]{:S(2)}, u32[]{:S(2)}) async-start(bf16[64,32,256]{2,1,0:T(8,128)(2,1)} %bitcast.98), calls=%async_computation.3 | async-start | bytes 2097152 | tf_op jit(solution)/shard_map/all_to_all | solution.py:456
  447.5 7.1 %dqkv_project.1 = (bf16[1024,384]{1,0:T(8,128)(2,1)}, bf16[1024,2048]{1,0:T(8,128)(2,1)}) custom-call(s32[3]{0:T(128)} %pad_add_fusion.at_ref, f32[1024,256]{1,0:T(8,128)} %get-tuple-element.31.dq_ref, f32[1024,128]{1,0:T(8,128)} %bitcast_add_fusion.dkv_ref, bf16[2048,384]{1,0:T(8,128)(2,1)} %bitcast.10.w_ref, f32[1024,128]{1,0:T(8,128)} %get-tuple-element.100.cos_ref, ...), custom_call_target="tpu_custom_call" | custom-call | flops 1610612736 | bytes 8388608 | tf_op jit(solution)/shard_map/dqkv_project/pallas_call | solution.py:393
  463.8 11.4 %all-to-all-start.2 = ((bf16[64,32,384]{2,1,0:T(8,128)(2,1)}), bf16[64,32,384]{2,1,0:T(8,128)(2,1)}, u32[]{:S(2)}, u32[]{:S(2)}) async-start(bf16[64,32,384]{2,1,0:T(8,128)(2,1)} %bitcast.95), calls=%async_computation.2 | async-start | bytes 3145728 | tf_op jit(solution)/shard_map/all_to_all | solution.py:456
  488.6 11.4 %all-to-all-done.2 = bf16[64,32,384]{2,1,0:T(8,128)(2,1)} async-done(((bf16[64,32,384]{2,1,0:T(8,128)(2,1)}), bf16[64,32,384]{2,1,0:T(8,128)(2,1)}, u32[]{:S(2)}, u32[]{:S(2)}) %all-to-all-start.2) | async-done | bytes 1572896 | tf_op jit(solution)/shard_map/all_to_all | solution.py:456
  503.1 11.2 %collective-permute-done.46 = bf16[128,2048]{1,0:T(8,128)(2,1)} collective-permute-done((bf16[128,2048]{1,0:T(8,128)(2,1)}, bf16[128,2048]{1,0:T(8,128)(2,1)}, u32[]{:S(2)}, u32[]{:S(2)}) %collective-permute-start.46) | collective-permute-done | bytes 524320 | tf_op jit(solution)/shard_map/ppermute | solution.py:419
  523.4 8.7 %all-to-all-start.5 = ((f32[64,1,64]{2,1,0:T(1,128)}), f32[64,1,64]{2,1,0:T(1,128)S(1)}, u32[]{:S(2)}, u32[]{:S(2)}) async-start(f32[64,1,64]{2,1,0:T(1,128)} %copy.101), calls=%async_computation.6 | async-start | bytes 65536 | tf_op jit(solution)/shard_map/all_to_all | solution.py:573
  532.4 17.2 %all-to-all-done.5 = f32[64,1,64]{2,1,0:T(1,128)S(1)} async-done(((f32[64,1,64]{2,1,0:T(1,128)}), f32[64,1,64]{2,1,0:T(1,128)S(1)}, u32[]{:S(2)}, u32[]{:S(2)}) %all-to-all-start.5) | async-done | bytes 16416 | tf_op jit(solution)/shard_map/all_to_all | solution.py:573
  552.2 5.6 all-to-all-start.4
  560.4 7.5 %all-to-all-done.4 = bf16[4,32,2304]{2,1,0:T(8,128)(2,1)S(1)} async-done(((bf16[4,32,2304]{2,1,0:T(8,128)(2,1)}), bf16[4,32,2304]{2,1,0:T(8,128)(2,1)S(1)}, u32[]{:S(2)}, u32[]{:S(2)}) %all-to-all-start.4) | async-done | bytes 589856 | tf_op jit(solution)/shard_map/all_to_all | solution.py:539
  (257 shorter events, 166.1 us)
Async XLA Ops:
  7.2 116.3 %all-gather.3.cloned.1.call-start = ((), (), s32[]{:S(2)}) async-start(), calls=%async_computation.7 | async-start | bytes 1114112 | tf_op jit(solution)/shard_map/all_gather | solution.py:508
  28.9 183.4 %all-gather.5.cloned.1.call-start = ((), (), s32[]{:S(2)}) async-start(), calls=%async_computation.8 | async-start | bytes 10027008 | tf_op jit(solution)/shard_map/all_gather | solution.py:509
  30.8 37.9 %collective-permute-start.1 = (bf16[256,2048]{1,0:T(8,128)(2,1)S(1)}, bf16[256,2048]{1,0:T(8,128)(2,1)}, u32[]{:S(2)}, u32[]{:S(2)}) collective-permute-start(bf16[256,2048]{1,0:T(8,128)(2,1)S(1)} %multiply_convert_fusion), channel_id=1, source_target_pairs={{0,4},{4,0},{1,5},{5,1},{2,6},{6,2},{3,7},{7,3},{8,12},{12,8},{9,1... | collective-permute-start | bytes 3145736 | tf_op jit(solution)/shard_map/ppermute | solution.py:419
  33.3 46.3 %all-to-all-start = ((bf16[64,32,384]{2,1,0:T(8,128)(2,1)}), bf16[64,32,384]{2,1,0:T(8,128)(2,1)}, u32[]{:S(2)}, u32[]{:S(2)}) async-start(bf16[64,32,384]{2,1,0:T(8,128)(2,1)} %bitcast.91), calls=%async_computation | async-start | bytes 3145728 | tf_op jit(solution)/shard_map/all_to_all | solution.py:491
  45.3 506.9 %reduce-scatter.2.cloned.1.call-start = ((), (), s32[]{:S(2)}) async-start(), calls=%async_computation.9 | async-start | bytes 10027008 | tf_op jit(solution)/shard_map/reduce_scatter | solution.py:538
  45.3 30.7 %collective-permute-start = (bf16[256,2048]{1,0:T(8,128)(2,1)S(1)}, bf16[256,2048]{1,0:T(8,128)(2,1)}, u32[]{:S(2)}, u32[]{:S(2)}) collective-permute-start(bf16[256,2048]{1,0:T(8,128)(2,1)S(1)} %multiply_convert_fusion), channel_id=1, source_target_pairs={{0,2},{2,0},{1,3},{3,1},{4,6},{6,4},{5,7},{7,5},{8,10},{10,8},{9,1... | collective-permute-start | bytes 3145736 | tf_op jit(solution)/shard_map/ppermute | solution.py:419
  86.4 22.8 %collective-permute-start.5 = (bf16[1024,128]{1,0:T(8,128)(2,1)}, bf16[1024,128]{1,0:T(8,128)(2,1)S(1)}, u32[]{:S(2)}, u32[]{:S(2)}) collective-permute-start(bf16[1024,128]{1,0:T(8,128)(2,1)} %get-tuple-element.25), channel_id=1, source_target_pairs={{0,24},{1,25},{2,26},{3,27},{4,28},{5,29},{6,30},{7,31},{32,56},{3... | collective-permute-start | bytes 786440 | tf_op jit(solution)/shard_map/ppermute | solution.py:424
  128.3 25.8 %collective-permute-start.19 = (bf16[256,2048]{1,0:T(8,128)(2,1)S(1)}, bf16[256,2048]{1,0:T(8,128)(2,1)S(1)}, u32[]{:S(2)}, u32[]{:S(2)}) collective-permute-start(bf16[256,2048]{1,0:T(8,128)(2,1)S(1)} %fusion.11), channel_id=1, source_target_pairs={{0,4},{4,0},{1,5},{5,1},{2,6},{6,2},{3,7},{7,3},{8,12},{12,8},{9,1... | collective-permute-start | bytes 3145736 | tf_op jit(solution)/shard_map/ppermute | solution.py:419
  131.7 33.5 %collective-permute-start.7 = (bf16[128,2048]{1,0:T(8,128)(2,1)S(1)}, bf16[128,2048]{1,0:T(8,128)(2,1)S(1)}, u32[]{:S(2)}, u32[]{:S(2)}) collective-permute-start(bf16[128,2048]{1,0:T(8,128)(2,1)S(1)} %slice.302), channel_id=1, source_target_pairs={{0,1},{1,0},{2,3},{3,2},{4,5},{5,4},{6,7},{7,6},{8,9},{9,8},{10,11... | collective-permute-start | bytes 1572872 | tf_op jit(solution)/shard_map/ppermute | solution.py:419
  133.2 33.8 %collective-permute-start.9 = (bf16[128,2048]{1,0:T(8,128)(2,1)S(1)}, bf16[128,2048]{1,0:T(8,128)(2,1)S(1)}, u32[]{:S(2)}, u32[]{:S(2)}) collective-permute-start(bf16[128,2048]{1,0:T(8,128)(2,1)S(1)} %get-tuple-element.81), channel_id=1, source_target_pairs={{0,5},{1,4},{4,1},{5,0},{2,7},{3,6},{6,3},{7,2},{8,13},{9,12},{12,... | collective-permute-start | bytes 1572872 | tf_op jit(solution)/shard_map/ppermute | solution.py:419
  134.7 42.0 %collective-permute-start.10 = (bf16[128,2048]{1,0:T(8,128)(2,1)S(1)}, bf16[128,2048]{1,0:T(8,128)(2,1)S(1)}, u32[]{:S(2)}, u32[]{:S(2)}) collective-permute-start(bf16[128,2048]{1,0:T(8,128)(2,1)S(1)} %get-tuple-element.82), channel_id=1, source_target_pairs={{0,4},{4,0},{1,5},{5,1},{2,6},{6,2},{3,7},{7,3},{8,12},{12,8},{9,1... | collective-permute-start | bytes 1572872 | tf_op jit(solution)/shard_map/ppermute | solution.py:419
  135.5 46.0 %collective-permute-start.18 = (bf16[256,2048]{1,0:T(8,128)(2,1)S(1)}, bf16[256,2048]{1,0:T(8,128)(2,1)S(1)}, u32[]{:S(2)}, u32[]{:S(2)}) collective-permute-start(bf16[256,2048]{1,0:T(8,128)(2,1)S(1)} %fusion.11), channel_id=1, source_target_pairs={{0,2},{2,0},{1,3},{3,1},{4,6},{6,4},{5,7},{7,5},{8,10},{10,8},{9,1... | collective-permute-start | bytes 3145736 | tf_op jit(solution)/shard_map/ppermute | solution.py:419
  154.2 40.5 %collective-permute-start.20 = (bf16[256,2048]{1,0:T(8,128)(2,1)S(1)}, bf16[256,2048]{1,0:T(8,128)(2,1)S(1)}, u32[]{:S(2)}, u32[]{:S(2)}) collective-permute-start(bf16[256,2048]{1,0:T(8,128)(2,1)S(1)} %collective-permute-done.19), channel_id=1, source_target_pairs={{0,2},{2,0},{1,3},{3,1},{4,6},{6,4},{5,7},{7,5},{8,10},{10,8},{9,1... | collective-permute-start | bytes 3145736 | tf_op jit(solution)/shard_map/ppermute | solution.py:419
  180.7 25.7 %collective-permute-start.14 = (bf16[128,2048]{1,0:T(8,128)(2,1)S(1)}, bf16[128,2048]{1,0:T(8,128)(2,1)S(1)}, u32[]{:S(2)}, u32[]{:S(2)}) collective-permute-start(bf16[128,2048]{1,0:T(8,128)(2,1)S(1)} %get-tuple-element.47), channel_id=1, source_target_pairs={{0,4},{4,0},{1,5},{5,1},{2,6},{6,2},{3,7},{7,3},{8,12},{12,8},{9,1... | collective-permute-start | bytes 1572872 | tf_op jit(solution)/shard_map/ppermute | solution.py:419
  181.4 25.7 %collective-permute-start.12 = (bf16[128,2048]{1,0:T(8,128)(2,1)S(1)}, bf16[128,2048]{1,0:T(8,128)(2,1)S(1)}, u32[]{:S(2)}, u32[]{:S(2)}) collective-permute-start(bf16[128,2048]{1,0:T(8,128)(2,1)S(1)} %get-tuple-element.47), channel_id=1, source_target_pairs={{0,2},{2,0},{1,3},{3,1},{4,6},{6,4},{5,7},{7,5},{8,10},{10,8},{9,1... | collective-permute-start | bytes 1572872 | tf_op jit(solution)/shard_map/ppermute | solution.py:419
  265.9 23.7 %collective-permute-start.25 = (bf16[128,2048]{1,0:T(8,128)(2,1)S(1)}, bf16[128,2048]{1,0:T(8,128)(2,1)S(1)}, u32[]{:S(2)}, u32[]{:S(2)}) collective-permute-start(bf16[128,2048]{1,0:T(8,128)(2,1)S(1)} %get-tuple-element.80), channel_id=1, source_target_pairs={{0,4},{4,0},{1,5},{5,1},{2,6},{6,2},{3,7},{7,3},{8,12},{12,8},{9,1... | collective-permute-start | bytes 1572872 | tf_op jit(solution)/shard_map/ppermute | solution.py:419
  268.8 31.2 %collective-permute-start.28 = (bf16[128,2048]{1,0:T(8,128)(2,1)S(1)}, bf16[128,2048]{1,0:T(8,128)(2,1)S(1)}, u32[]{:S(2)}, u32[]{:S(2)}) collective-permute-start(bf16[128,2048]{1,0:T(8,128)(2,1)S(1)} %slice.300), channel_id=1, source_target_pairs={{0,1},{1,0},{2,3},{3,2},{4,5},{5,4},{6,7},{7,6},{8,9},{9,8},{10,11... | collective-permute-start | bytes 1572872 | tf_op jit(solution)/shard_map/ppermute | solution.py:419
  269.0 32.7 %collective-permute-start.30 = (bf16[128,2048]{1,0:T(8,128)(2,1)S(1)}, bf16[128,2048]{1,0:T(8,128)(2,1)S(1)}, u32[]{:S(2)}, u32[]{:S(2)}) collective-permute-start(bf16[128,2048]{1,0:T(8,128)(2,1)S(1)} %get-tuple-element.77), channel_id=1, source_target_pairs={{0,5},{1,4},{4,1},{5,0},{2,7},{3,6},{6,3},{7,2},{8,13},{9,12},{12,... | collective-permute-start | bytes 1572872 | tf_op jit(solution)/shard_map/ppermute | solution.py:419
  277.4 34.6 %collective-permute-start.31 = (bf16[128,2048]{1,0:T(8,128)(2,1)S(1)}, bf16[128,2048]{1,0:T(8,128)(2,1)S(1)}, u32[]{:S(2)}, u32[]{:S(2)}) collective-permute-start(bf16[128,2048]{1,0:T(8,128)(2,1)S(1)} %get-tuple-element.78), channel_id=1, source_target_pairs={{0,4},{4,0},{1,5},{5,1},{2,6},{6,2},{3,7},{7,3},{8,12},{12,8},{9,1... | collective-permute-start | bytes 1572872 | tf_op jit(solution)/shard_map/ppermute | solution.py:419
  316.4 23.4 %collective-permute-start.35 = (bf16[128,2048]{1,0:T(8,128)(2,1)S(1)}, bf16[128,2048]{1,0:T(8,128)(2,1)S(1)}, u32[]{:S(2)}, u32[]{:S(2)}) collective-permute-start(bf16[128,2048]{1,0:T(8,128)(2,1)S(1)} %get-tuple-element.43), channel_id=1, source_target_pairs={{0,4},{4,0},{1,5},{5,1},{2,6},{6,2},{3,7},{7,3},{8,12},{12,8},{9,1... | collective-permute-start | bytes 1572872 | tf_op jit(solution)/shard_map/ppermute | solution.py:419
  318.1 23.6 %collective-permute-start.33 = (bf16[128,2048]{1,0:T(8,128)(2,1)S(1)}, bf16[128,2048]{1,0:T(8,128)(2,1)S(1)}, u32[]{:S(2)}, u32[]{:S(2)}) collective-permute-start(bf16[128,2048]{1,0:T(8,128)(2,1)S(1)} %get-tuple-element.43), channel_id=1, source_target_pairs={{0,2},{2,0},{1,3},{3,1},{4,6},{6,4},{5,7},{7,5},{8,10},{10,8},{9,1... | collective-permute-start | bytes 1572872 | tf_op jit(solution)/shard_map/ppermute | solution.py:419
  361.0 30.4 %collective-permute-start.39 = (bf16[1024,128]{1,0:T(8,128)(2,1)S(1)}, bf16[1024,128]{1,0:T(8,128)(2,1)S(1)}, u32[]{:S(2)}, u32[]{:S(2)}) collective-permute-start(bf16[1024,128]{1,0:T(8,128)(2,1)S(1)} %get-tuple-element.73), channel_id=1, source_target_pairs={{8,0},{16,8},{24,16},{9,1},{17,9},{25,17},{10,2},{18,10},{26,18},{... | collective-permute-start | bytes 786440 | tf_op jit(solution)/shard_map/ppermute | solution.py:424
  362.3 63.9 %collective-permute-start.41 = (bf16[1024,128]{1,0:T(8,128)(2,1)S(1)}, bf16[1024,128]{1,0:T(8,128)(2,1)S(1)}, u32[]{:S(2)}, u32[]{:S(2)}) collective-permute-start(bf16[1024,128]{1,0:T(8,128)(2,1)S(1)} %get-tuple-element.74), channel_id=1, source_target_pairs={{24,0},{25,1},{26,2},{27,3},{28,4},{29,5},{30,6},{31,7},{56,32},{5... | collective-permute-start | bytes 786440 | tf_op jit(solution)/shard_map/ppermute | solution.py:424
  363.6 62.6 %collective-permute-start.40 = (bf16[1024,128]{1,0:T(8,128)(2,1)S(1)}, bf16[1024,128]{1,0:T(8,128)(2,1)S(1)}, u32[]{:S(2)}, u32[]{:S(2)}) collective-permute-start(bf16[1024,128]{1,0:T(8,128)(2,1)S(1)} %get-tuple-element.75), channel_id=1, source_target_pairs={{16,0},{24,8},{17,1},{25,9},{18,2},{26,10},{19,3},{27,11},{20,4},{... | collective-permute-start | bytes 786440 | tf_op jit(solution)/shard_map/ppermute | solution.py:424
  433.5 30.3 %all-to-all-start.3 = ((bf16[64,32,256]{2,1,0:T(8,128)(2,1)}), bf16[64,32,256]{2,1,0:T(8,128)(2,1)S(1)}, u32[]{:S(2)}, u32[]{:S(2)}) async-start(bf16[64,32,256]{2,1,0:T(8,128)(2,1)} %bitcast.98), calls=%async_computation.3 | async-start | bytes 2097152 | tf_op jit(solution)/shard_map/all_to_all | solution.py:456
  457.7 20.6 %collective-permute-start.43 = (bf16[256,2048]{1,0:T(8,128)(2,1)}, bf16[256,2048]{1,0:T(8,128)(2,1)}, u32[]{:S(2)}, u32[]{:S(2)}) collective-permute-start(bf16[256,2048]{1,0:T(8,128)(2,1)} %get-tuple-element.54), channel_id=1, source_target_pairs={{0,2},{2,0},{1,3},{3,1},{4,6},{6,4},{5,7},{7,5},{8,10},{10,8},{9,1... | collective-permute-start | bytes 3145736 | tf_op jit(solution)/shard_map/ppermute | solution.py:419
  458.2 20.1 %collective-permute-start.45 = (bf16[256,2048]{1,0:T(8,128)(2,1)}, bf16[256,2048]{1,0:T(8,128)(2,1)}, u32[]{:S(2)}, u32[]{:S(2)}) collective-permute-start(bf16[256,2048]{1,0:T(8,128)(2,1)} %get-tuple-element.55), channel_id=1, source_target_pairs={{0,2},{2,0},{1,3},{3,1},{4,6},{6,4},{5,7},{7,5},{8,10},{10,8},{9,1... | collective-permute-start | bytes 3145736 | tf_op jit(solution)/shard_map/ppermute | solution.py:419
  463.8 36.3 %all-to-all-start.2 = ((bf16[64,32,384]{2,1,0:T(8,128)(2,1)}), bf16[64,32,384]{2,1,0:T(8,128)(2,1)}, u32[]{:S(2)}, u32[]{:S(2)}) async-start(bf16[64,32,384]{2,1,0:T(8,128)(2,1)} %bitcast.95), calls=%async_computation.2 | async-start | bytes 3145728 | tf_op jit(solution)/shard_map/all_to_all | solution.py:456
  484.5 29.8 %collective-permute-start.46 = (bf16[128,2048]{1,0:T(8,128)(2,1)}, bf16[128,2048]{1,0:T(8,128)(2,1)}, u32[]{:S(2)}, u32[]{:S(2)}) collective-permute-start(bf16[128,2048]{1,0:T(8,128)(2,1)} %get-tuple-element.71), channel_id=1, source_target_pairs={{0,5},{1,4},{4,1},{5,0},{2,7},{3,6},{6,3},{7,2},{8,13},{9,12},{12,... | collective-permute-start | bytes 1572872 | tf_op jit(solution)/shard_map/ppermute | solution.py:419
  487.7 30.3 %collective-permute-start.47 = (bf16[128,2048]{1,0:T(8,128)(2,1)}, bf16[128,2048]{1,0:T(8,128)(2,1)}, u32[]{:S(2)}, u32[]{:S(2)}) collective-permute-start(bf16[128,2048]{1,0:T(8,128)(2,1)} %get-tuple-element.72), channel_id=1, source_target_pairs={{0,4},{4,0},{1,5},{5,1},{2,6},{6,2},{3,7},{7,3},{8,12},{12,8},{9,1... | collective-permute-start | bytes 1572872 | tf_op jit(solution)/shard_map/ppermute | solution.py:419
  521.6 36.7 %collective-permute-start.48 = (f32[128,2048]{1,0:T(8,128)S(1)}, f32[128,2048]{1,0:T(8,128)S(1)}, u32[]{:S(2)}, u32[]{:S(2)}) collective-permute-start(f32[128,2048]{1,0:T(8,128)S(1)} %multiply_subtract_fusion), channel_id=1, source_target_pairs={{0,1},{1,0},{2,3},{3,2},{4,5},{5,4},{6,7},{7,6},{8,9},{9,8},{10,11... | collective-permute-start | bytes 3145736 | tf_op jit(solution)/shard_map/ppermute | solution.py:419
  523.4 26.2 %all-to-all-start.5 = ((f32[64,1,64]{2,1,0:T(1,128)}), f32[64,1,64]{2,1,0:T(1,128)S(1)}, u32[]{:S(2)}, u32[]{:S(2)}) async-start(f32[64,1,64]{2,1,0:T(1,128)} %copy.101), calls=%async_computation.6 | async-start | bytes 65536 | tf_op jit(solution)/shard_map/all_to_all | solution.py:573
  (50 other events, 785.6 us)
Sparse Core Ops, SparseCore 0:
  29.0 49.6 all-gather.2
  80.9 83.2 all-gather.4
  259.3 102.3 reduce-scatter.1

commit v2 on v1

v2 whole, which is shorter than its diff:
```python
import functools

import jax
import jax.numpy as jnp
from jax import lax
from jax.experimental import pallas as pl
from jax.experimental.pallas import tpu as pltpu
from jax.sharding import Mesh, PartitionSpec as P

HD = 64
HEADS = 4
FF_BLOCK = 704
FF_PAD = 768
OUT = 256
LOG2E = 1.4426950408889634
epsilon = 1e-05
rope_base = 10000.0
masked_low = -1e30
f32 = jnp.float32
bf16 = jnp.bfloat16

ALL = ("x", "z", "yh", "c")
MODEL = ("yh", "c")

NN = (((1,), (0,)), ((), ()))
NT = (((1,), (1,)), ((), ()))
TN = (((0,), (0,)), ((), ()))

VMEM = pl.BlockSpec(memory_space=pltpu.VMEM)
SMEM = pl.BlockSpec(memory_space=pltpu.SMEM)
BIG = pltpu.CompilerParams(vmem_limit_bytes=56 * 2**20)


def mm(a, b, dims):
    return lax.dot_general(a, b, dims, preferred_element_type=f32)


def turn(u, cosine, sine_signed):
    width = u.shape[-1]
    lane = lax.broadcasted_iota(jnp.int32, u.shape, 1)
    turned = jnp.where(
        lane % HD < HD // 2, pltpu.roll(u, width - HD // 2, 1), pltpu.roll(u, HD // 2, 1)
    )
    return u * cosine + turned * sine_signed


def qkv_kernel(x0, x1, x2, x3, w_ref, cos_ref, sin_ref, q_ref, kv_ref):
    scale = HD**-0.5 * LOG2E
    for part, x_ref in enumerate((x0, x1, x2, x3)):
        rows = slice(part * 256, part * 256 + 256)
        lin = mm(x_ref[...], w_ref[...], NN)
        cosine, sine = cos_ref[rows], sin_ref[rows]
        for half in range(2):
            cols = slice(half * 128, half * 128 + 128)
            q_ref[rows, cols] = (turn(lin[:, cols], cosine, sine) * scale).astype(bf16)
        kv = lin[:, 256:384]
        lane = lax.broadcasted_iota(jnp.int32, kv.shape, 1)
        kv_ref[rows, :] = jnp.where(lane < HD, turn(kv, cosine, sine), kv).astype(bf16)


def qkv_project(xs, w, cosine, sine):
    return pl.pallas_call(
        qkv_kernel,
        in_specs=[VMEM] * 7,
        out_specs=(VMEM, VMEM),
        out_shape=(
            jax.ShapeDtypeStruct((1024, 256), bf16),
            jax.ShapeDtypeStruct((1024, 128), bf16),
        ),
        cost_estimate=pl.CostEstimate(
            flops=2 * 1024 * 2048 * 384, bytes_accessed=6 * 2**20, transcendentals=0
        ),
        compiler_params=BIG,
        name="qkv_project",
    )(*xs, w, cosine, sine)


def attn_fwd_kernel(
    at_ref, q_ref, kv0, kv1, kv2, kv3, o_ref, ot_ref, lse_ref, q_pad, keys_all, values_t, *, bq, bk
):
    rows = q_ref.shape[0]
    depth, flip = at_ref[0], at_ref[1]
    for h in range(HEADS):
        q_pad[h, :, :HD] = q_ref[:, h * HD : (h + 1) * HD]
        q_pad[h, :, HD:] = jnp.zeros((rows, HD), bf16)
    for b, kv_ref in enumerate((kv0, kv1, kv2, kv3)):

        @pl.when(depth >= b)
        def _():
            keys_all[b] = kv_ref[...]
            values_t[b, :HD] = kv_ref[...].T[HD:]
            values_t[b, HD:] = jnp.ones((16, rows), bf16)

    pair = flip // bq

    def q_step(i, _):
        cols = pl.ds(pl.multiple_of(i * bq, bq), bq)
        queries = [q_pad[h, cols, :] for h in range(HEADS)]

        def block(b, offset, state, masked, count):
            keys = keys_all[b, pl.ds(offset, count), :]
            values = values_t[b, :, pl.ds(offset, count)]
            scores = [mm(keys, queries[h], NT) for h in range(HEADS)]
            if masked:
                k_pos = (lax.broadcasted_iota(jnp.int32, (count, bq), 0) + offset) ^ flip
                q_pos = (lax.broadcasted_iota(jnp.int32, (count, bq), 1) + i * bq) ^ flip
                visible = k_pos <= q_pos
                scores = [jnp.where(visible, s, masked_low) for s in scores]
            out = []
            for h in range(HEADS):
                top, acc = state[h]
                s = scores[h]
                new_top = jnp.maximum(top, jnp.max(s, axis=0, keepdims=True))
                p = jnp.exp2(s - new_top).astype(bf16)
                acc = acc * jnp.exp2(top - new_top) + mm(values, p, NN)
                out.append((new_top, acc))
            return tuple(out)

        state = tuple(
            (jnp.full((1, bq), masked_low, f32), jnp.zeros((HD + 16, bq), f32))
            for _ in range(HEADS)
        )
        state = block(0, pl.multiple_of(i * bq, bq), state, True, bq)
        state = lax.fori_loop(
            0,
            i ^ pair,
            lambda j, st: block(0, pl.multiple_of((j ^ pair) * bq, bq), st, False, bq),
            state,
        )
        per = rows // bk
        state = lax.fori_loop(
            0,
            depth * per,
            lambda j, st: block(
                1 + j // per, pl.multiple_of((j % per) * bk, bk), st, False, bk
            ),
            state,
        )
        outs = []
        for h in range(HEADS):
            top, acc = state[h]
            total = acc[HD : HD + 1]
            lse_ref[pl.ds(h, 1), cols] = top + jnp.log2(total)
            outs.append(acc[:HD] * (1.0 / total))
        o_t = jnp.concatenate(outs, 0)
        ot_ref[:, cols] = o_t
        o_ref[cols, :] = o_t.T.astype(bf16)
        return 0

    lax.fori_loop(0, rows // bq, q_step, 0)


def attn_fwd(at, q, kvs):
    rows = q.shape[0]
    return pl.pallas_call(
        functools.partial(attn_fwd_kernel, bq=512, bk=512),
        out_shape=(
            jax.ShapeDtypeStruct((rows, HEADS * HD), bf16),
            jax.ShapeDtypeStruct((HEADS * HD, rows), f32),
            jax.ShapeDtypeStruct((HEADS, rows), f32),
        ),
        in_specs=[SMEM] + [VMEM] * 5,
        out_specs=(VMEM,) * 3,
        scratch_shapes=[
            pltpu.VMEM((HEADS, rows, 128), bf16),
            pltpu.VMEM((4, rows, 128), bf16),
            pltpu.VMEM((4, HD + 16, rows), bf16),
        ],
        cost_estimate=pl.CostEstimate(
            flops=25 * 10**9, bytes_accessed=6 * 2**20, transcendentals=12 * 10**6
        ),
        compiler_params=BIG,
        name="attn_fwd",
    )(at, q, *kvs)


def branch_kernel(o_ref, w_ref, a0, a1, a2, a3):
    for k, out_ref in enumerate((a0, a1, a2, a3)):
        @pl.when(pl.program_id(0) == k)
        def _():
            out_ref[...] = mm(o_ref[...], w_ref[...], NT).astype(bf16)


def branch_project(o, w):
    depth = w.shape[0]
    part = jax.ShapeDtypeStruct((256, depth), bf16)
    return pl.pallas_call(
        branch_kernel,
        grid=(4,),
        in_specs=[pl.BlockSpec((256, OUT), lambda i: (i, 0)), VMEM],
        out_specs=(pl.BlockSpec((256, depth), lambda i: (0, 0)),) * 4,
        out_shape=(part,) * 4,
        cost_estimate=pl.CostEstimate(
            flops=2 * 1024 * depth * OUT, bytes_accessed=6 * 2**20, transcendentals=0
        ),
        compiler_params=BIG,
        name="branch_project",
    )(o, w)


def attn_bwd_kernel(
    at_ref, q_ref, kv0, kv1, kv2, kv3, do_ref, ot_ref, lse_ref,
    dq_ref, dkv0, dkv1, dkv2, dkv3,
    q_pad, do_pad, keys_all, keys_t, dkv_all, dqt, delta, *, bq, bk,
):
    rows = q_ref.shape[0]
    depth, flip = at_ref[0], at_ref[1]
    nothing = jnp.zeros((rows, HD), bf16)
    for h in range(HEADS):
        cols = slice(h * HD, (h + 1) * HD)
        q_pad[h, :, :HD] = q_ref[:, cols]
        q_pad[h, :, HD:] = nothing
        do_pad[h, :, :HD] = nothing
        do_pad[h, :, HD:] = do_ref[:, cols]
    do_t = do_ref[...].astype(f32).T
    for h in range(HEADS):
        cols = slice(h * HD, (h + 1) * HD)
        delta[pl.ds(h, 1), :] = jnp.sum(do_t[cols] * ot_ref[cols, :], axis=0, keepdims=True)
    for b, kv_ref in enumerate((kv0, kv1, kv2, kv3)):

        @pl.when(depth >= b)
        def _():
            keys_all[b] = kv_ref[...]
            keys_t[b] = kv_ref[...].T[:HD]

    dqt[...] = jnp.zeros_like(dqt)
    pair = flip // bq

    def tile(b, offset, i, masked, count, dkv):
        keys = keys_all[b, pl.ds(offset, count), :]
        turned = keys_t[b, :, pl.ds(offset, count)]
        at = pl.ds(pl.multiple_of(i * bq, bq), bq)
        if masked:
            k_pos = (lax.broadcasted_iota(jnp.int32, (count, bq), 0) + offset) ^ flip
            q_pos = (lax.broadcasted_iota(jnp.int32, (count, bq), 1) + i * bq) ^ flip
            visible = k_pos <= q_pos
        for h in range(HEADS):
            query, grad = q_pad[h, at, :], do_pad[h, at, :]
            p = jnp.exp2(mm(keys, query, NT) - lse_ref[pl.ds(h, 1), at])
            if masked:
                p = jnp.where(visible, p, 0.0)
            dp = mm(keys, grad, NT)
            ds = (p * (dp - delta[pl.ds(h, 1), at])).astype(bf16)
            dkv = dkv + mm(p.astype(bf16), grad, NN) + mm(ds, query, NN)
            dqt[h * HD : (h + 1) * HD, at] += mm(turned, ds, NN)
        return dkv

    lane = lax.broadcasted_iota(jnp.int32, (1, 128), 1)
    out_scale = jnp.where(lane < HD, 1.0 / LOG2E, 1.0)
    per = rows // bk

    def far(j, _):
        b, offset = 1 + j // per, pl.multiple_of((j % per) * bk, bk)
        dkv = lax.fori_loop(
            0,
            rows // bq,
            lambda i, st: tile(b, offset, i, False, bk, st),
            jnp.zeros((bk, 128), f32),
        )
        dkv_all[b, pl.ds(offset, bk), :] = (dkv * out_scale).astype(bf16)
        return 0

    lax.fori_loop(0, depth * per, far, 0)

    def near(j, _):
        offset = pl.multiple_of(j * bq, bq)
        dkv = tile(0, offset, j, True, bq, jnp.zeros((bq, 128), f32))
        dkv = lax.fori_loop(
            (j ^ pair) + 1,
            rows // bq,
            lambda i, st: tile(0, offset, i ^ pair, False, bq, st),
            dkv,
        )
        dkv_all[0, pl.ds(offset, bq), :] = (dkv * out_scale).astype(bf16)
        return 0

    lax.fori_loop(0, rows // bq, near, 0)
    dq_ref[...] = dqt[...].T * HD**-0.5
    for b, out_ref in enumerate((dkv0, dkv1, dkv2, dkv3)):
        out_ref[...] = dkv_all[b]


def attn_bwd(at, q, kvs, do, ot, lse):
    rows = q.shape[0]
    block = jax.ShapeDtypeStruct(kvs[0].shape, bf16)
    return pl.pallas_call(
        functools.partial(attn_bwd_kernel, bq=512, bk=512),
        out_shape=(jax.ShapeDtypeStruct((rows, HEADS * HD), f32), block, block, block, block),
        in_specs=[SMEM] + [VMEM] * 8,
        out_specs=(VMEM,) * 5,
        scratch_shapes=[
            pltpu.VMEM((HEADS, rows, 128), bf16),
            pltpu.VMEM((HEADS, rows, 128), bf16),
            pltpu.VMEM((4, rows, 128), bf16),
            pltpu.VMEM((4, HD, rows), bf16),
            pltpu.VMEM((4, rows, 128), bf16),
            pltpu.VMEM((HEADS * HD, rows), f32),
            pltpu.VMEM((HEADS, rows), f32),
        ],
        cost_estimate=pl.CostEstimate(
            flops=50 * 10**9, bytes_accessed=8 * 2**20, transcendentals=12 * 10**6
        ),
        compiler_params=BIG,
        name="attn_bwd",
    )(at, q, *kvs, do, ot, lse)


def ffn_kernel(*refs):
    hns, cots, w_hbm = refs[:8], refs[8:12], refs[12]
    hid_ref, dgu_ref = refs[13:15]
    ys, dns = refs[15:19], refs[19:23]
    hn_buf, cot_buf, y_buf, dn_buf, w_ref, w_sems, in_sems, out_sems = refs[23:]
    step = pl.program_id(0)
    slot = lax.rem(step, 2)
    parts = [slice(k * FF_PAD, (k + 1) * FF_PAD) for k in range(3)]
    weights = [
        pltpu.make_async_copy(w_hbm.at[:, parts[k]], w_ref.at[:, parts[k]], w_sems.at[k])
        for k in range(3)
    ]

    def fetch(k):
        b = k % 2
        return [
            pltpu.make_async_copy(hns[2 * k], hn_buf.at[b, :128], in_sems.at[b, 0]),
            pltpu.make_async_copy(hns[2 * k + 1], hn_buf.at[b, 128:], in_sems.at[b, 1]),
            pltpu.make_async_copy(cots[k], cot_buf.at[b], in_sems.at[b, 2]),
        ]

    def flush(k):
        b = k % 2
        return [
            pltpu.make_async_copy(y_buf.at[b], ys[k], out_sems.at[b, 0]),
            pltpu.make_async_copy(dn_buf.at[b], dns[k], out_sems.at[b, 1]),
        ]

    def start(copies):
        for copy in copies:
            copy.start()

    def wait(copies):
        for copy in copies:
            copy.wait()

    def arrived(k):
        @pl.when(step == 0)
        def _():
            weights[k].wait()

    for k in range(4):

        @pl.when(step == k)
        def _():
            if k == 0:
                start(fetch(0))
                start(weights)
            if k < 3:
                start(fetch(k + 1))
            wait(fetch(k))

    hn, cot = hn_buf[slot], cot_buf[slot]
    arrived(0)
    gate = mm(hn, w_ref[:, parts[0]], NN)
    arrived(1)
    up = mm(hn, w_ref[:, parts[1]], NN)
    arrived(2)
    dhid = mm(cot, w_ref[:, parts[2]], NN)
    sg = 1.0 / (1.0 + jnp.exp(-gate))
    act = gate * sg
    hid = (act * up).astype(bf16)
    dgate = (dhid * up * sg * (1.0 + gate * (1.0 - sg))).astype(bf16)
    dup = (dhid * act).astype(bf16)
    hid_ref[...] = hid
    dgu_ref[:, parts[0]] = dgate
    dgu_ref[:, parts[1]] = dup
    for k in (2, 3):

        @pl.when(step == k)
        def _():
            wait(flush(k - 2))

    dn_buf[slot] = (mm(dgate, w_ref[:, parts[0]], NT) + mm(dup, w_ref[:, parts[1]], NT)).astype(
        bf16
    )
    y_buf[slot] = mm(hid, w_ref[:, parts[2]], NT).astype(bf16)
    for k in range(4):

        @pl.when(step == k)
        def _():
            start(flush(k))
            if k == 3:
                wait(flush(2))
                wait(flush(3))


def ffn(hns, cots, w):
    depth = w.shape[0]
    rowwise = lambda width: pl.BlockSpec((256, width), lambda i: (i, 0))
    hbm = pl.BlockSpec(memory_space=pl.ANY)
    quarter = jax.ShapeDtypeStruct((256, depth), bf16)
    outs = pl.pallas_call(
        ffn_kernel,
        grid=(4,),
        in_specs=[hbm] * 13,
        out_specs=(rowwise(FF_PAD), rowwise(2 * FF_PAD)) + (hbm,) * 8,
        out_shape=(
            jax.ShapeDtypeStruct((1024, FF_PAD), bf16),
            jax.ShapeDtypeStruct((1024, 2 * FF_PAD), bf16),
        )
        + (quarter,) * 8,
        scratch_shapes=[pltpu.VMEM((2, 256, depth), bf16)] * 4
        + [
            pltpu.VMEM((depth, 3 * FF_PAD), bf16),
            pltpu.SemaphoreType.DMA((3,)),
            pltpu.SemaphoreType.DMA((2, 3)),
            pltpu.SemaphoreType.DMA((2, 2)),
        ],
        cost_estimate=pl.CostEstimate(
            flops=12 * 1024 * depth * FF_PAD,
            bytes_accessed=35 * 2**20,
            transcendentals=1024 * FF_PAD,
        ),
        compiler_params=BIG,
        name="ffn",
    )(*hns, *cots, w)
    return outs[0], outs[1], outs[2:6], outs[6:10]


def ffn_grad_kernel(*refs):
    hn = jnp.concatenate([r[...] for r in refs[:8]], 0)
    cot = jnp.concatenate([r[...] for r in refs[8:12]], 0)
    dgu_ref, hid_ref, out_ref = refs[12:]
    out_ref[:, : 2 * FF_PAD] = mm(hn, dgu_ref[...], TN).astype(bf16)
    out_ref[:, 2 * FF_PAD :] = mm(cot, hid_ref[...], TN).astype(bf16)


def ffn_grad(hns, cots, dgu, hid):
    depth = hns[0].shape[1]
    block = 256
    return pl.pallas_call(
        ffn_grad_kernel,
        grid=(depth // block,),
        in_specs=[pl.BlockSpec((128, block), lambda i: (0, i))] * 8
        + [pl.BlockSpec((256, block), lambda i: (0, i))] * 4
        + [VMEM] * 2,
        out_specs=pl.BlockSpec((block, 3 * FF_PAD), lambda i: (i, 0)),
        out_shape=jax.ShapeDtypeStruct((depth, 3 * FF_PAD + OUT), bf16),
        cost_estimate=pl.CostEstimate(
            flops=6 * 1024 * depth * FF_PAD, bytes_accessed=24 * 2**20, transcendentals=0
        ),
        compiler_params=BIG,
        name="ffn_grad",
    )(*hns, *cots, dgu, hid)


def dh_kernel(*refs):
    pieces, w_ref, ob_ref, _ = refs[:8], refs[8], refs[9], refs[10]
    do_ref, grads_hbm, part, sem = refs[11:]
    for k in range(4):
        cols = slice(k * 512, k * 512 + 512)
        dh = jnp.concatenate([r[:, cols] for r in pieces], 0)
        part[cols, :] = mm(dh, ob_ref[...], TN).astype(bf16)
    copy = pltpu.make_async_copy(part, grads_hbm.at[:, 3 * FF_PAD :], sem)
    copy.start()
    for k in range(4):
        dh = jnp.concatenate([pieces[2 * k][...], pieces[2 * k + 1][...]], 0)
        do_ref[k * 256 : k * 256 + 256, :] = mm(dh, w_ref[...], NN).astype(bf16)
    copy.wait()


def dh_project(pieces, w, ob, grads):
    depth = w.shape[0]
    hbm = pl.BlockSpec(memory_space=pl.ANY)
    return pl.pallas_call(
        dh_kernel,
        in_specs=[VMEM] * 10 + [hbm],
        out_specs=(VMEM, hbm),
        out_shape=(
            jax.ShapeDtypeStruct((1024, OUT), bf16),
            jax.ShapeDtypeStruct(grads.shape, bf16),
        ),
        scratch_shapes=[pltpu.VMEM((depth, OUT), bf16), pltpu.SemaphoreType.DMA(())],
        input_output_aliases={10: 1},
        cost_estimate=pl.CostEstimate(
            flops=4 * 1024 * depth * OUT, bytes_accessed=8 * 2**20, transcendentals=0
        ),
        compiler_params=BIG,
        name="dh_project",
    )(*pieces, w, ob, grads)


def qkv_grad_kernel(x0, x1, x2, x3, near_ref, far_ref, out_ref):
    xh = jnp.concatenate([r[...] for r in (x0, x1, x2, x3)], 0)
    out_ref[...] = mm(xh, jnp.concatenate([near_ref[...], far_ref[...]], 0), TN).astype(bf16)


def qkv_grad(xs, dqkvs):
    depth = xs[0].shape[1]
    block = 512
    return pl.pallas_call(
        qkv_grad_kernel,
        grid=(depth // block,),
        in_specs=[pl.BlockSpec((256, block), lambda i: (0, i))] * 4 + [VMEM] * 2,
        out_specs=pl.BlockSpec((block, 384), lambda i: (i, 0)),
        out_shape=jax.ShapeDtypeStruct((depth, 384), bf16),
        cost_estimate=pl.CostEstimate(
            flops=2 * 1024 * depth * 384, bytes_accessed=8 * 2**20, transcendentals=0
        ),
        compiler_params=BIG,
        name="qkv_grad",
    )(*xs, *dqkvs)


def dqkv_kernel(at_ref, dq_ref, *refs):
    parts, (w_ref, cos_ref, sin_ref, dqkv_ref, keep_ref, send_ref) = refs[:8], refs[8:]
    cosine, sine = cos_ref[...], -sin_ref[...]
    core = at_ref[2]
    for part in range(2):
        cols = slice(part * 128, part * 128 + 128)
        dqkv_ref[:, cols] = turn(dq_ref[:, cols], cosine, sine).astype(bf16)
    dkv = sum(part[...].astype(f32) for part in parts)
    lane = lax.broadcasted_iota(jnp.int32, dkv.shape, 1)
    is_key = lane < HD
    turned = jnp.where(is_key, turn(dkv, cosine, sine), dkv)
    mine = jnp.where(is_key, 1 - core, core) > 0
    dqkv_ref[:, 256:] = jnp.where(mine, turned, 0.0).astype(bf16)
    dn = mm(dqkv_ref[...], w_ref[...], NT).astype(bf16)

    @pl.when(pl.program_id(0) == 0)
    def _():
        send_ref[...] = dn

    @pl.when(pl.program_id(0) == 1)
    def _():
        keep_ref[...] = dn


def dqkv_project(half, at, dq, dkvs, others, w, cosine, sine):
    depth = w.shape[0]
    turned = pl.BlockSpec((256, 128), lambda i: (2 * half + i, 0))
    rowwise = lambda width: pl.BlockSpec((256, width), lambda i: (2 * half + 1 - i, 0))
    whole = pl.BlockSpec((256, depth), lambda i: (0, 0))
    return pl.pallas_call(
        dqkv_kernel,
        grid=(2,),
        in_specs=[SMEM, rowwise(256)]
        + [rowwise(128)] * 4
        + [turned] * 4
        + [VMEM, rowwise(128), rowwise(128)],
        out_specs=(pl.BlockSpec((256, 384), lambda i: (1 - i, 0)), whole, whole),
        out_shape=(
            jax.ShapeDtypeStruct((512, 384), bf16),
            jax.ShapeDtypeStruct((256, depth), bf16),
            jax.ShapeDtypeStruct((256, depth), bf16),
        ),
        cost_estimate=pl.CostEstimate(
            flops=2 * 512 * depth * 384, bytes_accessed=6 * 2**20, transcendentals=0
        ),
        compiler_params=BIG,
        name="dqkv_project",
    )(at, dq, *dkvs, *others, w, cosine, sine)


def swap(value, axes):
    count = 2 ** len(axes)
    return lax.ppermute(value, axes, [(i, count - 1 - i) for i in range(count)])


def shifted(value, steps):
    first, last = max(0, -steps), min(4, 4 - steps)
    return lax.ppermute(value, "z", [(i, i + steps) for i in range(first, last)])


def gather_group(own):
    by_l, by_c = swap(own, ("yl",)), swap(own, ("c",))
    by_d, by_h = swap(own, ("yh", "yl")), swap(own, ("yh",))
    near = [own, by_l, by_c, swap(by_l, ("c",))]
    return near + [by_h, by_d, swap(by_h, ("c",)), swap(by_d, ("c",))]


def sum_cores(keep, send):
    return keep.astype(f32) + swap(send, ("c",)).astype(f32)


def from_chips(near, far):
    far = far.astype(bf16)
    by_h = swap(far[:128], ("yh",))
    by_d = swap(far[128:], ("yh", "yl"))
    by_l = swap(near[128:].astype(bf16), ("yl",))
    return by_l, by_d, by_h


def sum_chips(near, received):
    by_l, by_d, by_h = received
    return near[:128] + by_l.astype(f32) + by_d.astype(f32) + by_h.astype(f32)


def pick(parts, index):
    return lax.dynamic_index_in_dim(parts, index, 0, False)


def trade_cores(parts, core):
    parts = parts.reshape(2, 2, *parts.shape[1:]).swapaxes(0, 1)
    mine, got = pick(parts, core), swap(pick(parts, 1 - core), ("c",))
    return jnp.where(core == 0, jnp.stack([mine, got], 1), jnp.stack([got, mine], 1))


def trade_chips(parts, yh):
    mine, got = pick(parts, yh), swap(pick(parts, 1 - yh), ("yh",))
    parts = jnp.where(yh == 0, jnp.stack([mine, got]), jnp.stack([got, mine]))
    return parts.reshape(4, *parts.shape[2:])


def both_halves(own, other, yl):
    return jnp.where(yl == 0, jnp.concatenate([own, other], 0), jnp.concatenate([other, own], 0))


def on_device(
    tokens, w_query, w_key, w_value, w_output, w_gate, w_up, w_down, norm_attn, norm_ffn, cotangent
):
    together = lax.optimization_barrier
    z, yh = lax.axis_index("z"), lax.axis_index("yh")
    core, yl = lax.axis_index("c"), lax.axis_index("yl")
    gain_one = norm_attn.astype(f32)[:, None]
    gain_two = norm_ffn.astype(f32)[:, None]
    flip = (yh * 4 + core * 2 + yl) * 128
    at = jnp.stack([z, flip, core]).astype(jnp.int32)

    both = lambda a: jnp.where(yl == 0, a, jnp.concatenate([a[128:], a[:128]], 0))
    inputs = both(tokens[0]).astype(f32)
    inverse_one = lax.rsqrt(jnp.mean(inputs * inputs, axis=-1, keepdims=True) + epsilon)
    xh = (inputs * inverse_one).astype(bf16)
    inputs, inverse_one = inputs[:128], inverse_one[:128]
    cot_here = both(cotangent[0])

    def by_model(w):
        return w.reshape(32, 4, -1).transpose(1, 0, 2)

    def by_head(w):
        return jnp.repeat(w.reshape(32, 2, HD).transpose(1, 0, 2), 2, axis=0)

    scaled = lambda w, gain: (w.astype(f32) * gain).astype(bf16)

    def padded(w):
        return jnp.pad(by_model(w), ((0, 0), (0, 0), (0, FF_PAD - FF_BLOCK)))

    qkv_rows = jnp.concatenate(
        [
            by_model(scaled(w_query, gain_one)),
            by_head(scaled(w_key, gain_one)),
            by_head(scaled(w_value, gain_one)),
        ],
        -1,
    )
    ffn_rows = jnp.concatenate(
        [padded(scaled(w_gate, gain_two)), padded(scaled(w_up, gain_two)), padded(w_down.T)], -1
    )

    def spread(rows):
        copies = jnp.broadcast_to(rows[None], (16,) + rows.shape).reshape(64, 32, -1)
        return lax.all_to_all(copies, ALL, 0, 0).reshape(2048, -1)

    w_qkv = spread(qkv_rows)
    positions = (z * 1024 + (jnp.arange(1024, dtype=jnp.int32) ^ flip)).astype(f32)
    freqs = rope_base ** (-2.0 * jnp.arange(HD // 2, dtype=f32) / HD)
    angles = positions[:, None] * freqs[None, :]
    cosine, sine = jnp.cos(angles), jnp.sin(angles)
    cosine = jnp.concatenate([cosine] * 4, -1)
    sine = jnp.concatenate([-sine, sine, -sine, sine], -1)

    xh_c, xh_h = swap(xh, ("c",)), swap(xh, ("yh",))
    ffn_rows = trade_chips(trade_cores(ffn_rows, core), yh).reshape(128, -1)
    out_rows = by_model(w_output.T)
    xh_h, w_qkv, cosine, sine, cot_here, ffn_rows, out_rows = together(
        (xh_h, w_qkv, cosine, sine, cot_here, ffn_rows, out_rows)
    )
    xhs = [xh, xh_c, xh_h, swap(xh_h, ("c",))]

    q, kv = qkv_project(xhs, w_qkv, cosine, sine)
    cot_c, cot_h = swap(cot_here, ("c",)), swap(cot_here, ("yh",))
    kvs = [kv] + [shifted(kv, by) for by in (1, 2, 3)]
    kvs, cot_h, ffn_rows, out_rows = together((kvs, cot_h, ffn_rows, out_rows))
    w_ffn = lax.all_gather(ffn_rows, ("x", "z"), axis=0, tiled=True)
    w_out = spread(out_rows)
    cots = [cot_here, cot_c, cot_h, swap(cot_h, ("c",))]
    ob, o_t, lse = attn_fwd(at, q, kvs)
    branch = branch_project(ob, w_out)
    near, far = sum_cores(*branch[:2]), sum_cores(*branch[2:])
    middle = inputs + sum_chips(near, from_chips(near, far))
    inverse_two = lax.rsqrt(jnp.mean(middle * middle, axis=-1, keepdims=True) + epsilon)
    hns = gather_group((middle * inverse_two).astype(bf16))

    hid, dgu, ys, dns = ffn(hns, cots, w_ffn)
    near, far = sum_cores(*dns[:2]), sum_cores(*dns[2:])
    received = from_chips(near, far)
    grads = ffn_grad(hns, cots, dgu, hid)
    received, grads = together((received, grads))
    dn2 = sum_chips(near, received)
    dh = (
        cots[0][:128].astype(f32)
        + inverse_two * dn2
        - middle * inverse_two**3 * jnp.mean(dn2 * middle, axis=-1, keepdims=True)
    )
    dh_low, ys = together((dh.astype(bf16), ys))
    dhs = gather_group(dh_low)
    y_near, y_far = sum_cores(*ys[:2]), sum_cores(*ys[2:])
    dhs, y_near, y_far = together((dhs, y_near, y_far))

    do, grads = dh_project(dhs, w_out, ob, grads)
    grads = lax.psum_scatter(grads, ("x", "z"), scatter_dimension=0, tiled=True)
    do, y_near, y_far = together((do, y_near, y_far))
    received = from_chips(y_near, y_far)
    dq, *dkvs = attn_bwd(at, q, kvs, do, o_t, lse)
    received, dkvs = together((received, dkvs))
    block_out = (middle + sum_chips(y_near, received)).astype(bf16)
    block_out, dkvs = together((block_out, dkvs))
    block_other = swap(block_out, ("yl",))
    dkvs = dkvs[:1] + [shifted(dkvs[by], -by) for by in (1, 2, 3)]
    dkvs, block_other = together((dkvs, block_other))
    block_out = both_halves(block_out, block_other, yl)
    others = [swap(part, ("c",)) for part in dkvs]
    dqkv_far, dn_far, dn_far_c = dqkv_project(1, at, dq, dkvs, others, w_qkv, cosine, sine)
    dqkv_near, dn_near, dn_near_c = dqkv_project(0, at, dq, dkvs, others, w_qkv, cosine, sine)
    near, far = sum_cores(dn_near, dn_near_c), sum_cores(dn_far, dn_far_c)
    near, far, dqkv_near, dqkv_far = together((near, far, dqkv_near, dqkv_far))
    received = from_chips(near, far)
    dn1 = sum_chips(near, received)
    grad_qkv = qkv_grad(xhs, (dqkv_near, dqkv_far))
    grad_qkv = lax.all_to_all(grad_qkv.reshape(16, 128, 384), ("x", "z"), 0, 0)
    grads = trade_cores(grads.reshape(4, 32, 3 * FF_PAD + OUT), core)
    input_grad = (
        dh
        + inverse_one * dn1
        - inputs * inverse_one**3 * jnp.mean(dn1 * inputs, axis=-1, keepdims=True)
    )
    input_grad, grad_qkv, grads = together((input_grad, grad_qkv, grads))
    other = swap(input_grad.astype(bf16), ("yl",)).astype(f32)
    input_grad = both_halves(input_grad, other, yl)
    grads = trade_chips(grads, yh).astype(f32)
    grad_qkv = jnp.sum(grad_qkv.astype(f32), 0).astype(bf16).reshape(4, 32, 384)
    grad_qkv = trade_chips(trade_cores(grad_qkv, core), yh).astype(f32)

    def joined(parts):
        return parts.transpose(1, 0, 2).reshape(32, -1)

    ffn_part = lambda k: joined(grads[:, :, k * FF_PAD : k * FF_PAD + FF_BLOCK])
    grad_gate, grad_up, grad_down = ffn_part(0), ffn_part(1), ffn_part(2).T
    grad_query = joined(grad_qkv[:, :, :256])
    by_core = grad_qkv[:, :, 256:].reshape(2, 2, 32, 2 * HD).sum(1)
    grad_key, grad_value = joined(by_core[:, :, :HD]), joined(by_core[:, :, HD:])

    def gain_grad(*pairs):
        return sum(jnp.sum(w.astype(f32) * grad, 1) for w, grad in pairs)

    gains = jnp.stack(
        [
            gain_grad((w_query, grad_query), (w_key, grad_key), (w_value, grad_value)),
            gain_grad((w_gate, grad_gate), (w_up, grad_up)),
        ]
    )
    gains = gains + swap(gains, ("yl",))
    return (
        block_out[None],
        input_grad[None],
        grad_query * gain_one,
        grad_key * gain_one,
        grad_value * gain_one,
        joined(grads[:, :, 3 * FF_PAD :]).T,
        grad_gate * gain_two,
        grad_up * gain_two,
        grad_down,
        gains[0],
        gains[1],
    )


def solution(mesh):
    mesh = Mesh(mesh.devices.reshape(4, 4, 2, 2, 2), ("x", "z", "yh", "c", "yl"))
    ctx = ("z", "yh", "c")
    rows, cols = P(ALL, "yl"), P("yl", ALL)
    seq = P("x", ctx, None)
    vec = P(ALL)
    in_specs = (seq, rows, rows, rows, cols, rows, rows, cols, vec, vec, seq)
    out_specs = (seq, seq, rows, rows, rows, cols, rows, rows, cols, vec, vec)
    return jax.shard_map(
        on_device, mesh=mesh, in_specs=in_specs, out_specs=out_specs, check_vma=False
    )
```

time: 587 us -> 498 us (0.85)
  waiting for transfers between devices: 245 us -> 185 us
  starting transfers between devices: 131 us -> 96.2 us
  Pallas kernels: 80.2 us -> 106 us
  blocking collectives: 16.5 us -> 0 us
  matrix products: 12.9 us -> 0 us
    ppermute x6, waiting for transfers between devices: 77.3 us -> 32.6 us  [shifted(): lax.ppermute(value, 'z', [(i, i + steps) for i in range(first, last)])]
    pallas_call x3 -> x7, Pallas kernels: 41 us -> 67.1 us  [the longest x1 32 us: ffn(): pl.pallas_call(ffn_kernel, grid=(4,), in_specs=[hbm] * 13, out_specs=(row...]
    all_to_all x5 -> x3, starting transfers between devices: 47.6 us -> 26.5 us  [the longest x2 18.8 us: spread(): return lax.all_to_all(copies, ALL, 0, 0).reshape(2048, -1)]
    all_to_all x1 -> x0, blocking collectives: 16.5 us -> none  [on_device(): lax.all_to_all(other_rows, MODEL, 0, 0).reshape(128, 256 + 3 * FF_PAD)]
    ppermute x44 -> x53, starting transfers between devices: 70.1 us -> 56.1 us  [swap(): return lax.ppermute(value, axes, [(i, count - 1 - i) for i in range(count)])]
    dot_general x4 -> x0, matrix products: 12.9 us -> none  [mm(): return lax.dot_general(a, b, dims, preferred_element_type=f32)]
    all_to_all x5 -> x3, waiting for transfers between devices: 36.2 us -> 24.7 us  [the longest x2 20.7 us: spread(): return lax.all_to_all(copies, ALL, 0, 0).reshape(2048, -1)]
    select_n x0 -> x9, other arithmetic: none -> 7.48 us  [the longest x2 2.78 us: both_halves(): jnp.where(yl == 0, jnp.concatenate([own, other], 0), jnp.concatenate([oth...]
  transfers between devices with their start and end apart: 58 -> 64, of which waited for: 25 -> 28; matrix products, arithmetic and copies ran while one was open for 13% -> 13% of each run, Pallas kernels for 9% -> 14%
where the time goes in v2:
time: 498 us; the launch traced here: 488 us
  waiting for transfers between devices  185 us (37%)
  Pallas kernels  106 us (21%)
  starting transfers between devices  96.2 us (19%)
  other arithmetic  49.2 us (10%)
  local copies, waits for them, and re-layouts  36.4 us (7%)
  between operations  15.6 us (3%)
    ppermute x53, waiting for transfers between devices, swap(): return lax.ppermute(value, axes, [(i, count - 1 - i) for i in range(count)])  127 us
    ppermute x53, starting transfers between devices, swap(): return lax.ppermute(value, axes, [(i, count - 1 - i) for i in range(count)])  56.1 us
    ppermute x6, waiting for transfers between devices, shifted(): lax.ppermute(value, 'z', [(i, i + steps) for i in range(first, last)])  32.6 us
    pallas_call x1, Pallas kernels, ffn(): pl.pallas_call(ffn_kernel, grid=(4,), in_specs=[hbm] * 13, out_specs=(row...  32 us
    all_to_all x2, waiting for transfers between devices, spread(): return lax.all_to_all(copies, ALL, 0, 0).reshape(2048, -1)  20.7 us
    all_to_all x2, starting transfers between devices, spread(): return lax.all_to_all(copies, ALL, 0, 0).reshape(2048, -1)  18.8 us
    pallas_call x1, Pallas kernels, ffn_grad(): pl.pallas_call(ffn_grad_kernel, grid=(depth // block,), in_specs=[pl.Bloc...  16.4 us
    pallas_call x1, Pallas kernels, attn_bwd(): pl.pallas_call(functools.partial(attn_bwd_kernel, bq=512, bk=512), out_sh...  14.7 us
  transfers between devices with their start and end apart: 64, of which 28 were waited for; matrix products, arithmetic and copies ran while one was open for 13% of the time, Pallas kernels for 14%

profile of v2, /device:TPU:1, one launch (start us, length us, event | category | flops | bytes accessed | tf_op | source)
XLA Modules:
  0.0 488.2 jit_solution(9190761365930265569)
XLA Ops:
  11.4 3.8 collective-permute-start.1
  30.9 9.0 %all-to-all-start = ((bf16[64,32,384]{2,1,0:T(8,128)(2,1)}), bf16[64,32,384]{2,1,0:T(8,128)(2,1)}, u32[]{:S(2)}, u32[]{:S(2)}) async-start(bf16[64,32,384]{2,1,0:T(8,128)(2,1)} %bitcast.106), calls=%async_computation | async-start | bytes 3145728 | tf_op jit(solution)/shard_map/all_to_all | solution.py:660
  57.5 9.0 %collective-permute-done.3 = bf16[2,32,2304]{2,1,0:T(8,128)(2,1)} collective-permute-done((bf16[2,32,2304]{2,1,0:T(8,128)(2,1)}, bf16[2,32,2304]{2,1,0:T(8,128)(2,1)}, u32[]{:S(2)}, u32[]{:S(2)}) %collective-permute-start.3) | collective-permute-done | bytes 294944 | tf_op jit(solution)/shard_map/ppermute | solution.py:565
  72.8 6.3 %qkv_project.1 = (bf16[1024,256]{1,0:T(8,128)(2,1)}, bf16[1024,128]{1,0:T(8,128)(2,1)}) custom-call(bf16[256,2048]{1,0:T(8,128)(2,1)} %copy-done.1, bf16[256,2048]{1,0:T(8,128)(2,1)} %collective-permute-done.x1, bf16[256,2048]{1,0:T(8,128)(2,1)} %collective-permute-done.1.x2, bf16[256,2048]{1,0:T(8,128)(2,1)} %copy-done.7, ...), custom_call_target="tpu_custom_call" | custom-call | flops 1610612736 | bytes 6291456 | tf_op jit(solution)/shard_map/qkv_project/pallas_call | solution.py:62
  79.1 4.3 collective-permute-start.7
  88.6 7.3 %collective-permute-done.8.refs_10_ = bf16[256,2048]{1,0:T(8,128)(2,1)} collective-permute-done((bf16[256,2048]{1,0:T(8,128)(2,1)}, bf16[256,2048]{1,0:T(8,128)(2,1)}, u32[]{:S(2)}, u32[]{:S(2)}) %collective-permute-start.8) | collective-permute-done | bytes 1048608 | tf_op jit(solution)/shard_map/ppermute | solution.py:565
  97.7 9.8 %all-to-all-start.1 = ((bf16[64,32,256]{2,1,0:T(8,128)(2,1)}), bf16[64,32,256]{2,1,0:T(8,128)(2,1)S(1)}, u32[]{:S(2)}, u32[]{:S(2)}) async-start(bf16[64,32,256]{2,1,0:T(8,128)(2,1)} %bitcast.110), calls=%async_computation.1 | async-start | bytes 2097152 | tf_op jit(solution)/shard_map/all_to_all | solution.py:660
  107.8 8.0 %attn_fwd.1 = (bf16[1024,256]{1,0:T(8,128)(2,1)}, f32[256,1024]{1,0:T(8,128)}, f32[4,1024]{1,0:T(4,128)}) custom-call(s32[3]{0:T(128)} %pad_add_fusion.at_ref, bf16[1024,256]{1,0:T(8,128)(2,1)} %get-tuple-element.107.q_ref, bf16[1024,128]{1,0:T(8,128)(2,1)} %get-tuple-element.112.kv0, bf16[1024,128]{1,0:T(8,128)(2,1)} %collective-permute-done.5.kv1, ...), custom_call_target="tpu_custom_call" | custom-call | flops 24999999488 | bytes 6291456 | tf_op jit(solution)/shard_map/attn_fwd/pallas_call | solution.py:155
  115.8 20.7 %all-to-all-done.1 = bf16[64,32,256]{2,1,0:T(8,128)(2,1)S(1)} async-done(((bf16[64,32,256]{2,1,0:T(8,128)(2,1)}), bf16[64,32,256]{2,1,0:T(8,128)(2,1)S(1)}, u32[]{:S(2)}, u32[]{:S(2)}) %all-to-all-start.1) | async-done | bytes 1048608 | tf_op jit(solution)/shard_map/all_to_all | solution.py:660
  137.5 5.7 %branch_project.1 = (bf16[256,2048]{1,0:T(8,128)(2,1)}, bf16[256,2048]{1,0:T(8,128)(2,1)}, bf16[256,2048]{1,0:T(8,128)(2,1)}, bf16[256,2048]{1,0:T(8,128)(2,1)}) custom-call(bf16[1024,256]{1,0:T(8,128)(2,1)} %get-tuple-element.116.o_ref.refs_9_, bf16[2048,256]{1,0:T(8,128)(2,1)} %bitcast.108), custom_call_target="tpu_custom_call" | custom-call | flops 1073741824 | bytes 6291456 | tf_op jit(solution)/shard_map/branch_project/pallas_call | solution.py:187
  152.7 8.6 %collective-permute-done.10 = bf16[128,2048]{1,0:T(8,128)(2,1)S(1)} collective-permute-done((bf16[128,2048]{1,0:T(8,128)(2,1)S(1)}, bf16[128,2048]{1,0:T(8,128)(2,1)S(1)}, u32[]{:S(2)}, u32[]{:S(2)}) %collective-permute-start.10) | collective-permute-done | bytes 524320 | tf_op jit(solution)/shard_map/ppermute | solution.py:565
  161.4 13.6 %collective-permute-done.12 = bf16[128,2048]{1,0:T(8,128)(2,1)S(1)} collective-permute-done((bf16[128,2048]{1,0:T(8,128)(2,1)S(1)}, bf16[128,2048]{1,0:T(8,128)(2,1)S(1)}, u32[]{:S(2)}, u32[]{:S(2)}) %collective-permute-start.12) | collective-permute-done | bytes 524320 | tf_op jit(solution)/shard_map/ppermute | solution.py:565
  181.0 19.3 %collective-permute-done.18.refs_5_ = bf16[128,2048]{1,0:T(8,128)(2,1)S(1)} collective-permute-done((bf16[128,2048]{1,0:T(8,128)(2,1)S(1)}, bf16[128,2048]{1,0:T(8,128)(2,1)S(1)}, u32[]{:S(2)}, u32[]{:S(2)}) %collective-permute-start.18) | collective-permute-done | bytes 524320 | tf_op jit(solution)/shard_map/ppermute | solution.py:565
  207.5 32.0 %ffn.1 = (bf16[1024,768]{1,0:T(8,128)(2,1)}, bf16[1024,1536]{1,0:T(8,128)(2,1)}, bf16[256,2048]{1,0:T(8,128)(2,1)}, bf16[256,2048]{1,0:T(8,128)(2,1)}, bf16[256,...) custom-call(bf16[128,2048]{1,0:T(8,128)(2,1)} %copy-done.39, ...), custom_call_target="tpu_custom_call" | custom-call | flops 19327352832 | bytes 36700160 | tf_op jit(solution)/shard_map/ffn/pallas_call | solution.py:400
  250.3 16.4 %ffn_grad.1.refs_10_ = bf16[2048,2560]{1,0:T(8,128)(2,1)} custom-call(bf16[128,2048]{1,0:T(8,128)(2,1)} %copy-done.39, bf16[128,2048]{1,0:T(8,128)(2,1)} %copy-done.57, bf16[128,2048]{1,0:T(8,128)(2,1)} %copy-done.58, bf16[128,2048]{1,0:T(8,128)(2,1)} %collective-permute-done.16.refs_3_, bf16[128,2048]{1,0:T(8,128)(2,1)} %copy-done.56, ...), custom_call_target="tpu_custom_call" | custom-call | flops 9663676416 | bytes 25165824 | tf_op jit(solution)/shard_map/ffn_grad/pallas_call | solution.py:439
  269.6 3.5 collective-permute-done.26
  282.3 21.7 %collective-permute-done.32.refs_5_ = bf16[128,2048]{1,0:T(8,128)(2,1)S(1)} collective-permute-done((bf16[128,2048]{1,0:T(8,128)(2,1)S(1)}, bf16[128,2048]{1,0:T(8,128)(2,1)S(1)}, u32[]{:S(2)}, u32[]{:S(2)}) %collective-permute-start.32) | collective-permute-done | bytes 524320 | tf_op jit(solution)/shard_map/ppermute | solution.py:565
  310.2 5.9 %dh_project.1 = (bf16[1024,256]{1,0:T(8,128)(2,1)}, bf16[2048,2560]{1,0:T(8,128)(2,1)}) custom-call(bf16[128,2048]{1,0:T(8,128)(2,1)} %copy-done.10, bf16[128,2048]{1,0:T(8,128)(2,1)} %copy-done.35, bf16[128,2048]{1,0:T(8,128)(2,1)} %copy-done.36, bf16[128,2048]{1,0:T(8,128)(2,1)} %collective-permute-done.30.refs_3_, ...), custom_call_target="tpu_custom_call", output_to_operand_aliasing={{1}: (10, {})} | custom-call | flops 2147483648 | bytes 8388608 | tf_op jit(solution)/shard_map/dh_project/pallas_call | solution.py:473
  322.7 14.7 %attn_bwd.1 = (f32[1024,256]{1,0:T(8,128)}, bf16[1024,128]{1,0:T(8,128)(2,1)}, bf16[1024,128]{1,0:T(8,128)(2,1)}, bf16[1024,128]{1,0:T(8,128)(2,1)}, bf16[1024,128]{1,0:T(8,128)(2,1)}) custom-call(s32[3]{0:T(128)} %pad_add_fusion.at_ref, bf16[1024,256]{1,0:T(8,128)(2,1)} %get-tuple-element.107.q_ref, bf16[1024,128]{1,0:T(8,128)(2,1)} %get-tuple-element.112.kv0, ...), custom_call_target="tpu_custom_call" | custom-call | flops 49999998976 | bytes 8388608 | tf_op jit(solution)/shard_map/attn_bwd/pallas_call | solution.py:286
  337.4 6.8 %collective-permute-done.39 = bf16[128,2048]{1,0:T(8,128)(2,1)S(1)} collective-permute-done((bf16[128,2048]{1,0:T(8,128)(2,1)S(1)}, bf16[128,2048]{1,0:T(8,128)(2,1)S(1)}, u32[]{:S(2)}, u32[]{:S(2)}) %collective-permute-start.39) | collective-permute-done | bytes 524320 | tf_op jit(solution)/shard_map/ppermute | solution.py:565
  353.3 11.0 %collective-permute-done.40.refs_1_ = bf16[1024,128]{1,0:T(8,128)(2,1)S(1)} collective-permute-done((bf16[1024,128]{1,0:T(8,128)(2,1)S(1)}, bf16[1024,128]{1,0:T(8,128)(2,1)S(1)}, u32[]{:S(2)}, u32[]{:S(2)}) %collective-permute-start.40) | collective-permute-done | bytes 262176 | tf_op jit(solution)/shard_map/ppermute | solution.py:570
  364.3 13.4 %collective-permute-done.41.refs_2_ = bf16[1024,128]{1,0:T(8,128)(2,1)S(1)} collective-permute-done((bf16[1024,128]{1,0:T(8,128)(2,1)S(1)}, bf16[1024,128]{1,0:T(8,128)(2,1)S(1)}, u32[]{:S(2)}, u32[]{:S(2)}) %collective-permute-start.41) | collective-permute-done | bytes 262176 | tf_op jit(solution)/shard_map/ppermute | solution.py:570
  377.8 8.0 %collective-permute-done.42.refs_3_ = bf16[1024,128]{1,0:T(8,128)(2,1)S(1)} collective-permute-done((bf16[1024,128]{1,0:T(8,128)(2,1)S(1)}, bf16[1024,128]{1,0:T(8,128)(2,1)S(1)}, u32[]{:S(2)}, u32[]{:S(2)}) %collective-permute-start.42) | collective-permute-done | bytes 262176 | tf_op jit(solution)/shard_map/ppermute | solution.py:570
  390.8 5.8 %dqkv_project.3 = (bf16[512,384]{1,0:T(8,128)(2,1)}, bf16[256,2048]{1,0:T(8,128)(2,1)}, bf16[256,2048]{1,0:T(8,128)(2,1)}) custom-call(s32[3]{0:T(128)} %pad_add_fusion.at_ref, f32[1024,256]{1,0:T(8,128)} %get-tuple-element.176.dq_ref, bf16[1024,128]{1,0:T(8,128)(2,1)} %get-tuple-element.177.refs_0_, bf16[1024,128]{1,0:T(8,128)(2,1)} %copy-done.21, ...), custom_call_target="tpu_custom_call" | custom-call | flops 805306368 | bytes 6291456 | tf_op jit(solution)/shard_map/dqkv_project/pallas_call | solution.py:542
  397.1 5.4 %dqkv_project.2 = (bf16[512,384]{1,0:T(8,128)(2,1)}, bf16[256,2048]{1,0:T(8,128)(2,1)}, bf16[256,2048]{1,0:T(8,128)(2,1)}) custom-call(s32[3]{0:T(128)} %pad_add_fusion.at_ref, f32[1024,256]{1,0:T(8,128)} %get-tuple-element.176.dq_ref, bf16[1024,128]{1,0:T(8,128)(2,1)} %get-tuple-element.177.refs_0_, bf16[1024,128]{1,0:T(8,128)(2,1)} %copy-done.21, ...), custom_call_target="tpu_custom_call" | custom-call | flops 805306368 | bytes 6291456 | tf_op jit(solution)/shard_map/dqkv_project/pallas_call | solution.py:542
  412.9 6.0 %qkv_grad.1 = bf16[2048,384]{1,0:T(8,128)(2,1)} custom-call(bf16[256,2048]{1,0:T(8,128)(2,1)} %copy-done.1, bf16[256,2048]{1,0:T(8,128)(2,1)} %collective-permute-done.x1, bf16[256,2048]{1,0:T(8,128)(2,1)} %collective-permute-done.1.x2, bf16[256,2048]{1,0:T(8,128)(2,1)} %copy-done.7, bf16[512,384]{1,0:T(8,128)(2,1)} %get-tuple-element.189.near_ref, ...), custom_call_target="tpu_custom_call" | custom-call | flops 1610612736 | bytes 8388608 | tf_op jit(solution)/shard_map/qkv_grad/pallas_call | solution.py:499
  418.9 7.7 %all-to-all-start.2 = ((bf16[16,128,384]{2,1,0:T(8,128)(2,1)}), bf16[16,128,384]{2,1,0:T(8,128)(2,1)}, u32[]{:S(2)}, u32[]{:S(2)}) async-start(bf16[16,128,384]{2,1,0:T(8,128)(2,1)} %bitcast.107), calls=%async_computation.2 | async-start | bytes 3145728 | tf_op jit(solution)/shard_map/all_to_all | solution.py:728
  426.6 9.6 %collective-permute-done.51 = bf16[128,2048]{1,0:T(8,128)(2,1)S(1)} collective-permute-done((bf16[128,2048]{1,0:T(8,128)(2,1)}, bf16[128,2048]{1,0:T(8,128)(2,1)S(1)}, u32[]{:S(2)}, u32[]{:S(2)}) %collective-permute-start.51) | collective-permute-done | bytes 524320 | tf_op jit(solution)/shard_map/ppermute | solution.py:565
  443.2 3.9 all-to-all-done.2
  448.8 4.3 collective-permute-start.55
  461.8 5.2 %collective-permute-done.57 = bf16[2,32,2560]{2,1,0:T(8,128)(2,1)S(1)} collective-permute-done((bf16[2,32,2560]{2,1,0:T(8,128)(2,1)S(1)}, bf16[2,32,2560]{2,1,0:T(8,128)(2,1)S(1)}, u32[]{:S(2)}, u32[]{:S(2)}) %collective-permute-start.57) | collective-permute-done | bytes 327712 | tf_op jit(solution)/shard_map/ppermute | solution.py:565
  473.7 4.0 collective-permute-done.58
  (350 shorter events, 161.8 us)
Async XLA Ops:
  11.4 57.0 %collective-permute-start.1 = (bf16[256,2048]{1,0:T(8,128)(2,1)S(1)}, bf16[256,2048]{1,0:T(8,128)(2,1)}, u32[]{:S(2)}, u32[]{:S(2)}) collective-permute-start(bf16[256,2048]{1,0:T(8,128)(2,1)S(1)} %multiply_convert_fusion.x0), channel_id=1, source_target_pairs={{0,4},{4,0},{1,5},{5,1},{2,6},{6,2},{3,7},{7,3},{8,12},{12,8},{9,1... | collective-permute-start | bytes 3145736 | tf_op jit(solution)/shard_map/ppermute | solution.py:565
  15.2 54.2 %collective-permute-start = (bf16[256,2048]{1,0:T(8,128)(2,1)S(1)}, bf16[256,2048]{1,0:T(8,128)(2,1)}, u32[]{:S(2)}, u32[]{:S(2)}) collective-permute-start(bf16[256,2048]{1,0:T(8,128)(2,1)S(1)} %multiply_convert_fusion.x0), channel_id=1, source_target_pairs={{0,2},{2,0},{1,3},{3,1},{4,6},{6,4},{5,7},{7,5},{8,10},{10,8},{9,1... | collective-permute-start | bytes 3145736 | tf_op jit(solution)/shard_map/ppermute | solution.py:565
  30.9 37.6 %all-to-all-start = ((bf16[64,32,384]{2,1,0:T(8,128)(2,1)}), bf16[64,32,384]{2,1,0:T(8,128)(2,1)}, u32[]{:S(2)}, u32[]{:S(2)}) async-start(bf16[64,32,384]{2,1,0:T(8,128)(2,1)} %bitcast.106), calls=%async_computation | async-start | bytes 3145728 | tf_op jit(solution)/shard_map/all_to_all | solution.py:660
  39.9 167.6 %all-gather.2.cloned.1.call-start = ((), (), s32[]{:S(2)}) async-start(), calls=%async_computation.4 | async-start | bytes 10027008 | tf_op jit(solution)/shard_map/all_gather | solution.py:682
  44.8 21.7 %collective-permute-start.3 = (bf16[2,32,2304]{2,1,0:T(8,128)(2,1)}, bf16[2,32,2304]{2,1,0:T(8,128)(2,1)}, u32[]{:S(2)}, u32[]{:S(2)}) collective-permute-start(bf16[2,32,2304]{2,1,0:T(8,128)(2,1)} %get-tuple-element.221), channel_id=1, source_target_pairs={{0,4},{4,0},{1,5},{5,1},{2,6},{6,2},{3,7},{7,3},{8,12},{12,8},{9,1... | collective-permute-start | bytes 884744 | tf_op jit(solution)/shard_map/ppermute | solution.py:565
  69.3 26.5 %collective-permute-start.8 = (bf16[256,2048]{1,0:T(8,128)(2,1)}, bf16[256,2048]{1,0:T(8,128)(2,1)}, u32[]{:S(2)}, u32[]{:S(2)}) collective-permute-start(bf16[256,2048]{1,0:T(8,128)(2,1)} %maximum_select_fusion.2.refs_8_), channel_id=1, source_target_pairs={{0,4},{4,0},{1,5},{5,1},{2,6},{6,2},{3,7},{7,3},{8,12},{12,8},{9,1... | collective-permute-start | bytes 3145736 | tf_op jit(solution)/shard_map/ppermute | solution.py:565
  97.7 38.7 %all-to-all-start.1 = ((bf16[64,32,256]{2,1,0:T(8,128)(2,1)}), bf16[64,32,256]{2,1,0:T(8,128)(2,1)S(1)}, u32[]{:S(2)}, u32[]{:S(2)}) async-start(bf16[64,32,256]{2,1,0:T(8,128)(2,1)} %bitcast.110), calls=%async_computation.1 | async-start | bytes 2097152 | tf_op jit(solution)/shard_map/all_to_all | solution.py:660
  107.5 330.7 %reduce-scatter.2.cloned.1.call-start = ((), (), s32[]{:S(2)}) async-start(), calls=%async_computation.5 | async-start | bytes 11141120 | tf_op jit(solution)/shard_map/reduce_scatter | solution.py:709
  149.2 25.7 %collective-permute-start.12 = (bf16[128,2048]{1,0:T(8,128)(2,1)S(1)}, bf16[128,2048]{1,0:T(8,128)(2,1)S(1)}, u32[]{:S(2)}, u32[]{:S(2)}) collective-permute-start(bf16[128,2048]{1,0:T(8,128)(2,1)S(1)} %get-tuple-element.210), channel_id=1, source_target_pairs={{0,5},{1,4},{4,1},{5,0},{2,7},{3,6},{6,3},{7,2},{8,13},{9,12},{12,... | collective-permute-start | bytes 1572872 | tf_op jit(solution)/shard_map/ppermute | solution.py:565
  149.3 25.6 %collective-permute-start.13 = (bf16[128,2048]{1,0:T(8,128)(2,1)S(1)}, bf16[128,2048]{1,0:T(8,128)(2,1)S(1)}, u32[]{:S(2)}, u32[]{:S(2)}) collective-permute-start(bf16[128,2048]{1,0:T(8,128)(2,1)S(1)} %get-tuple-element.211), channel_id=1, source_target_pairs={{0,4},{4,0},{1,5},{5,1},{2,6},{6,2},{3,7},{7,3},{8,12},{12,8},{9,1... | collective-permute-start | bytes 1572872 | tf_op jit(solution)/shard_map/ppermute | solution.py:565
  151.7 28.6 %collective-permute-start.21 = (bf16[256,2048]{1,0:T(8,128)(2,1)S(1)}, bf16[256,2048]{1,0:T(8,128)(2,1)S(1)}, u32[]{:S(2)}, u32[]{:S(2)}) collective-permute-start(bf16[256,2048]{1,0:T(8,128)(2,1)S(1)} %copy-done.8), channel_id=1, source_target_pairs={{0,2},{2,0},{1,3},{3,1},{4,6},{6,4},{5,7},{7,5},{8,10},{10,8},{9,1... | collective-permute-start | bytes 3145736 | tf_op jit(solution)/shard_map/ppermute | solution.py:565
  175.6 24.8 %collective-permute-start.18 = (bf16[128,2048]{1,0:T(8,128)(2,1)S(1)}, bf16[128,2048]{1,0:T(8,128)(2,1)S(1)}, u32[]{:S(2)}, u32[]{:S(2)}) collective-permute-start(bf16[128,2048]{1,0:T(8,128)(2,1)S(1)} %multiply_convert_fusion.1.refs_0_), channel_id=1, source_target_pairs={{0,5},{1,4},{4,1},{5,0},{2,7},{3,6},{6,3},{7,2},{8,13},{9,12},{12,... | collective-permute-start | bytes 1572872 | tf_op jit(solution)/shard_map/ppermute | solution.py:565
  175.7 29.2 %collective-permute-start.22 = (bf16[256,2048]{1,0:T(8,128)(2,1)}, bf16[256,2048]{1,0:T(8,128)(2,1)S(1)}, u32[]{:S(2)}, u32[]{:S(2)}) collective-permute-start(bf16[256,2048]{1,0:T(8,128)(2,1)} %collective-permute-done.8.refs_10_), channel_id=1, source_target_pairs={{0,2},{2,0},{1,3},{3,1},{4,6},{6,4},{5,7},{7,5},{8,10},{10,8},{9,1... | collective-permute-start | bytes 3145736 | tf_op jit(solution)/shard_map/ppermute | solution.py:565
  177.1 25.3 %collective-permute-start.17 = (bf16[128,2048]{1,0:T(8,128)(2,1)S(1)}, bf16[128,2048]{1,0:T(8,128)(2,1)S(1)}, u32[]{:S(2)}, u32[]{:S(2)}) collective-permute-start(bf16[128,2048]{1,0:T(8,128)(2,1)S(1)} %multiply_convert_fusion.1.refs_0_), channel_id=1, source_target_pairs={{0,4},{4,0},{1,5},{5,1},{2,6},{6,2},{3,7},{7,3},{8,12},{12,8},{9,1... | collective-permute-start | bytes 1572872 | tf_op jit(solution)/shard_map/ppermute | solution.py:565
  178.3 25.4 %collective-permute-start.14 = (bf16[128,2048]{1,0:T(8,128)(2,1)S(1)}, bf16[128,2048]{1,0:T(8,128)(2,1)S(1)}, u32[]{:S(2)}, u32[]{:S(2)}) collective-permute-start(bf16[128,2048]{1,0:T(8,128)(2,1)S(1)} %multiply_convert_fusion.1.refs_0_), channel_id=1, source_target_pairs={{0,1},{1,0},{2,3},{3,2},{4,5},{5,4},{6,7},{7,6},{8,9},{9,8},{10,11... | collective-permute-start | bytes 1572872 | tf_op jit(solution)/shard_map/ppermute | solution.py:565
  180.4 24.5 %collective-permute-start.15 = (bf16[128,2048]{1,0:T(8,128)(2,1)S(1)}, bf16[128,2048]{1,0:T(8,128)(2,1)S(1)}, u32[]{:S(2)}, u32[]{:S(2)}) collective-permute-start(bf16[128,2048]{1,0:T(8,128)(2,1)S(1)} %multiply_convert_fusion.1.refs_0_), channel_id=1, source_target_pairs={{0,2},{2,0},{1,3},{3,1},{4,6},{6,4},{5,7},{7,5},{8,10},{10,8},{9,1... | collective-permute-start | bytes 1572872 | tf_op jit(solution)/shard_map/ppermute | solution.py:565
  245.0 21.8 %collective-permute-start.24 = (bf16[128,2048]{1,0:T(8,128)(2,1)}, bf16[128,2048]{1,0:T(8,128)(2,1)S(1)}, u32[]{:S(2)}, u32[]{:S(2)}) collective-permute-start(bf16[128,2048]{1,0:T(8,128)(2,1)} %slice.222), channel_id=1, source_target_pairs={{0,1},{1,0},{2,3},{3,2},{4,5},{5,4},{6,7},{7,6},{8,9},{9,8},{10,11... | collective-permute-start | bytes 1572872 | tf_op jit(solution)/shard_map/ppermute | solution.py:565
  246.5 23.1 %collective-permute-start.27 = (bf16[128,2048]{1,0:T(8,128)(2,1)}, bf16[128,2048]{1,0:T(8,128)(2,1)S(1)}, u32[]{:S(2)}, u32[]{:S(2)}) collective-permute-start(bf16[128,2048]{1,0:T(8,128)(2,1)} %get-tuple-element.208), channel_id=1, source_target_pairs={{0,4},{4,0},{1,5},{5,1},{2,6},{6,2},{3,7},{7,3},{8,12},{12,8},{9,1... | collective-permute-start | bytes 1572872 | tf_op jit(solution)/shard_map/ppermute | solution.py:565
  247.6 25.4 %collective-permute-start.26 = (bf16[128,2048]{1,0:T(8,128)(2,1)}, bf16[128,2048]{1,0:T(8,128)(2,1)S(1)}, u32[]{:S(2)}, u32[]{:S(2)}) collective-permute-start(bf16[128,2048]{1,0:T(8,128)(2,1)} %get-tuple-element.209), channel_id=1, source_target_pairs={{0,5},{1,4},{4,1},{5,0},{2,7},{3,6},{6,3},{7,2},{8,13},{9,12},{12,... | collective-permute-start | bytes 1572872 | tf_op jit(solution)/shard_map/ppermute | solution.py:565
  276.5 29.0 %collective-permute-start.35 = (bf16[256,2048]{1,0:T(8,128)(2,1)S(1)}, bf16[256,2048]{1,0:T(8,128)(2,1)S(1)}, u32[]{:S(2)}, u32[]{:S(2)}) collective-permute-start(bf16[256,2048]{1,0:T(8,128)(2,1)S(1)} %copy-done.53), channel_id=1, source_target_pairs={{0,2},{2,0},{1,3},{3,1},{4,6},{6,4},{5,7},{7,5},{8,10},{10,8},{9,1... | collective-permute-start | bytes 3145736 | tf_op jit(solution)/shard_map/ppermute | solution.py:565
  278.1 25.9 %collective-permute-start.32 = (bf16[128,2048]{1,0:T(8,128)(2,1)S(1)}, bf16[128,2048]{1,0:T(8,128)(2,1)S(1)}, u32[]{:S(2)}, u32[]{:S(2)}) collective-permute-start(bf16[128,2048]{1,0:T(8,128)(2,1)S(1)} %get-tuple-element.142.refs_0_), channel_id=1, source_target_pairs={{0,5},{1,4},{4,1},{5,0},{2,7},{3,6},{6,3},{7,2},{8,13},{9,12},{12,... | collective-permute-start | bytes 1572872 | tf_op jit(solution)/shard_map/ppermute | solution.py:565
  280.8 24.1 %collective-permute-start.31 = (bf16[128,2048]{1,0:T(8,128)(2,1)S(1)}, bf16[128,2048]{1,0:T(8,128)(2,1)S(1)}, u32[]{:S(2)}, u32[]{:S(2)}) collective-permute-start(bf16[128,2048]{1,0:T(8,128)(2,1)S(1)} %get-tuple-element.142.refs_0_), channel_id=1, source_target_pairs={{0,4},{4,0},{1,5},{5,1},{2,6},{6,2},{3,7},{7,3},{8,12},{12,8},{9,1... | collective-permute-start | bytes 1572872 | tf_op jit(solution)/shard_map/ppermute | solution.py:565
  280.8 24.2 %collective-permute-start.28 = (bf16[128,2048]{1,0:T(8,128)(2,1)S(1)}, bf16[128,2048]{1,0:T(8,128)(2,1)S(1)}, u32[]{:S(2)}, u32[]{:S(2)}) collective-permute-start(bf16[128,2048]{1,0:T(8,128)(2,1)S(1)} %get-tuple-element.142.refs_0_), channel_id=1, source_target_pairs={{0,1},{1,0},{2,3},{3,2},{4,5},{5,4},{6,7},{7,6},{8,9},{9,8},{10,11... | collective-permute-start | bytes 1572872 | tf_op jit(solution)/shard_map/ppermute | solution.py:565
  281.4 26.1 %collective-permute-start.36 = (bf16[256,2048]{1,0:T(8,128)(2,1)S(1)}, bf16[256,2048]{1,0:T(8,128)(2,1)S(1)}, u32[]{:S(2)}, u32[]{:S(2)}) collective-permute-start(bf16[256,2048]{1,0:T(8,128)(2,1)S(1)} %copy-done.52), channel_id=1, source_target_pairs={{0,2},{2,0},{1,3},{3,1},{4,6},{6,4},{5,7},{7,5},{8,10},{10,8},{9,1... | collective-permute-start | bytes 3145736 | tf_op jit(solution)/shard_map/ppermute | solution.py:565
  319.7 24.6 %collective-permute-start.39 = (bf16[128,2048]{1,0:T(8,128)(2,1)S(1)}, bf16[128,2048]{1,0:T(8,128)(2,1)S(1)}, u32[]{:S(2)}, u32[]{:S(2)}) collective-permute-start(bf16[128,2048]{1,0:T(8,128)(2,1)S(1)} %get-tuple-element.206), channel_id=1, source_target_pairs={{0,4},{4,0},{1,5},{5,1},{2,6},{6,2},{3,7},{7,3},{8,12},{12,8},{9,1... | collective-permute-start | bytes 1572872 | tf_op jit(solution)/shard_map/ppermute | solution.py:565
  322.7 25.0 %collective-permute-start.38 = (bf16[128,2048]{1,0:T(8,128)(2,1)S(1)}, bf16[128,2048]{1,0:T(8,128)(2,1)}, u32[]{:S(2)}, u32[]{:S(2)}) collective-permute-start(bf16[128,2048]{1,0:T(8,128)(2,1)S(1)} %get-tuple-element.207), channel_id=1, source_target_pairs={{0,5},{1,4},{4,1},{5,0},{2,7},{3,6},{6,3},{7,2},{8,13},{9,12},{12,... | collective-permute-start | bytes 1572872 | tf_op jit(solution)/shard_map/ppermute | solution.py:565
  349.3 36.5 %collective-permute-start.43 = (bf16[128,2048]{1,0:T(8,128)(2,1)S(1)}, bf16[128,2048]{1,0:T(8,128)(2,1)S(1)}, u32[]{:S(2)}, u32[]{:S(2)}) collective-permute-start(bf16[128,2048]{1,0:T(8,128)(2,1)S(1)} %add_convert_fusion.2), channel_id=1, source_target_pairs={{0,1},{1,0},{2,3},{3,2},{4,5},{5,4},{6,7},{7,6},{8,9},{9,8},{10,11... | collective-permute-start | bytes 1572872 | tf_op jit(solution)/shard_map/ppermute | solution.py:565
  350.7 27.0 %collective-permute-start.41 = (bf16[1024,128]{1,0:T(8,128)(2,1)S(1)}, bf16[1024,128]{1,0:T(8,128)(2,1)S(1)}, u32[]{:S(2)}, u32[]{:S(2)}) collective-permute-start(bf16[1024,128]{1,0:T(8,128)(2,1)S(1)} %copy-done.63), channel_id=1, source_target_pairs={{16,0},{24,8},{17,1},{25,9},{18,2},{26,10},{19,3},{27,11},{20,4},{... | collective-permute-start | bytes 786440 | tf_op jit(solution)/shard_map/ppermute | solution.py:570
  352.0 33.7 %collective-permute-start.42 = (bf16[1024,128]{1,0:T(8,128)(2,1)S(1)}, bf16[1024,128]{1,0:T(8,128)(2,1)S(1)}, u32[]{:S(2)}, u32[]{:S(2)}) collective-permute-start(bf16[1024,128]{1,0:T(8,128)(2,1)S(1)} %copy-done.62), channel_id=1, source_target_pairs={{24,0},{25,1},{26,2},{27,3},{28,4},{29,5},{30,6},{31,7},{56,32},{5... | collective-permute-start | bytes 786440 | tf_op jit(solution)/shard_map/ppermute | solution.py:570
  410.5 25.8 %collective-permute-start.51 = (bf16[128,2048]{1,0:T(8,128)(2,1)}, bf16[128,2048]{1,0:T(8,128)(2,1)S(1)}, u32[]{:S(2)}, u32[]{:S(2)}) collective-permute-start(bf16[128,2048]{1,0:T(8,128)(2,1)} %get-tuple-element.204), channel_id=1, source_target_pairs={{0,5},{1,4},{4,1},{5,0},{2,7},{3,6},{6,3},{7,2},{8,13},{9,12},{12,... | collective-permute-start | bytes 1572872 | tf_op jit(solution)/shard_map/ppermute | solution.py:565
  412.3 24.0 %collective-permute-start.52 = (bf16[128,2048]{1,0:T(8,128)(2,1)}, bf16[128,2048]{1,0:T(8,128)(2,1)}, u32[]{:S(2)}, u32[]{:S(2)}) collective-permute-start(bf16[128,2048]{1,0:T(8,128)(2,1)} %get-tuple-element.205), channel_id=1, source_target_pairs={{0,4},{4,0},{1,5},{5,1},{2,6},{6,2},{3,7},{7,3},{8,12},{12,8},{9,1... | collective-permute-start | bytes 1572872 | tf_op jit(solution)/shard_map/ppermute | solution.py:565
  418.9 28.3 %all-to-all-start.2 = ((bf16[16,128,384]{2,1,0:T(8,128)(2,1)}), bf16[16,128,384]{2,1,0:T(8,128)(2,1)}, u32[]{:S(2)}, u32[]{:S(2)}) async-start(bf16[16,128,384]{2,1,0:T(8,128)(2,1)} %bitcast.107), calls=%async_computation.2 | async-start | bytes 3145728 | tf_op jit(solution)/shard_map/all_to_all | solution.py:728
  (101 other events, 752.6 us)
Sparse Core Ops, SparseCore 0:
  96.2 86.6 all-gather.1
  316.2 91.7 reduce-scatter.1

commit v3 on v2

--- a/solution.py
+++ b/solution.py
@@ -44,9 +44,145 @@
     return u * cosine + turned * sine_signed
 
 
-def qkv_kernel(x0, x1, x2, x3, w_ref, cos_ref, sin_ref, q_ref, kv_ref):
+def order_kernel(at_ref, x_ref, cot_ref, xh_ref, inv_ref, cot_out):
+    for half in range(2):
+        first = pl.multiple_of((at_ref[3] ^ half) * 128, 128)
+        rows = slice(half * 128, half * 128 + 128)
+        x = x_ref[pl.ds(first, 128), :].astype(f32)
+        inverse = lax.rsqrt(jnp.mean(x * x, axis=-1, keepdims=True) + epsilon)
+        xh_ref[rows, :] = (x * inverse).astype(bf16)
+        cot_out[rows, :] = cot_ref[pl.ds(first, 128), :]
+        if half == 0:
+            inv_ref[...] = inverse
+
+
+def order(at, x, cot):
+    low = jax.ShapeDtypeStruct(x.shape, bf16)
+    return pl.pallas_call(
+        order_kernel,
+        in_specs=[SMEM, VMEM, VMEM],
+        out_specs=(VMEM,) * 3,
+        out_shape=(low, jax.ShapeDtypeStruct((128, 1), f32), low),
+        cost_estimate=pl.CostEstimate(flops=2**20, bytes_accessed=4 * 2**20, transcendentals=0),
+        compiler_params=BIG,
+        name="order",
+    )(at, x, cot)
+
+
+def prepare_kernel(wq, wk, wv, wo_t, wg, wu, wd_t, g_one, g_two, qkv_ref, rest_ref, out_ref):
+    g_one, g_two = g_one[...], g_two[...]
+    scaled = lambda ref, gain: (ref[...].astype(f32) * gain).astype(bf16)
+    query, key, value = scaled(wq, g_one), scaled(wk, g_one), scaled(wv, g_one)
+    for part in range(4):
+        head = slice(part // 2 * HD, part // 2 * HD + HD)
+        rows = jnp.concatenate(
+            [query[:, part * 256 : part * 256 + 256], key[:, head], value[:, head]], 1
+        )
+        for copy in range(16):
+            qkv_ref[copy * 4 + part] = rows
+    lane = lax.broadcasted_iota(jnp.int32, (32, FF_PAD), 1)
+    for k, (ref, gain) in enumerate(((wg, g_two), (wu, g_two), (wd_t, None))):
+        w = ref[...].astype(f32)
+        w = w if gain is None else w * gain
+        for part in range(4):
+            shift = (w.shape[1] - part * FF_BLOCK) % w.shape[1]
+            block = pltpu.roll(w, shift, 1)[:, :FF_PAD] if shift else w[:, :FF_PAD]
+            block = jnp.where(lane < FF_BLOCK, block, 0.0)
+            rest_ref[part, :, k * FF_PAD : (k + 1) * FF_PAD] = block.astype(bf16)
+    for part in range(4):
+        out_ref[part] = wo_t[:, part * OUT : part * OUT + OUT]
+
+
+def prepare(*args):
+    return pl.pallas_call(
+        prepare_kernel,
+        in_specs=[VMEM] * 9,
+        out_specs=(VMEM,) * 3,
+        out_shape=(
+            jax.ShapeDtypeStruct((64, 32, 384), bf16),
+            jax.ShapeDtypeStruct((4, 32, 3 * FF_PAD), bf16),
+            jax.ShapeDtypeStruct((4, 32, OUT), bf16),
+        ),
+        cost_estimate=pl.CostEstimate(flops=2**20, bytes_accessed=3 * 2**20, transcendentals=0),
+        compiler_params=BIG,
+        name="prepare",
+    )(*args)
+
+
+def finish_ffn_kernel(parts, wg, wu, g_two, gate_ref, up_ref, down_ref, out_ref, gain_ref):
+    def joined(first):
+        total = jnp.zeros(gate_ref.shape, f32)
+        for part in range(4):
+            block = parts[part, :, first : first + FF_PAD].astype(f32)
+            block = jnp.concatenate(
+                [block, jnp.zeros((32, total.shape[1] - FF_PAD), f32)], 1
+            )
+            total = total + (pltpu.roll(block, part * FF_BLOCK, 1) if part else block)
+        return total
+
+    gate, up = joined(0), joined(FF_PAD)
+    gain_ref[...] = jnp.sum(
+        wg[...].astype(f32) * gate + wu[...].astype(f32) * up, axis=1, keepdims=True
+    )
+    gate_ref[...] = gate * g_two[...]
+    up_ref[...] = up * g_two[...]
+    down_ref[...] = joined(2 * FF_PAD)
+    for part in range(4):
+        out_ref[:, part * OUT : part * OUT + OUT] = parts[part, :, 3 * FF_PAD :].astype(f32)
+
+
+def finish_ffn(parts, wg, wu, g_two):
+    wide = jax.ShapeDtypeStruct(wg.shape, f32)
+    return pl.pallas_call(
+        finish_ffn_kernel,
+        in_specs=[VMEM] * 4,
+        out_specs=(VMEM,) * 5,
+        out_shape=(
+            wide,
+            wide,
+            wide,
+            jax.ShapeDtypeStruct((32, 4 * OUT), f32),
+            jax.ShapeDtypeStruct((32, 1), f32),
+        ),
+        cost_estimate=pl.CostEstimate(flops=2**20, bytes_accessed=3 * 2**20, transcendentals=0),
+        compiler_params=BIG,
+        name="finish_ffn",
+    )(parts, wg, wu, g_two)
+
+
+def finish_qkv_kernel(parts, wq, wk, wv, g_one, q_ref, k_ref, v_ref, gain_ref):
+    grads = [parts[part].astype(f32) for part in range(4)]
+    query = jnp.concatenate([grad[:, :256] for grad in grads], 1)
+    both = [grads[0] + grads[1], grads[2] + grads[3]]
+    key = jnp.concatenate([grad[:, 256:320] for grad in both], 1)
+    value = jnp.concatenate([grad[:, 320:] for grad in both], 1)
+    total = jnp.sum(wq[...].astype(f32) * query, axis=1, keepdims=True)
+    total = total + jnp.sum(
+        wk[...].astype(f32) * key + wv[...].astype(f32) * value, axis=1, keepdims=True
+    )
+    gain_ref[...] = total
+    q_ref[...] = query * g_one[...]
+    k_ref[...] = key * g_one[...]
+    v_ref[...] = value * g_one[...]
+
+
+def finish_qkv(parts, wq, wk, wv, g_one):
+    shapes = [w.shape for w in (wq, wk, wv)] + [(32, 1)]
+    return pl.pallas_call(
+        finish_qkv_kernel,
+        in_specs=[VMEM] * 5,
+        out_specs=(VMEM,) * 4,
+        out_shape=tuple(jax.ShapeDtypeStruct(shape, f32) for shape in shapes),
+        cost_estimate=pl.CostEstimate(flops=2**18, bytes_accessed=2**19, transcendentals=0),
+        compiler_params=BIG,
+        name="finish_qkv",
+    )(parts, wq, wk, wv, g_one)
+
+
+def qkv_kernel(*refs):
+    w_ref, cos_ref, sin_ref, q_ref, kv_ref = refs[4:]
     scale = HD**-0.5 * LOG2E
-    for part, x_ref in enumerate((x0, x1, x2, x3)):
+    for part, x_ref in enumerate(refs[:4]):
         rows = slice(part * 256, part * 256 + 256)
         lin = mm(x_ref[...], w_ref[...], NN)
         cosine, sine = cos_ref[rows], sin_ref[rows]
@@ -174,28 +310,37 @@
     )(at, q, *kvs)
 
 
-def branch_kernel(o_ref, w_ref, a0, a1, a2, a3):
+def branch_kernel(at_ref, o_ref, w0, w1, w2, w3, a0, a1, a2, a3, w_ref):
+    @pl.when(pl.program_id(0) == 0)
+    def _():
+        for i, piece in enumerate((w0, w1, w2, w3)):
+            for j in range(4):
+                first = ((at_ref[4] ^ j) * 4 + (at_ref[0] ^ i)) * 128
+                w_ref[pl.ds(pl.multiple_of(first, 128), 128), :] = piece[j * 128 : j * 128 + 128]
+
     for k, out_ref in enumerate((a0, a1, a2, a3)):
+
         @pl.when(pl.program_id(0) == k)
         def _():
             out_ref[...] = mm(o_ref[...], w_ref[...], NT).astype(bf16)
 
 
-def branch_project(o, w):
-    depth = w.shape[0]
+def branch_project(at, o, ws):
+    depth = 4 * ws[0].shape[0]
     part = jax.ShapeDtypeStruct((256, depth), bf16)
-    return pl.pallas_call(
+    outs = pl.pallas_call(
         branch_kernel,
         grid=(4,),
-        in_specs=[pl.BlockSpec((256, OUT), lambda i: (i, 0)), VMEM],
-        out_specs=(pl.BlockSpec((256, depth), lambda i: (0, 0)),) * 4,
-        out_shape=(part,) * 4,
+        in_specs=[SMEM, pl.BlockSpec((256, OUT), lambda i: (i, 0))] + [VMEM] * 4,
+        out_specs=(pl.BlockSpec((256, depth), lambda i: (0, 0)),) * 4 + (VMEM,),
+        out_shape=(part,) * 4 + (jax.ShapeDtypeStruct((depth, OUT), bf16),),
         cost_estimate=pl.CostEstimate(
             flops=2 * 1024 * depth * OUT, bytes_accessed=6 * 2**20, transcendentals=0
         ),
         compiler_params=BIG,
         name="branch_project",
-    )(o, w)
+    )(at, o, *ws)
+    return outs[:4], outs[4]
 
 
 def attn_bwd_kernel(
@@ -284,7 +429,7 @@
     rows = q.shape[0]
     block = jax.ShapeDtypeStruct(kvs[0].shape, bf16)
     return pl.pallas_call(
-        functools.partial(attn_bwd_kernel, bq=512, bk=512),
+        functools.partial(attn_bwd_kernel, bq=512, bk=1024),
         out_shape=(jax.ShapeDtypeStruct((rows, HEADS * HD), f32), block, block, block, block),
         in_specs=[SMEM] + [VMEM] * 8,
         out_specs=(VMEM,) * 5,
@@ -305,151 +450,149 @@
     )(at, q, *kvs, do, ot, lse)
 
 
+def dhid_kernel(*refs):
+    w_ref, out_ref = refs[4:]
+    for part, cot_ref in enumerate(refs[:4]):
+        out_ref[part * 256 : part * 256 + 256, :] = mm(cot_ref[...], w_ref[...], NN)
+
+
+def dhid_project(cots, w):
+    depth = w.shape[0]
+    return pl.pallas_call(
+        dhid_kernel,
+        grid=(1,),
+        in_specs=[VMEM] * 4 + [pl.BlockSpec((depth, FF_PAD), lambda i: (0, 2))],
+        out_specs=VMEM,
+        out_shape=jax.ShapeDtypeStruct((1024, FF_PAD), f32),
+        cost_estimate=pl.CostEstimate(
+            flops=2 * 1024 * depth * FF_PAD, bytes_accessed=10 * 2**20, transcendentals=0
+        ),
+        compiler_params=BIG,
+        name="dhid_project",
+    )(*cots, w)
+
+
 def ffn_kernel(*refs):
-    hns, cots, w_hbm = refs[:8], refs[8:12], refs[12]
-    hid_ref, dgu_ref = refs[13:15]
-    ys, dns = refs[15:19], refs[19:23]
-    hn_buf, cot_buf, y_buf, dn_buf, w_ref, w_sems, in_sems, out_sems = refs[23:]
+    hns, dhid_ref, w_hbm = refs[:8], refs[8], refs[9]
+    hid_ref, dgu_ref = refs[10:12]
+    dns = refs[12:16]
+    hn_buf, dn_buf, w_ref, w_sems, in_sems, out_sems = refs[16:]
     step = pl.program_id(0)
-    slot = lax.rem(step, 2)
-    parts = [slice(k * FF_PAD, (k + 1) * FF_PAD) for k in range(3)]
+    parts = [slice(k * FF_PAD, (k + 1) * FF_PAD) for k in range(2)]
     weights = [
         pltpu.make_async_copy(w_hbm.at[:, parts[k]], w_ref.at[:, parts[k]], w_sems.at[k])
-        for k in range(3)
+        for k in range(2)
     ]
 
-    def fetch(k):
-        b = k % 2
+    def fetch(s):
         return [
-            pltpu.make_async_copy(hns[2 * k], hn_buf.at[b, :128], in_sems.at[b, 0]),
-            pltpu.make_async_copy(hns[2 * k + 1], hn_buf.at[b, 128:], in_sems.at[b, 1]),
-            pltpu.make_async_copy(cots[k], cot_buf.at[b], in_sems.at[b, 2]),
+            pltpu.make_async_copy(
+                hns[4 * s + k], hn_buf.at[s, k * 128 : k * 128 + 128], in_sems.at[s, k]
+            )
+            for k in range(4)
         ]
 
-    def flush(k):
-        b = k % 2
+    def flush(s):
         return [
-            pltpu.make_async_copy(y_buf.at[b], ys[k], out_sems.at[b, 0]),
-            pltpu.make_async_copy(dn_buf.at[b], dns[k], out_sems.at[b, 1]),
+            pltpu.make_async_copy(
+                dn_buf.at[s, k * 256 : k * 256 + 256], dns[2 * s + k], out_sems.at[s, k]
+            )
+            for k in range(2)
         ]
 
-    def start(copies):
-        for copy in copies:
-            copy.start()
-
-    def wait(copies):
-        for copy in copies:
-            copy.wait()
-
-    def arrived(k):
-        @pl.when(step == 0)
+    def at(s, action, copies):
+        @pl.when(step == s)
         def _():
-            weights[k].wait()
-
-    for k in range(4):
-
-        @pl.when(step == k)
-        def _():
-            if k == 0:
-                start(fetch(0))
-                start(weights)
-            if k < 3:
-                start(fetch(k + 1))
-            wait(fetch(k))
-
-    hn, cot = hn_buf[slot], cot_buf[slot]
-    arrived(0)
+            for copy in copies:
+                action(copy)
+
+    start = lambda copy: copy.start()
+    wait = lambda copy: copy.wait()
+    at(0, start, fetch(0) + weights + fetch(1))
+    for s in range(2):
+        at(s, wait, fetch(s))
+    at(0, wait, weights[:1])
+    hn = hn_buf[step]
     gate = mm(hn, w_ref[:, parts[0]], NN)
-    arrived(1)
+    at(0, wait, weights[1:])
     up = mm(hn, w_ref[:, parts[1]], NN)
-    arrived(2)
-    dhid = mm(cot, w_ref[:, parts[2]], NN)
+    dhid = dhid_ref[...]
     sg = 1.0 / (1.0 + jnp.exp(-gate))
     act = gate * sg
-    hid = (act * up).astype(bf16)
-    dgate = (dhid * up * sg * (1.0 + gate * (1.0 - sg))).astype(bf16)
-    dup = (dhid * act).astype(bf16)
-    hid_ref[...] = hid
-    dgu_ref[:, parts[0]] = dgate
-    dgu_ref[:, parts[1]] = dup
-    for k in (2, 3):
-
-        @pl.when(step == k)
-        def _():
-            wait(flush(k - 2))
-
-    dn_buf[slot] = (mm(dgate, w_ref[:, parts[0]], NT) + mm(dup, w_ref[:, parts[1]], NT)).astype(
-        bf16
-    )
-    y_buf[slot] = mm(hid, w_ref[:, parts[2]], NT).astype(bf16)
-    for k in range(4):
-
-        @pl.when(step == k)
-        def _():
-            start(flush(k))
-            if k == 3:
-                wait(flush(2))
-                wait(flush(3))
-
-
-def ffn(hns, cots, w):
+    hid_ref[...] = (act * up).astype(bf16)
+    dgu_ref[:, parts[0]] = (dhid * up * sg * (1.0 + gate * (1.0 - sg))).astype(bf16)
+    dgu_ref[:, parts[1]] = (dhid * act).astype(bf16)
+    dn_buf[step] = mm(dgu_ref[...], w_ref[...], NT).astype(bf16)
+    for s in range(2):
+        at(s, start, flush(s))
+    at(1, wait, flush(0) + flush(1))
+
+
+def ffn(hns, dhid, w):
     depth = w.shape[0]
-    rowwise = lambda width: pl.BlockSpec((256, width), lambda i: (i, 0))
+    rowwise = lambda width: pl.BlockSpec((512, width), lambda i: (i, 0))
     hbm = pl.BlockSpec(memory_space=pl.ANY)
     quarter = jax.ShapeDtypeStruct((256, depth), bf16)
     outs = pl.pallas_call(
         ffn_kernel,
-        grid=(4,),
-        in_specs=[hbm] * 13,
-        out_specs=(rowwise(FF_PAD), rowwise(2 * FF_PAD)) + (hbm,) * 8,
+        grid=(2,),
+        in_specs=[hbm] * 8 + [rowwise(FF_PAD), hbm],
+        out_specs=(rowwise(FF_PAD), rowwise(2 * FF_PAD)) + (hbm,) * 4,
         out_shape=(
             jax.ShapeDtypeStruct((1024, FF_PAD), bf16),
             jax.ShapeDtypeStruct((1024, 2 * FF_PAD), bf16),
         )
-        + (quarter,) * 8,
-        scratch_shapes=[pltpu.VMEM((2, 256, depth), bf16)] * 4
-        + [
-            pltpu.VMEM((depth, 3 * FF_PAD), bf16),
-            pltpu.SemaphoreType.DMA((3,)),
-            pltpu.SemaphoreType.DMA((2, 3)),
+        + (quarter,) * 4,
+        scratch_shapes=[
+            pltpu.VMEM((2, 512, depth), bf16),
+            pltpu.VMEM((2, 512, depth), bf16),
+            pltpu.VMEM((depth, 2 * FF_PAD), bf16),
+            pltpu.SemaphoreType.DMA((2,)),
+            pltpu.SemaphoreType.DMA((2, 4)),
             pltpu.SemaphoreType.DMA((2, 2)),
         ],
         cost_estimate=pl.CostEstimate(
-            flops=12 * 1024 * depth * FF_PAD,
-            bytes_accessed=35 * 2**20,
+            flops=8 * 1024 * depth * FF_PAD,
+            bytes_accessed=25 * 2**20,
             transcendentals=1024 * FF_PAD,
         ),
         compiler_params=BIG,
         name="ffn",
-    )(*hns, *cots, w)
-    return outs[0], outs[1], outs[2:6], outs[6:10]
+    )(*hns, dhid, w)
+    return outs[0], outs[1], outs[2:]
 
 
 def ffn_grad_kernel(*refs):
     hn = jnp.concatenate([r[...] for r in refs[:8]], 0)
     cot = jnp.concatenate([r[...] for r in refs[8:12]], 0)
-    dgu_ref, hid_ref, out_ref = refs[12:]
+    dgu_ref, hid_ref, w_ref, out_ref = refs[12:16]
+    hid = hid_ref[...]
     out_ref[:, : 2 * FF_PAD] = mm(hn, dgu_ref[...], TN).astype(bf16)
-    out_ref[:, 2 * FF_PAD :] = mm(cot, hid_ref[...], TN).astype(bf16)
-
-
-def ffn_grad(hns, cots, dgu, hid):
+    out_ref[:, 2 * FF_PAD :] = mm(cot, hid, TN).astype(bf16)
+    for part, y_ref in enumerate(refs[16:]):
+        y_ref[...] = mm(hid[part * 256 : part * 256 + 256], w_ref[...], NT).astype(bf16)
+
+
+def ffn_grad(hns, cots, dgu, hid, w):
     depth = hns[0].shape[1]
     block = 256
-    return pl.pallas_call(
+    piece = lambda rows: pl.BlockSpec((rows, block), lambda i: (0, i))
+    outs = pl.pallas_call(
         ffn_grad_kernel,
         grid=(depth // block,),
-        in_specs=[pl.BlockSpec((128, block), lambda i: (0, i))] * 8
-        + [pl.BlockSpec((256, block), lambda i: (0, i))] * 4
-        + [VMEM] * 2,
-        out_specs=pl.BlockSpec((block, 3 * FF_PAD), lambda i: (i, 0)),
-        out_shape=jax.ShapeDtypeStruct((depth, 3 * FF_PAD + OUT), bf16),
+        in_specs=[piece(a.shape[0]) for a in hns + cots]
+        + [VMEM] * 2
+        + [pl.BlockSpec((block, FF_PAD), lambda i: (i, 2))],
+        out_specs=(pl.BlockSpec((block, 3 * FF_PAD), lambda i: (i, 0)),) + (piece(256),) * 4,
+        out_shape=(jax.ShapeDtypeStruct((depth, 3 * FF_PAD + OUT), bf16),)
+        + (jax.ShapeDtypeStruct((256, depth), bf16),) * 4,
         cost_estimate=pl.CostEstimate(
-            flops=6 * 1024 * depth * FF_PAD, bytes_accessed=24 * 2**20, transcendentals=0
+            flops=8 * 1024 * depth * FF_PAD, bytes_accessed=30 * 2**20, transcendentals=0
         ),
         compiler_params=BIG,
         name="ffn_grad",
-    )(*hns, *cots, dgu, hid)
+    )(*hns, *cots, dgu, hid, w)
+    return outs[0], outs[1:]
 
 
 def dh_kernel(*refs):
@@ -488,18 +631,19 @@
     )(*pieces, w, ob, grads)
 
 
-def qkv_grad_kernel(x0, x1, x2, x3, near_ref, far_ref, out_ref):
-    xh = jnp.concatenate([r[...] for r in (x0, x1, x2, x3)], 0)
-    out_ref[...] = mm(xh, jnp.concatenate([near_ref[...], far_ref[...]], 0), TN).astype(bf16)
-
-
-def qkv_grad(xs, dqkvs):
+def qkv_grad_kernel(*refs):
+    xh = jnp.concatenate([r[...] for r in refs[:4]], 0)
+    dqkv_ref, out_ref = refs[4:]
+    out_ref[...] = mm(xh, dqkv_ref[...], TN).astype(bf16)
+
+
+def qkv_grad(xs, dqkv):
     depth = xs[0].shape[1]
     block = 512
     return pl.pallas_call(
         qkv_grad_kernel,
         grid=(depth // block,),
-        in_specs=[pl.BlockSpec((256, block), lambda i: (0, i))] * 4 + [VMEM] * 2,
+        in_specs=[pl.BlockSpec((x.shape[0], block), lambda i: (0, i)) for x in xs] + [VMEM],
         out_specs=pl.BlockSpec((block, 384), lambda i: (i, 0)),
         out_shape=jax.ShapeDtypeStruct((depth, 384), bf16),
         cost_estimate=pl.CostEstimate(
@@ -507,11 +651,12 @@
         ),
         compiler_params=BIG,
         name="qkv_grad",
-    )(*xs, *dqkvs)
+    )(*xs, dqkv)
 
 
 def dqkv_kernel(at_ref, dq_ref, *refs):
-    parts, (w_ref, cos_ref, sin_ref, dqkv_ref, keep_ref, send_ref) = refs[:8], refs[8:]
+    parts, (w_ref, cos_ref, sin_ref, dqkv_ref) = refs[:8], refs[8:12]
+    far_send, near_send, far_keep, near_keep = refs[12:]
     cosine, sine = cos_ref[...], -sin_ref[...]
     core = at_ref[2]
     for part in range(2):
@@ -524,36 +669,31 @@
     mine = jnp.where(is_key, 1 - core, core) > 0
     dqkv_ref[:, 256:] = jnp.where(mine, turned, 0.0).astype(bf16)
     dn = mm(dqkv_ref[...], w_ref[...], NT).astype(bf16)
-
-    @pl.when(pl.program_id(0) == 0)
-    def _():
-        send_ref[...] = dn
-
-    @pl.when(pl.program_id(0) == 1)
-    def _():
-        keep_ref[...] = dn
-
-
-def dqkv_project(half, at, dq, dkvs, others, w, cosine, sine):
+    for step, out_ref in enumerate((far_send, near_send, far_keep, near_keep)):
+
+        @pl.when(pl.program_id(0) == step)
+        def _():
+            out_ref[...] = dn
+
+
+def dqkv_project(at, dq, dkvs, others, w, cosine, sine):
     depth = w.shape[0]
-    turned = pl.BlockSpec((256, 128), lambda i: (2 * half + i, 0))
-    rowwise = lambda width: pl.BlockSpec((256, width), lambda i: (2 * half + 1 - i, 0))
+    own = lambda i: jnp.where(i < 2, 3 - 2 * i, 6 - 2 * i)
+    rowwise = lambda width: pl.BlockSpec((256, width), lambda i: (own(i), 0))
+    turned = pl.BlockSpec((256, 128), lambda i: (own(i) ^ 1, 0))
     whole = pl.BlockSpec((256, depth), lambda i: (0, 0))
     return pl.pallas_call(
         dqkv_kernel,
-        grid=(2,),
+        grid=(4,),
         in_specs=[SMEM, rowwise(256)]
         + [rowwise(128)] * 4
         + [turned] * 4
         + [VMEM, rowwise(128), rowwise(128)],
-        out_specs=(pl.BlockSpec((256, 384), lambda i: (1 - i, 0)), whole, whole),
-        out_shape=(
-            jax.ShapeDtypeStruct((512, 384), bf16),
-            jax.ShapeDtypeStruct((256, depth), bf16),
-            jax.ShapeDtypeStruct((256, depth), bf16),
-        ),
+        out_specs=(rowwise(384),) + (whole,) * 4,
+        out_shape=(jax.ShapeDtypeStruct((1024, 384), bf16),)
+        + (jax.ShapeDtypeStruct((256, depth), bf16),) * 4,
         cost_estimate=pl.CostEstimate(
-            flops=2 * 512 * depth * 384, bytes_accessed=6 * 2**20, transcendentals=0
+            flops=2 * 1024 * depth * 384, bytes_accessed=10 * 2**20, transcendentals=0
         ),
         compiler_params=BIG,
         name="dqkv_project",
@@ -565,15 +705,22 @@
     return lax.ppermute(value, axes, [(i, count - 1 - i) for i in range(count)])
 
 
+def crossed(value, axis, mask):
+    return lax.ppermute(value, axis, [(i, i ^ mask) for i in range(4)])
+
+
 def shifted(value, steps):
     first, last = max(0, -steps), min(4, 4 - steps)
     return lax.ppermute(value, "z", [(i, i + steps) for i in range(first, last)])
 
 
-def gather_group(own):
-    by_l, by_c = swap(own, ("yl",)), swap(own, ("c",))
-    by_d, by_h = swap(own, ("yh", "yl")), swap(own, ("yh",))
-    near = [own, by_l, by_c, swap(by_l, ("c",))]
+def gather_chips(own):
+    return swap(own, ("yl",)), swap(own, ("yh", "yl")), swap(own, ("yh",))
+
+
+def gather_cores(own, received):
+    by_l, by_d, by_h = received
+    near = [own, by_l, swap(own, ("c",)), swap(by_l, ("c",))]
     return near + [by_h, by_d, swap(by_h, ("c",)), swap(by_d, ("c",))]
 
 
@@ -623,43 +770,19 @@
     gain_one = norm_attn.astype(f32)[:, None]
     gain_two = norm_ffn.astype(f32)[:, None]
     flip = (yh * 4 + core * 2 + yl) * 128
-    at = jnp.stack([z, flip, core]).astype(jnp.int32)
-
-    both = lambda a: jnp.where(yl == 0, a, jnp.concatenate([a[128:], a[:128]], 0))
-    inputs = both(tokens[0]).astype(f32)
-    inverse_one = lax.rsqrt(jnp.mean(inputs * inputs, axis=-1, keepdims=True) + epsilon)
-    xh = (inputs * inverse_one).astype(bf16)
-    inputs, inverse_one = inputs[:128], inverse_one[:128]
-    cot_here = both(cotangent[0])
-
-    def by_model(w):
-        return w.reshape(32, 4, -1).transpose(1, 0, 2)
-
-    def by_head(w):
-        return jnp.repeat(w.reshape(32, 2, HD).transpose(1, 0, 2), 2, axis=0)
-
-    scaled = lambda w, gain: (w.astype(f32) * gain).astype(bf16)
-
-    def padded(w):
-        return jnp.pad(by_model(w), ((0, 0), (0, 0), (0, FF_PAD - FF_BLOCK)))
-
-    qkv_rows = jnp.concatenate(
-        [
-            by_model(scaled(w_query, gain_one)),
-            by_head(scaled(w_key, gain_one)),
-            by_head(scaled(w_value, gain_one)),
-        ],
-        -1,
-    )
-    ffn_rows = jnp.concatenate(
-        [padded(scaled(w_gate, gain_two)), padded(scaled(w_up, gain_two)), padded(w_down.T)], -1
-    )
-
-    def spread(rows):
-        copies = jnp.broadcast_to(rows[None], (16,) + rows.shape).reshape(64, 32, -1)
-        return lax.all_to_all(copies, ALL, 0, 0).reshape(2048, -1)
-
-    w_qkv = spread(qkv_rows)
+    at = jnp.stack([z, flip, core, yl, lax.axis_index("x")]).astype(jnp.int32)
+
+    xh, inverse_one, cot_here = order(at, tokens[0], cotangent[0])
+    inputs = lax.dynamic_slice_in_dim(tokens[0], yl * 128, 128, 0).astype(f32)
+
+    xh_c, xh_h = swap(xh, ("c",)), swap(xh, ("yh",))
+    copies, rest, out_rows = prepare(
+        w_query, w_key, w_value, w_output.T, w_gate, w_up, w_down.T, gain_one, gain_two
+    )
+    w_qkv = lax.all_to_all(copies, ALL, 0, 0).reshape(2048, 384)
+    rest = trade_chips(trade_cores(rest, core), yh)
+    out_rows = trade_chips(trade_cores(out_rows, core), yh).reshape(128, OUT)
+
     positions = (z * 1024 + (jnp.arange(1024, dtype=jnp.int32) ^ flip)).astype(f32)
     freqs = rope_base ** (-2.0 * jnp.arange(HD // 2, dtype=f32) / HD)
     angles = positions[:, None] * freqs[None, :]
@@ -667,32 +790,36 @@
     cosine = jnp.concatenate([cosine] * 4, -1)
     sine = jnp.concatenate([-sine, sine, -sine, sine], -1)
 
-    xh_c, xh_h = swap(xh, ("c",)), swap(xh, ("yh",))
-    ffn_rows = trade_chips(trade_cores(ffn_rows, core), yh).reshape(128, -1)
-    out_rows = by_model(w_output.T)
-    xh_h, w_qkv, cosine, sine, cot_here, ffn_rows, out_rows = together(
-        (xh_h, w_qkv, cosine, sine, cot_here, ffn_rows, out_rows)
+    xh_h, w_qkv, cosine, sine, rest, out_rows = together(
+        (xh_h, w_qkv, cosine, sine, rest, out_rows)
     )
     xhs = [xh, xh_c, xh_h, swap(xh_h, ("c",))]
 
     q, kv = qkv_project(xhs, w_qkv, cosine, sine)
+    kv, out_rows = together((kv, out_rows))
+    kvs = [kv] + [shifted(kv, by) for by in (1, 2, 3)]
+    ws = jnp.concatenate([out_rows] + [crossed(out_rows, "x", mask) for mask in (1, 2, 3)], 0)
+    kvs, rest, ws, cot_here = together((kvs, rest, ws, cot_here))
+    w_ffn = lax.all_gather(rest.reshape(128, -1), ("x", "z"), axis=0, tiled=True)
+    ws = [ws] + [crossed(ws, "z", mask) for mask in (1, 2, 3)]
     cot_c, cot_h = swap(cot_here, ("c",)), swap(cot_here, ("yh",))
-    kvs = [kv] + [shifted(kv, by) for by in (1, 2, 3)]
-    kvs, cot_h, ffn_rows, out_rows = together((kvs, cot_h, ffn_rows, out_rows))
-    w_ffn = lax.all_gather(ffn_rows, ("x", "z"), axis=0, tiled=True)
-    w_out = spread(out_rows)
+    ob, o_t, lse = attn_fwd(at, q, kvs)
+    ob, cot_h, ws = together((ob, cot_h, ws))
     cots = [cot_here, cot_c, cot_h, swap(cot_h, ("c",))]
-    ob, o_t, lse = attn_fwd(at, q, kvs)
-    branch = branch_project(ob, w_out)
+    branch, w_out = branch_project(at, ob, ws)
     near, far = sum_cores(*branch[:2]), sum_cores(*branch[2:])
     middle = inputs + sum_chips(near, from_chips(near, far))
     inverse_two = lax.rsqrt(jnp.mean(middle * middle, axis=-1, keepdims=True) + epsilon)
-    hns = gather_group((middle * inverse_two).astype(bf16))
-
-    hid, dgu, ys, dns = ffn(hns, cots, w_ffn)
+    hn = (middle * inverse_two).astype(bf16)
+
+    received = gather_chips(hn)
+    dhid = dhid_project(cots, w_ffn)
+    received, dhid = together((received, dhid))
+    hns = gather_cores(hn, received)
+    hid, dgu, dns = ffn(hns, dhid, w_ffn)
     near, far = sum_cores(*dns[:2]), sum_cores(*dns[2:])
     received = from_chips(near, far)
-    grads = ffn_grad(hns, cots, dgu, hid)
+    grads, ys = ffn_grad(hns, cots, dgu, hid, w_ffn)
     received, grads = together((received, grads))
     dn2 = sum_chips(near, received)
     dh = (
@@ -701,9 +828,10 @@
         - middle * inverse_two**3 * jnp.mean(dn2 * middle, axis=-1, keepdims=True)
     )
     dh_low, ys = together((dh.astype(bf16), ys))
-    dhs = gather_group(dh_low)
+    received = gather_chips(dh_low)
     y_near, y_far = sum_cores(*ys[:2]), sum_cores(*ys[2:])
-    dhs, y_near, y_far = together((dhs, y_near, y_far))
+    received, y_near, y_far = together((received, y_near, y_far))
+    dhs = gather_cores(dh_low, received)
 
     do, grads = dh_project(dhs, w_out, ob, grads)
     grads = lax.psum_scatter(grads, ("x", "z"), scatter_dimension=0, tiled=True)
@@ -718,13 +846,14 @@
     dkvs, block_other = together((dkvs, block_other))
     block_out = both_halves(block_out, block_other, yl)
     others = [swap(part, ("c",)) for part in dkvs]
-    dqkv_far, dn_far, dn_far_c = dqkv_project(1, at, dq, dkvs, others, w_qkv, cosine, sine)
-    dqkv_near, dn_near, dn_near_c = dqkv_project(0, at, dq, dkvs, others, w_qkv, cosine, sine)
-    near, far = sum_cores(dn_near, dn_near_c), sum_cores(dn_far, dn_far_c)
-    near, far, dqkv_near, dqkv_far = together((near, far, dqkv_near, dqkv_far))
+    dqkv, far_send, near_send, far_keep, near_keep = dqkv_project(
+        at, dq, dkvs, others, w_qkv, cosine, sine
+    )
+    near, far = sum_cores(near_keep, near_send), sum_cores(far_keep, far_send)
+    near, far, dqkv = together((near, far, dqkv))
     received = from_chips(near, far)
     dn1 = sum_chips(near, received)
-    grad_qkv = qkv_grad(xhs, (dqkv_near, dqkv_far))
+    grad_qkv = qkv_grad(xhs, dqkv)
     grad_qkv = lax.all_to_all(grad_qkv.reshape(16, 128, 384), ("x", "z"), 0, 0)
     grads = trade_cores(grads.reshape(4, 32, 3 * FF_PAD + OUT), core)
     input_grad = (
@@ -735,41 +864,28 @@
     input_grad, grad_qkv, grads = together((input_grad, grad_qkv, grads))
     other = swap(input_grad.astype(bf16), ("yl",)).astype(f32)
     input_grad = both_halves(input_grad, other, yl)
-    grads = trade_chips(grads, yh).astype(f32)
     grad_qkv = jnp.sum(grad_qkv.astype(f32), 0).astype(bf16).reshape(4, 32, 384)
-    grad_qkv = trade_chips(trade_cores(grad_qkv, core), yh).astype(f32)
-
-    def joined(parts):
-        return parts.transpose(1, 0, 2).reshape(32, -1)
-
-    ffn_part = lambda k: joined(grads[:, :, k * FF_PAD : k * FF_PAD + FF_BLOCK])
-    grad_gate, grad_up, grad_down = ffn_part(0), ffn_part(1), ffn_part(2).T
-    grad_query = joined(grad_qkv[:, :, :256])
-    by_core = grad_qkv[:, :, 256:].reshape(2, 2, 32, 2 * HD).sum(1)
-    grad_key, grad_value = joined(by_core[:, :, :HD]), joined(by_core[:, :, HD:])
-
-    def gain_grad(*pairs):
-        return sum(jnp.sum(w.astype(f32) * grad, 1) for w, grad in pairs)
-
-    gains = jnp.stack(
-        [
-            gain_grad((w_query, grad_query), (w_key, grad_key), (w_value, grad_value)),
-            gain_grad((w_gate, grad_gate), (w_up, grad_up)),
-        ]
-    )
-    gains = gains + swap(gains, ("yl",))
+    grad_qkv = trade_chips(trade_cores(grad_qkv, core), yh)
+    grad_gate, grad_up, grad_down, grad_out, gain_grad_two = finish_ffn(
+        trade_chips(grads, yh), w_gate, w_up, gain_two
+    )
+    grad_query, grad_key, grad_value, gain_grad_one = finish_qkv(
+        grad_qkv, w_query, w_key, w_value, gain_one
+    )
+    gain_grad_one = gain_grad_one + swap(gain_grad_one, ("yl",))
+    gain_grad_two = gain_grad_two + swap(gain_grad_two, ("yl",))
     return (
         block_out[None],
         input_grad[None],
-        grad_query * gain_one,
-        grad_key * gain_one,
-        grad_value * gain_one,
-        joined(grads[:, :, 3 * FF_PAD :]).T,
-        grad_gate * gain_two,
-        grad_up * gain_two,
-        grad_down,
-        gains[0],
-        gains[1],
+        grad_query,
+        grad_key,
+        grad_value,
+        grad_out.T,
+        grad_gate,
+        grad_up,
+        grad_down.T,
+        gain_grad_one[:, 0],
+        gain_grad_two[:, 0],
     )
 
 

time: 498 us -> 476 us (0.956)
  local copies, waits for them, and re-layouts: 36.4 us -> 19.5 us
  other arithmetic: 49.2 us -> 32.8 us
  Pallas kernels: 106 us -> 117 us
    all_to_all x2 -> x1, waiting for transfers between devices: 20.7 us -> 0.01 us  [on_device(): w_qkv = lax.all_to_all(copies, ALL, 0, 0).reshape(2048, 384)]
    pallas_call x6 -> x10, Pallas kernels: 80.1 us -> 90.3 us  [the longest x1 23.6 us: ffn(): pl.pallas_call(ffn_kernel, grid=(2,), in_specs=[hbm] * 8 + [rowwise(FF_PA...]
    all_to_all x2 -> x1, starting transfers between devices: 18.8 us -> 8.74 us  [on_device(): w_qkv = lax.all_to_all(copies, ALL, 0, 0).reshape(2048, 384)]
    ppermute x6, waiting for transfers between devices: 32.6 us -> 41.8 us  [shifted(): lax.ppermute(value, 'z', [(i, i + steps) for i in range(first, last)])]
    ppermute x0 -> x6, waiting for transfers between devices: none -> 7.97 us  [crossed(): return lax.ppermute(value, axis, [(i, i ^ mask) for i in range(4)])]
    reshape x13 -> x0, local copies, waits for them, and re-layouts: 7.78 us -> none  [the longest x5 5.94 us: by_model(): return w.reshape(32, 4, -1).transpose(1, 0, 2)]
    ppermute x0 -> x6, starting transfers between devices: none -> 7.64 us  [crossed(): return lax.ppermute(value, axis, [(i, i ^ mask) for i in range(4)])]
    reduce_sum x5 -> x0, other arithmetic: 5.35 us -> none  [the longest x3 3.72 us: gain_grad(): return sum((jnp.sum(w.astype(f32) * grad, 1) for w, grad in pairs))]
  transfers between devices with their start and end apart: 64 -> 72, of which waited for: 28 -> 39; matrix products, arithmetic and copies ran while one was open for 13% -> 8% of each run, Pallas kernels for 14% -> 17%
where the time goes in v3:
time: 476 us; the launch traced here: 467 us
  waiting for transfers between devices  185 us (39%)
  Pallas kernels  117 us (25%)
  starting transfers between devices  97 us (20%)
  other arithmetic  32.8 us (7%)
  local copies, waits for them, and re-layouts  19.5 us (4%)
  between operations  15.3 us (3%)
    ppermute x56, waiting for transfers between devices, swap(): return lax.ppermute(value, axes, [(i, count - 1 - i) for i in range(count)])  130 us
    ppermute x56, starting transfers between devices, swap(): return lax.ppermute(value, axes, [(i, count - 1 - i) for i in range(count)])  59.6 us
    ppermute x6, waiting for transfers between devices, shifted(): lax.ppermute(value, 'z', [(i, i + steps) for i in range(first, last)])  41.8 us
    pallas_call x1, Pallas kernels, ffn(): pl.pallas_call(ffn_kernel, grid=(2,), in_specs=[hbm] * 8 + [rowwise(FF_PA...  23.6 us
    pallas_call x1, Pallas kernels, ffn_grad(): pl.pallas_call(ffn_grad_kernel, grid=(depth // block,), in_specs=[piece(a...  19.2 us
    pallas_call x1, Pallas kernels, attn_bwd(): pl.pallas_call(functools.partial(attn_bwd_kernel, bq=512, bk=1024), out_s...  14.1 us
    ppermute x6, starting transfers between devices, shifted(): lax.ppermute(value, 'z', [(i, i + steps) for i in range(first, last)])  14 us
  transfers between devices with their start and end apart: 72, of which 39 were waited for; matrix products, arithmetic and copies ran while one was open for 8% of the time, Pallas kernels for 17%

profile of v3, /device:TPU:1, one launch (start us, length us, event | category | flops | bytes accessed | tf_op | source)
XLA Modules:
  0.0 466.6 jit_solution(11646078024652059629)
XLA Ops:
  7.8 3.2 order.1
  19.8 8.7 %all-to-all-start = ((bf16[64,32,384]{2,1,0:T(8,128)(2,1)}), bf16[64,32,384]{2,1,0:T(8,128)(2,1)S(1)}, u32[]{:S(2)}, u32[]{:S(2)}) async-start(bf16[64,32,384]{2,1,0:T(8,128)(2,1)} %get-tuple-element.125), calls=%async_computation | async-start | bytes 3145728 | tf_op jit(solution)/shard_map/all_to_all | solution.py:782
  41.0 22.0 %collective-permute-done.5 = bf16[2,32,256]{2,1,0:T(8,128)(2,1)S(1)} collective-permute-done((bf16[2,32,256]{2,1,0:T(8,128)(2,1)S(1)}, bf16[2,32,256]{2,1,0:T(8,128)(2,1)S(1)}, u32[]{:S(2)}, u32[]{:S(2)}) %collective-permute-start.5) | collective-permute-done | bytes 32800 | tf_op jit(solution)/shard_map/ppermute | solution.py:705
  69.3 6.3 %qkv_project.1 = (bf16[1024,256]{1,0:T(8,128)(2,1)}, bf16[1024,128]{1,0:T(8,128)(2,1)}) custom-call(bf16[256,2048]{1,0:T(8,128)(2,1)} %get-tuple-element.124.refs_0_, bf16[256,2048]{1,0:T(8,128)(2,1)} %copy-done.4, bf16[256,2048]{1,0:T(8,128)(2,1)} %collective-permute-done.1.refs_2_, bf16[256,2048]{1,0:T(8,128)(2,1)} %copy-done.5, ...), custom_call_target="tpu_custom_call" | custom-call | flops 1610612736 | bytes 6291456 | tf_op jit(solution)/shard_map/qkv_project/pallas_call | solution.py:198
  75.7 3.7 collective-permute-start.7
  79.4 5.1 %collective-permute-start.8 = (bf16[1024,128]{1,0:T(8,128)(2,1)}, bf16[1024,128]{1,0:T(8,128)(2,1)S(1)}, u32[]{:S(2)}, u32[]{:S(2)}) collective-permute-start(bf16[1024,128]{1,0:T(8,128)(2,1)} %get-tuple-element.139.kv0), channel_id=1, source_target_pairs={{0,16},{8,24},{1,17},{9,25},{2,18},{10,26},{3,19},{11,27},{4,20},{... | collective-permute-start | bytes 786440 | tf_op jit(solution)/shard_map/ppermute | solution.py:714
  95.1 4.5 collective-permute-start.15
  102.5 8.1 %attn_fwd.1 = (bf16[1024,256]{1,0:T(8,128)(2,1)}, f32[256,1024]{1,0:T(8,128)}, f32[4,1024]{1,0:T(4,128)}) custom-call(s32[5]{0:T(128)} %stack.127.at_ref, bf16[1024,256]{1,0:T(8,128)(2,1)} %get-tuple-element.132.q_ref, bf16[1024,128]{1,0:T(8,128)(2,1)} %get-tuple-element.139.kv0, bf16[1024,128]{1,0:T(8,128)(2,1)} %copy-done.42, ...), custom_call_target="tpu_custom_call" | custom-call | flops 24999999488 | bytes 6291456 | tf_op jit(solution)/shard_map/attn_fwd/pallas_call | solution.py:291
  114.1 10.0 %collective-permute-done.13.refs_2_.refs_10_ = bf16[256,2048]{1,0:T(8,128)(2,1)} collective-permute-done((bf16[256,2048]{1,0:T(8,128)(2,1)}, bf16[256,2048]{1,0:T(8,128)(2,1)}, u32[]{:S(2)}, u32[]{:S(2)}) %collective-permute-start.13) | collective-permute-done | bytes 1048608 | tf_op jit(solution)/shard_map/ppermute | solution.py:705
  124.1 6.2 %branch_project.1 = (bf16[256,2048]{1,0:T(8,128)(2,1)}, bf16[256,2048]{1,0:T(8,128)(2,1)}, bf16[256,2048]{1,0:T(8,128)(2,1)}, bf16[256,2048]{1,0:T(8,128)(2,1)}, bf16[2048,256]{1,0:T(8,128)(2,1)}) custom-call(s32[5]{0:T(128)} %stack.127.at_ref, bf16[1024,256]{1,0:T(8,128)(2,1)} %get-tuple-element.146.o_ref.refs_9_, bf16[512,256]{1,0:T(8,128)(2,1)} %copy-done.31, ...), custom_call_target="tpu_custom_call" | custom-call | flops 1073741824 | bytes 6291456 | tf_op jit(solution)/shard_map/branch_project/pallas_call | solution.py:331
  145.8 7.6 %collective-permute-done.21 = bf16[128,2048]{1,0:T(8,128)(2,1)S(1)} collective-permute-done((bf16[128,2048]{1,0:T(8,128)(2,1)}, bf16[128,2048]{1,0:T(8,128)(2,1)S(1)}, u32[]{:S(2)}, u32[]{:S(2)}) %collective-permute-start.21) | collective-permute-done | bytes 524320 | tf_op jit(solution)/shard_map/ppermute | solution.py:705
  153.3 12.0 %collective-permute-done.20 = bf16[128,2048]{1,0:T(8,128)(2,1)S(1)} collective-permute-done((bf16[128,2048]{1,0:T(8,128)(2,1)}, bf16[128,2048]{1,0:T(8,128)(2,1)S(1)}, u32[]{:S(2)}, u32[]{:S(2)}) %collective-permute-start.20) | collective-permute-done | bytes 524320 | tf_op jit(solution)/shard_map/ppermute | solution.py:705
  174.9 8.3 %dhid_project.1.refs_8_ = f32[1024,768]{1,0:T(8,128)} custom-call(bf16[256,2048]{1,0:T(8,128)(2,1)} %get-tuple-element.144.refs_0_.refs_8_, bf16[256,2048]{1,0:T(8,128)(2,1)} %copy-done.13, bf16[256,2048]{1,0:T(8,128)(2,1)} %collective-permute-done.13.refs_2_.refs_10_, bf16[256,2048]{1,0:T(8,128)(2,1)} %collective-permute-done.26.refs_3_.refs_11_, ...), custom_call_target="tpu_custom_call" | custom-call | flops 3221225472 | bytes 10485760 | tf_op jit(solution)/shard_map/dhid_project/pallas_call | solution.py:461
  183.2 10.2 %collective-permute-done.23.refs_5_ = bf16[128,2048]{1,0:T(8,128)(2,1)} collective-permute-done((bf16[128,2048]{1,0:T(8,128)(2,1)S(1)}, bf16[128,2048]{1,0:T(8,128)(2,1)}, u32[]{:S(2)}, u32[]{:S(2)}) %collective-permute-start.23) | collective-permute-done | bytes 524320 | tf_op jit(solution)/shard_map/ppermute | solution.py:705
  200.8 23.6 %ffn.1 = (bf16[1024,768]{1,0:T(8,128)(2,1)}, bf16[1024,1536]{1,0:T(8,128)(2,1)}, bf16[256,2048]{1,0:T(8,128)(2,1)}, bf16[256,2048]{1,0:T(8,128)(2,1)}, bf16[256,...) custom-call(bf16[128,2048]{1,0:T(8,128)(2,1)} %copy-done.30, bf16[128,2048]{1,0:T(8,128)(2,1)} %copy-done.37, ...), custom_call_target="tpu_custom_call" | custom-call | flops 12884901888 | bytes 26214400 | tf_op jit(solution)/shard_map/ffn/pallas_call | solution.py:536
  233.2 19.2 %ffn_grad.1 = (bf16[2048,2560]{1,0:T(8,128)(2,1)}, bf16[256,2048]{1,0:T(8,128)(2,1)}, bf16[256,2048]{1,0:T(8,128)(2,1)}, bf16[256,2048]{1,0:T(8,128)(2,1)}, bf16[256,2048]{1,0:T(8,128)(2,1)}) custom-call(bf16[128,2048]{1,0:T(8,128)(2,1)} %copy-done.30, bf16[128,2048]{1,0:T(8,128)(2,1)} %copy-done.37, bf16[128,2048]{1,0:T(8,128)(2,1)} %copy-done.38, ...), custom_call_target="tpu_custom_call" | custom-call | flops 12884901888 | bytes 31457280 | tf_op jit(solution)/shard_map/ffn_grad/pallas_call | solution.py:580
  264.9 7.4 %collective-permute-done.36.refs_1_ = bf16[128,2048]{1,0:T(8,128)(2,1)S(1)} collective-permute-done((bf16[128,2048]{1,0:T(8,128)(2,1)S(1)}, bf16[128,2048]{1,0:T(8,128)(2,1)S(1)}, u32[]{:S(2)}, u32[]{:S(2)}) %collective-permute-start.36) | collective-permute-done | bytes 524320 | tf_op jit(solution)/shard_map/ppermute | solution.py:705
  273.4 11.5 %collective-permute-done.38.refs_4_ = bf16[128,2048]{1,0:T(8,128)(2,1)S(1)} collective-permute-done((bf16[128,2048]{1,0:T(8,128)(2,1)S(1)}, bf16[128,2048]{1,0:T(8,128)(2,1)S(1)}, u32[]{:S(2)}, u32[]{:S(2)}) %collective-permute-start.38) | collective-permute-done | bytes 524320 | tf_op jit(solution)/shard_map/ppermute | solution.py:705
  289.7 5.8 %dh_project.1 = (bf16[1024,256]{1,0:T(8,128)(2,1)}, bf16[2048,2560]{1,0:T(8,128)(2,1)}) custom-call(bf16[128,2048]{1,0:T(8,128)(2,1)} %copy-done.8, bf16[128,2048]{1,0:T(8,128)(2,1)} %copy-done.21, bf16[128,2048]{1,0:T(8,128)(2,1)} %copy-done.24, bf16[128,2048]{1,0:T(8,128)(2,1)} %copy-done.27, ...), custom_call_target="tpu_custom_call", output_to_operand_aliasing={{1}: (10, {})} | custom-call | flops 2147483648 | bytes 8388608 | tf_op jit(solution)/shard_map/dh_project/pallas_call | solution.py:616
  300.4 14.1 %attn_bwd.1 = (f32[1024,256]{1,0:T(8,128)}, bf16[1024,128]{1,0:T(8,128)(2,1)}, bf16[1024,128]{1,0:T(8,128)(2,1)}, bf16[1024,128]{1,0:T(8,128)(2,1)}, bf16[1024,128]{1,0:T(8,128)(2,1)}) custom-call(s32[5]{0:T(128)} %stack.127.at_ref, bf16[1024,256]{1,0:T(8,128)(2,1)} %get-tuple-element.132.q_ref, bf16[1024,128]{1,0:T(8,128)(2,1)} %get-tuple-element.139.kv0, ...), custom_call_target="tpu_custom_call" | custom-call | flops 49999998976 | bytes 8388608 | tf_op jit(solution)/shard_map/attn_bwd/pallas_call | solution.py:431
  314.5 8.0 %collective-permute-done.46 = bf16[128,2048]{1,0:T(8,128)(2,1)S(1)} collective-permute-done((bf16[128,2048]{1,0:T(8,128)(2,1)S(1)}, bf16[128,2048]{1,0:T(8,128)(2,1)S(1)}, u32[]{:S(2)}, u32[]{:S(2)}) %collective-permute-start.46) | collective-permute-done | bytes 524320 | tf_op jit(solution)/shard_map/ppermute | solution.py:705
  327.8 12.4 %collective-permute-done.48.refs_1_ = bf16[1024,128]{1,0:T(8,128)(2,1)S(1)} collective-permute-done((bf16[1024,128]{1,0:T(8,128)(2,1)S(1)}, bf16[1024,128]{1,0:T(8,128)(2,1)S(1)}, u32[]{:S(2)}, u32[]{:S(2)}) %collective-permute-start.48) | collective-permute-done | bytes 262176 | tf_op jit(solution)/shard_map/ppermute | solution.py:714
  340.1 12.2 %collective-permute-done.49.refs_2_ = bf16[1024,128]{1,0:T(8,128)(2,1)S(1)} collective-permute-done((bf16[1024,128]{1,0:T(8,128)(2,1)S(1)}, bf16[1024,128]{1,0:T(8,128)(2,1)S(1)}, u32[]{:S(2)}, u32[]{:S(2)}) %collective-permute-start.49) | collective-permute-done | bytes 262176 | tf_op jit(solution)/shard_map/ppermute | solution.py:714
  352.3 15.7 %collective-permute-done.50.refs_3_ = bf16[1024,128]{1,0:T(8,128)(2,1)S(1)} collective-permute-done((bf16[1024,128]{1,0:T(8,128)(2,1)S(1)}, bf16[1024,128]{1,0:T(8,128)(2,1)S(1)}, u32[]{:S(2)}, u32[]{:S(2)}) %collective-permute-start.50) | collective-permute-done | bytes 262176 | tf_op jit(solution)/shard_map/ppermute | solution.py:714
  373.5 8.6 %dqkv_project.1 = (bf16[1024,384]{1,0:T(8,128)(2,1)}, bf16[256,2048]{1,0:T(8,128)(2,1)}, bf16[256,2048]{1,0:T(8,128)(2,1)}, bf16[256,2048]{1,0:T(8,128)(2,1)}, bf16[256,2048]{1,0:T(8,128)(2,1)}) custom-call(s32[5]{0:T(128)} %stack.127.at_ref, f32[1024,256]{1,0:T(8,128)} %get-tuple-element.211.dq_ref, bf16[1024,128]{1,0:T(8,128)(2,1)} %get-tuple-element.212.refs_0_, ...), custom_call_target="tpu_custom_call" | custom-call | flops 1610612736 | bytes 10485760 | tf_op jit(solution)/shard_map/dqkv_project/pallas_call | solution.py:685
  393.1 6.0 %qkv_grad.1 = bf16[2048,384]{1,0:T(8,128)(2,1)} custom-call(bf16[256,2048]{1,0:T(8,128)(2,1)} %get-tuple-element.124.refs_0_, bf16[256,2048]{1,0:T(8,128)(2,1)} %copy-done.4, bf16[256,2048]{1,0:T(8,128)(2,1)} %collective-permute-done.1.refs_2_, bf16[256,2048]{1,0:T(8,128)(2,1)} %copy-done.5, bf16[1024,384]{1,0:T(8,128)(2,1)} %get-tuple-element.223.refs_4_), custom_call_target="tpu_custom_call" | custom-call | flops 1610612736 | bytes 8388608 | tf_op jit(solution)/shard_map/qkv_grad/pallas_call | solution.py:643
  399.1 7.0 %all-to-all-start.1 = ((bf16[16,128,384]{2,1,0:T(8,128)(2,1)}), bf16[16,128,384]{2,1,0:T(8,128)(2,1)}, u32[]{:S(2)}, u32[]{:S(2)}) async-start(bf16[16,128,384]{2,1,0:T(8,128)(2,1)} %bitcast.66), calls=%async_computation.1 | async-start | bytes 3145728 | tf_op jit(solution)/shard_map/all_to_all | solution.py:857
  406.1 9.0 %collective-permute-done.59 = bf16[128,2048]{1,0:T(8,128)(2,1)} collective-permute-done((bf16[128,2048]{1,0:T(8,128)(2,1)}, bf16[128,2048]{1,0:T(8,128)(2,1)}, u32[]{:S(2)}, u32[]{:S(2)}) %collective-permute-start.59) | collective-permute-done | bytes 524320 | tf_op jit(solution)/shard_map/ppermute | solution.py:705
  421.0 5.7 %all-to-all-done.1 = bf16[16,128,384]{2,1,0:T(8,128)(2,1)} async-done(((bf16[16,128,384]{2,1,0:T(8,128)(2,1)}), bf16[16,128,384]{2,1,0:T(8,128)(2,1)}, u32[]{:S(2)}, u32[]{:S(2)}) %all-to-all-start.1) | async-done | bytes 1572896 | tf_op jit(solution)/shard_map/all_to_all | solution.py:857
  428.3 4.3 collective-permute-start.63
  438.7 6.2 %collective-permute-done.64 = bf16[2,32,384]{2,1,0:T(8,128)(2,1)S(1)} collective-permute-done((bf16[2,32,384]{2,1,0:T(8,128)(2,1)S(1)}, bf16[2,32,384]{2,1,0:T(8,128)(2,1)S(1)}, u32[]{:S(2)}, u32[]{:S(2)}) %collective-permute-start.64) | collective-permute-done | bytes 49184 | tf_op jit(solution)/shard_map/ppermute | solution.py:705
  452.2 3.6 collective-permute-done.66
  (310 shorter events, 155.4 us)
Async XLA Ops:
  11.1 54.7 %collective-permute-start = (bf16[256,2048]{1,0:T(8,128)(2,1)}, bf16[256,2048]{1,0:T(8,128)(2,1)S(1)}, u32[]{:S(2)}, u32[]{:S(2)}) collective-permute-start(bf16[256,2048]{1,0:T(8,128)(2,1)} %get-tuple-element.124.refs_0_), channel_id=1, source_target_pairs={{0,2},{2,0},{1,3},{3,1},{4,6},{6,4},{5,7},{7,5},{8,10},{10,8},{9,1... | collective-permute-start | bytes 3145736 | tf_op jit(solution)/shard_map/ppermute | solution.py:705
  12.5 52.6 %collective-permute-start.1 = (bf16[256,2048]{1,0:T(8,128)(2,1)}, bf16[256,2048]{1,0:T(8,128)(2,1)}, u32[]{:S(2)}, u32[]{:S(2)}) collective-permute-start(bf16[256,2048]{1,0:T(8,128)(2,1)} %get-tuple-element.124.refs_0_), channel_id=1, source_target_pairs={{0,4},{4,0},{1,5},{5,1},{2,6},{6,2},{3,7},{7,3},{8,12},{12,8},{9,1... | collective-permute-start | bytes 3145736 | tf_op jit(solution)/shard_map/ppermute | solution.py:705
  19.8 45.2 %all-to-all-start = ((bf16[64,32,384]{2,1,0:T(8,128)(2,1)}), bf16[64,32,384]{2,1,0:T(8,128)(2,1)S(1)}, u32[]{:S(2)}, u32[]{:S(2)}) async-start(bf16[64,32,384]{2,1,0:T(8,128)(2,1)} %get-tuple-element.125), calls=%async_computation | async-start | bytes 3145728 | tf_op jit(solution)/shard_map/all_to_all | solution.py:782
  28.6 146.3 %all-gather.2.cloned.1.call-start = ((), (), s32[]{:S(2)}) async-start(), calls=%async_computation.3 | async-start | bytes 10027008 | tf_op jit(solution)/shard_map/all_gather | solution.py:803
  36.2 26.9 %collective-permute-start.3 = (bf16[2,32,2304]{2,1,0:T(8,128)(2,1)}, bf16[2,32,2304]{2,1,0:T(8,128)(2,1)}, u32[]{:S(2)}, u32[]{:S(2)}) collective-permute-start(bf16[2,32,2304]{2,1,0:T(8,128)(2,1)} %get-tuple-element.256), channel_id=1, source_target_pairs={{0,4},{4,0},{1,5},{5,1},{2,6},{6,2},{3,7},{7,3},{8,12},{12,8},{9,1... | collective-permute-start | bytes 884744 | tf_op jit(solution)/shard_map/ppermute | solution.py:705
  39.1 24.0 %collective-permute-start.5 = (bf16[2,32,256]{2,1,0:T(8,128)(2,1)S(1)}, bf16[2,32,256]{2,1,0:T(8,128)(2,1)S(1)}, u32[]{:S(2)}, u32[]{:S(2)}) collective-permute-start(bf16[2,32,256]{2,1,0:T(8,128)(2,1)S(1)} %get-tuple-element.264), channel_id=1, source_target_pairs={{0,4},{4,0},{1,5},{5,1},{2,6},{6,2},{3,7},{7,3},{8,12},{12,8},{9,1... | collective-permute-start | bytes 98312 | tf_op jit(solution)/shard_map/ppermute | solution.py:705
  75.7 17.7 %collective-permute-start.7 = (bf16[1024,128]{1,0:T(8,128)(2,1)}, bf16[1024,128]{1,0:T(8,128)(2,1)S(1)}, u32[]{:S(2)}, u32[]{:S(2)}) collective-permute-start(bf16[1024,128]{1,0:T(8,128)(2,1)} %get-tuple-element.139.kv0), channel_id=1, source_target_pairs={{0,8},{8,16},{16,24},{1,9},{9,17},{17,25},{2,10},{10,18},{18,26},{... | collective-permute-start | bytes 786440 | tf_op jit(solution)/shard_map/ppermute | solution.py:714
  94.9 321.9 %reduce-scatter.2.cloned.1.call-start = ((), (), s32[]{:S(2)}) async-start(), calls=%async_computation.4 | async-start | bytes 11141120 | tf_op jit(solution)/shard_map/reduce_scatter | solution.py:837
  99.6 24.5 %collective-permute-start.13 = (bf16[256,2048]{1,0:T(8,128)(2,1)}, bf16[256,2048]{1,0:T(8,128)(2,1)}, u32[]{:S(2)}, u32[]{:S(2)}) collective-permute-start(bf16[256,2048]{1,0:T(8,128)(2,1)} %get-tuple-element.144.refs_0_.refs_8_), channel_id=1, source_target_pairs={{0,4},{4,0},{1,5},{5,1},{2,6},{6,2},{3,7},{7,3},{8,12},{12,8},{9,1... | collective-permute-start | bytes 3145736 | tf_op jit(solution)/shard_map/ppermute | solution.py:705
  141.3 24.0 %collective-permute-start.20 = (bf16[128,2048]{1,0:T(8,128)(2,1)}, bf16[128,2048]{1,0:T(8,128)(2,1)S(1)}, u32[]{:S(2)}, u32[]{:S(2)}) collective-permute-start(bf16[128,2048]{1,0:T(8,128)(2,1)} %get-tuple-element.249), channel_id=1, source_target_pairs={{0,5},{1,4},{4,1},{5,0},{2,7},{3,6},{6,3},{7,2},{8,13},{9,12},{12,... | collective-permute-start | bytes 1572872 | tf_op jit(solution)/shard_map/ppermute | solution.py:705
  144.7 21.4 %collective-permute-start.18 = (bf16[128,2048]{1,0:T(8,128)(2,1)}, bf16[128,2048]{1,0:T(8,128)(2,1)}, u32[]{:S(2)}, u32[]{:S(2)}) collective-permute-start(bf16[128,2048]{1,0:T(8,128)(2,1)} %slice.116), channel_id=1, source_target_pairs={{0,1},{1,0},{2,3},{3,2},{4,5},{5,4},{6,7},{7,6},{8,9},{9,8},{10,11... | collective-permute-start | bytes 1572872 | tf_op jit(solution)/shard_map/ppermute | solution.py:705
  144.7 27.7 %collective-permute-start.25 = (bf16[256,2048]{1,0:T(8,128)(2,1)S(1)}, bf16[256,2048]{1,0:T(8,128)(2,1)S(1)}, u32[]{:S(2)}, u32[]{:S(2)}) collective-permute-start(bf16[256,2048]{1,0:T(8,128)(2,1)S(1)} %copy-done.6), channel_id=1, source_target_pairs={{0,2},{2,0},{1,3},{3,1},{4,6},{6,4},{5,7},{7,5},{8,10},{10,8},{9,1... | collective-permute-start | bytes 3145736 | tf_op jit(solution)/shard_map/ppermute | solution.py:705
  145.7 29.1 %collective-permute-start.26 = (bf16[256,2048]{1,0:T(8,128)(2,1)}, bf16[256,2048]{1,0:T(8,128)(2,1)}, u32[]{:S(2)}, u32[]{:S(2)}) collective-permute-start(bf16[256,2048]{1,0:T(8,128)(2,1)} %collective-permute-done.13.refs_2_.refs_10_), channel_id=1, source_target_pairs={{0,2},{2,0},{1,3},{3,1},{4,6},{6,4},{5,7},{7,5},{8,10},{10,8},{9,1... | collective-permute-start | bytes 3145736 | tf_op jit(solution)/shard_map/ppermute | solution.py:705
  169.8 23.5 %collective-permute-start.23 = (bf16[128,2048]{1,0:T(8,128)(2,1)S(1)}, bf16[128,2048]{1,0:T(8,128)(2,1)}, u32[]{:S(2)}, u32[]{:S(2)}) collective-permute-start(bf16[128,2048]{1,0:T(8,128)(2,1)S(1)} %multiply_convert_fusion.refs_0_), channel_id=1, source_target_pairs={{0,5},{1,4},{4,1},{5,0},{2,7},{3,6},{6,3},{7,2},{8,13},{9,12},{12,... | collective-permute-start | bytes 1572872 | tf_op jit(solution)/shard_map/ppermute | solution.py:705
  171.4 24.1 %collective-permute-start.24 = (bf16[128,2048]{1,0:T(8,128)(2,1)S(1)}, bf16[128,2048]{1,0:T(8,128)(2,1)}, u32[]{:S(2)}, u32[]{:S(2)}) collective-permute-start(bf16[128,2048]{1,0:T(8,128)(2,1)S(1)} %multiply_convert_fusion.refs_0_), channel_id=1, source_target_pairs={{0,4},{4,0},{1,5},{5,1},{2,6},{6,2},{3,7},{7,3},{8,12},{12,8},{9,1... | collective-permute-start | bytes 1572872 | tf_op jit(solution)/shard_map/ppermute | solution.py:705
  173.4 23.8 %collective-permute-start.27 = (bf16[128,2048]{1,0:T(8,128)(2,1)S(1)}, bf16[128,2048]{1,0:T(8,128)(2,1)S(1)}, u32[]{:S(2)}, u32[]{:S(2)}) collective-permute-start(bf16[128,2048]{1,0:T(8,128)(2,1)S(1)} %multiply_convert_fusion.refs_0_), channel_id=1, source_target_pairs={{0,2},{2,0},{1,3},{3,1},{4,6},{6,4},{5,7},{7,5},{8,10},{10,8},{9,1... | collective-permute-start | bytes 1572872 | tf_op jit(solution)/shard_map/ppermute | solution.py:705
  229.1 23.2 %collective-permute-start.32 = (bf16[128,2048]{1,0:T(8,128)(2,1)S(1)}, bf16[128,2048]{1,0:T(8,128)(2,1)S(1)}, u32[]{:S(2)}, u32[]{:S(2)}) collective-permute-start(bf16[128,2048]{1,0:T(8,128)(2,1)S(1)} %slice.115), channel_id=1, source_target_pairs={{0,1},{1,0},{2,3},{3,2},{4,5},{5,4},{6,7},{7,6},{8,9},{9,8},{10,11... | collective-permute-start | bytes 1572872 | tf_op jit(solution)/shard_map/ppermute | solution.py:705
  229.7 22.6 %collective-permute-start.34 = (bf16[128,2048]{1,0:T(8,128)(2,1)S(1)}, bf16[128,2048]{1,0:T(8,128)(2,1)S(1)}, u32[]{:S(2)}, u32[]{:S(2)}) collective-permute-start(bf16[128,2048]{1,0:T(8,128)(2,1)S(1)} %get-tuple-element.248), channel_id=1, source_target_pairs={{0,5},{1,4},{4,1},{5,0},{2,7},{3,6},{6,3},{7,2},{8,13},{9,12},{12,... | collective-permute-start | bytes 1572872 | tf_op jit(solution)/shard_map/ppermute | solution.py:705
  231.5 23.4 %collective-permute-start.35 = (bf16[128,2048]{1,0:T(8,128)(2,1)S(1)}, bf16[128,2048]{1,0:T(8,128)(2,1)S(1)}, u32[]{:S(2)}, u32[]{:S(2)}) collective-permute-start(bf16[128,2048]{1,0:T(8,128)(2,1)S(1)} %get-tuple-element.247), channel_id=1, source_target_pairs={{0,4},{4,0},{1,5},{5,1},{2,6},{6,2},{3,7},{7,3},{8,12},{12,8},{9,1... | collective-permute-start | bytes 1572872 | tf_op jit(solution)/shard_map/ppermute | solution.py:705
  260.6 24.2 %collective-permute-start.38 = (bf16[128,2048]{1,0:T(8,128)(2,1)S(1)}, bf16[128,2048]{1,0:T(8,128)(2,1)S(1)}, u32[]{:S(2)}, u32[]{:S(2)}) collective-permute-start(bf16[128,2048]{1,0:T(8,128)(2,1)S(1)} %get-tuple-element.175.refs_0_), channel_id=1, source_target_pairs={{0,4},{4,0},{1,5},{5,1},{2,6},{6,2},{3,7},{7,3},{8,12},{12,8},{9,1... | collective-permute-start | bytes 1572872 | tf_op jit(solution)/shard_map/ppermute | solution.py:705
  262.1 24.3 %collective-permute-start.41 = (bf16[128,2048]{1,0:T(8,128)(2,1)S(1)}, bf16[128,2048]{1,0:T(8,128)(2,1)S(1)}, u32[]{:S(2)}, u32[]{:S(2)}) collective-permute-start(bf16[128,2048]{1,0:T(8,128)(2,1)S(1)} %get-tuple-element.175.refs_0_), channel_id=1, source_target_pairs={{0,2},{2,0},{1,3},{3,1},{4,6},{6,4},{5,7},{7,5},{8,10},{10,8},{9,1... | collective-permute-start | bytes 1572872 | tf_op jit(solution)/shard_map/ppermute | solution.py:705
  295.6 18.8 %collective-permute-start.45 = (bf16[128,2048]{1,0:T(8,128)(2,1)S(1)}, bf16[128,2048]{1,0:T(8,128)(2,1)S(1)}, u32[]{:S(2)}, u32[]{:S(2)}) collective-permute-start(bf16[128,2048]{1,0:T(8,128)(2,1)S(1)} %slice.114), channel_id=1, source_target_pairs={{0,1},{1,0},{2,3},{3,2},{4,5},{5,4},{6,7},{7,6},{8,9},{9,8},{10,11... | collective-permute-start | bytes 1572872 | tf_op jit(solution)/shard_map/ppermute | solution.py:705
  297.1 25.3 %collective-permute-start.46 = (bf16[128,2048]{1,0:T(8,128)(2,1)S(1)}, bf16[128,2048]{1,0:T(8,128)(2,1)S(1)}, u32[]{:S(2)}, u32[]{:S(2)}) collective-permute-start(bf16[128,2048]{1,0:T(8,128)(2,1)S(1)} %get-tuple-element.246), channel_id=1, source_target_pairs={{0,5},{1,4},{4,1},{5,0},{2,7},{3,6},{6,3},{7,2},{8,13},{9,12},{12,... | collective-permute-start | bytes 1572872 | tf_op jit(solution)/shard_map/ppermute | solution.py:705
  298.9 23.6 %collective-permute-start.47 = (bf16[128,2048]{1,0:T(8,128)(2,1)S(1)}, bf16[128,2048]{1,0:T(8,128)(2,1)S(1)}, u32[]{:S(2)}, u32[]{:S(2)}) collective-permute-start(bf16[128,2048]{1,0:T(8,128)(2,1)S(1)} %get-tuple-element.245), channel_id=1, source_target_pairs={{0,4},{4,0},{1,5},{5,1},{2,6},{6,2},{3,7},{7,3},{8,12},{12,8},{9,1... | collective-permute-start | bytes 1572872 | tf_op jit(solution)/shard_map/ppermute | solution.py:705
  323.6 44.4 %collective-permute-start.51 = (bf16[128,2048]{1,0:T(8,128)(2,1)S(1)}, bf16[128,2048]{1,0:T(8,128)(2,1)S(1)}, u32[]{:S(2)}, u32[]{:S(2)}) collective-permute-start(bf16[128,2048]{1,0:T(8,128)(2,1)S(1)} %add_convert_fusion.2), channel_id=1, source_target_pairs={{0,1},{1,0},{2,3},{3,2},{4,5},{5,4},{6,7},{7,6},{8,9},{9,8},{10,11... | collective-permute-start | bytes 1572872 | tf_op jit(solution)/shard_map/ppermute | solution.py:705
  325.2 27.1 %collective-permute-start.49 = (bf16[1024,128]{1,0:T(8,128)(2,1)S(1)}, bf16[1024,128]{1,0:T(8,128)(2,1)S(1)}, u32[]{:S(2)}, u32[]{:S(2)}) collective-permute-start(bf16[1024,128]{1,0:T(8,128)(2,1)S(1)} %copy-done.50), channel_id=1, source_target_pairs={{16,0},{24,8},{17,1},{25,9},{18,2},{26,10},{19,3},{27,11},{20,4},{... | collective-permute-start | bytes 786440 | tf_op jit(solution)/shard_map/ppermute | solution.py:714
  326.5 41.6 %collective-permute-start.50 = (bf16[1024,128]{1,0:T(8,128)(2,1)S(1)}, bf16[1024,128]{1,0:T(8,128)(2,1)S(1)}, u32[]{:S(2)}, u32[]{:S(2)}) collective-permute-start(bf16[1024,128]{1,0:T(8,128)(2,1)S(1)} %copy-done.49), channel_id=1, source_target_pairs={{24,0},{25,1},{26,2},{27,3},{28,4},{29,5},{30,6},{31,7},{56,32},{5... | collective-permute-start | bytes 786440 | tf_op jit(solution)/shard_map/ppermute | solution.py:714
  388.2 17.9 %collective-permute-start.60 = (bf16[128,2048]{1,0:T(8,128)(2,1)}, bf16[128,2048]{1,0:T(8,128)(2,1)}, u32[]{:S(2)}, u32[]{:S(2)}) collective-permute-start(bf16[128,2048]{1,0:T(8,128)(2,1)} %get-tuple-element.244), channel_id=1, source_target_pairs={{0,4},{4,0},{1,5},{5,1},{2,6},{6,2},{3,7},{7,3},{8,12},{12,8},{9,1... | collective-permute-start | bytes 1572872 | tf_op jit(solution)/shard_map/ppermute | solution.py:705
  390.7 24.3 %collective-permute-start.59 = (bf16[128,2048]{1,0:T(8,128)(2,1)}, bf16[128,2048]{1,0:T(8,128)(2,1)}, u32[]{:S(2)}, u32[]{:S(2)}) collective-permute-start(bf16[128,2048]{1,0:T(8,128)(2,1)} %get-tuple-element.243), channel_id=1, source_target_pairs={{0,5},{1,4},{4,1},{5,0},{2,7},{3,6},{6,3},{7,2},{8,13},{9,12},{12,... | collective-permute-start | bytes 1572872 | tf_op jit(solution)/shard_map/ppermute | solution.py:705
  393.0 22.1 %collective-permute-start.58 = (bf16[128,2048]{1,0:T(8,128)(2,1)}, bf16[128,2048]{1,0:T(8,128)(2,1)}, u32[]{:S(2)}, u32[]{:S(2)}) collective-permute-start(bf16[128,2048]{1,0:T(8,128)(2,1)} %slice.113), channel_id=1, source_target_pairs={{0,1},{1,0},{2,3},{3,2},{4,5},{5,4},{6,7},{7,6},{8,9},{9,8},{10,11... | collective-permute-start | bytes 1572872 | tf_op jit(solution)/shard_map/ppermute | solution.py:705
  399.1 27.6 %all-to-all-start.1 = ((bf16[16,128,384]{2,1,0:T(8,128)(2,1)}), bf16[16,128,384]{2,1,0:T(8,128)(2,1)}, u32[]{:S(2)}, u32[]{:S(2)}) async-start(bf16[16,128,384]{2,1,0:T(8,128)(2,1)} %bitcast.66), calls=%async_computation.1 | async-start | bytes 3145728 | tf_op jit(solution)/shard_map/all_to_all | solution.py:857
  438.1 19.7 %collective-permute-start.62 = (bf16[128,2048]{1,0:T(8,128)(2,1)S(1)}, bf16[128,2048]{1,0:T(8,128)(2,1)S(1)}, u32[]{:S(2)}, u32[]{:S(2)}) collective-permute-start(bf16[128,2048]{1,0:T(8,128)(2,1)S(1)} %convert_element_type.172), channel_id=1, source_target_pairs={{0,1},{1,0},{2,3},{3,2},{4,5},{5,4},{6,7},{7,6},{8,9},{9,8},{10,11... | collective-permute-start | bytes 1572872 | tf_op jit(solution)/shard_map/ppermute | solution.py:705
  (101 other events, 745.0 us)
Sparse Core Ops, SparseCore 0:
  95.1 79.8 all-gather.1
  295.7 97.7 reduce-scatter.1
